TPU v7x, 512 devices: a whole 4x8x8 slice. The times are simulated.
512 devices in a mesh: blk: 128 (over y_lo, z, x, core), grp: 4 (over y_hi).
Axes of the slice: x: 4, y: 8 (y_hi: 4, y_lo: 2; y = y_hi * 2 + y_lo), z: 8, core: 2. Of those that a mesh axis runs over, the one named last changes fastest.
Arguments:
- query_rows: bfloat16 [65536, 1024], P(('grp', 'blk')), parts along dimension 0, may hold values from -6 to 6
- key_rows: bfloat16 [65536, 1024], P(('grp', 'blk')), parts along dimension 0, may hold values from -6 to 6
- value_rows: bfloat16 [65536, 1024], P(('grp', 'blk')), parts along dimension 0, may hold values from -6 to 6
- gate_rows: bfloat16 [65536, 1024], P(('grp', 'blk')), parts along dimension 0, may hold values from -24 to 24
- segment: int32 [65536], P('grp'), parts along dimension 0, may hold values from 0 to 3, never falling along the last dimension, each value on 1 to 8192 neighbouring positions
- w_out: bfloat16 [1024, 1024], P('blk'), may hold values from -0.1875 to 0.1875
- cotangent: bfloat16 [65536, 1024], P(('grp', 'blk')), parts along dimension 0, may hold values from -6 to 6
Outputs:
- query_grad: bfloat16 [65536, 1024], P(('grp', 'blk')), parts along dimension 0
- key_grad: bfloat16 [65536, 1024], P(('grp', 'blk')), parts along dimension 0
- value_grad: bfloat16 [65536, 1024], P(('grp', 'blk')), parts along dimension 0
- gate_grad: bfloat16 [65536, 1024], P(('grp', 'blk')), parts along dimension 0
- w_grad: float32 [4096, 1024], P(('grp', 'blk')), parts along dimension 0
There are 4 independent parts, one for each index of `grp`. A program takes and returns all parts, laid end to end along the dimension named above; an argument that names none is the same for every part. Nothing has to cross between parts.
Inputs may be any that keep to these rules, and one draw needn't show every extreme that they name: Segment numbers never fall along the events; every segment holds 1 to 8192 events, and one holds exactly 8192.
All inputs are finite; a program needn't handle non-finite values.
Results may differ from a plain program's by a relative error of at most 0.0058.
Values may be sent and summed in bfloat16 or wider, within the bound.
No kernel may reach another device: no remote copies, remote signals or barrier semaphores. Data moves between devices by JAX's collectives and lax.ppermute only.
A program may use at most 64 MiB of HBM per device.

v0:
```python
import jax
import jax.numpy as jnp
from jax import lax
from jax.sharding import PartitionSpec as P

DH = 128
REACH = 4


def from_behind(value, axis, steps):
    count = lax.axis_size(axis)
    first, last = (max(0, -steps), min(count, count - steps))
    return lax.ppermute(value, axis, [(source, source + steps) for source in range(first, last)])


def body(query_rows, key_rows, value_rows, gate_rows, segment, w_out, cotangent):
    rows = query_rows.shape[0]
    width = query_rows.shape[1]
    heads = width // DH
    scale = DH ** (-0.5)
    total = segment.shape[0]
    reach_rows = (REACH - 1) * rows
    device = lax.axis_index("blk")
    own_start = device * rows
    local = jnp.arange(rows, dtype=jnp.int32)

    def split(array):
        return array.reshape(rows, heads, DH)

    def segment_slice(start):
        return lax.dynamic_slice_in_dim(segment, jnp.clip(start, 0, total - rows), rows, 0)

    def block_mask(query_start, key_start):
        query_pos = query_start + local
        key_pos = key_start + local
        same = segment_slice(query_start)[:, None] == segment_slice(key_start)[None, :]
        valid = (
            (key_pos[None, :] <= query_pos[:, None])
            & (key_pos[None, :] >= 0)
            & (query_pos[:, None] < total)
            & (key_pos[None, :] >= query_pos[:, None] - reach_rows)
        )
        return (same & valid).astype(jnp.float32)

    def scores_of(queries, keyed):
        return (
            jnp.einsum("qhd,khd->hqk", queries, keyed, preferred_element_type=jnp.float32) * scale
        )

    memory = [(key_rows, value_rows)]
    carried = (key_rows, value_rows)
    for offset in range(1, REACH):
        carried = from_behind((carried[0], carried[1]), "blk", 1)
        memory.append(carried)
    queries = split(query_rows)
    masks = [block_mask(own_start, own_start - offset * rows) for offset in range(REACH)]
    attended = jnp.zeros((rows, heads, DH), jnp.float32)
    for offset in range(REACH):
        keyed = split(memory[offset][0])
        valued = split(memory[offset][1])
        scores = scores_of(queries, keyed)
        weights = (jax.nn.sigmoid(scores) * scores * masks[offset][None]).astype(jnp.bfloat16)
        attended = attended + jnp.einsum(
            "hqk,khd->qhd", weights, valued, preferred_element_type=jnp.float32
        )
    attended = attended.reshape(rows, width)
    mean = jnp.mean(attended, axis=-1, keepdims=True)
    centred = attended - mean
    rstd = lax.rsqrt(jnp.mean(centred * centred, axis=-1, keepdims=True) + 1e-05)
    normed = centred * rstd
    gate = gate_rows.astype(jnp.float32)
    hidden = (normed * gate).astype(jnp.bfloat16)
    w_grad = lax.psum_scatter(
        jnp.einsum("tr,te->re", hidden, cotangent, preferred_element_type=jnp.float32),
        "blk",
        scatter_dimension=0,
        tiled=True,
    )
    full_weight = lax.all_gather(w_out, "blk", axis=0, tiled=True)
    hidden_grad = jnp.einsum(
        "te,de->td", cotangent, full_weight, preferred_element_type=jnp.float32
    )
    gate_grad = (hidden_grad * normed).astype(jnp.bfloat16)
    normed_grad = hidden_grad * gate
    attended_grad = rstd * (
        normed_grad
        - jnp.mean(normed_grad, axis=-1, keepdims=True)
        - normed * jnp.mean(normed_grad * normed, axis=-1, keepdims=True)
    )
    upstream = attended_grad.astype(jnp.bfloat16)
    upper = split(upstream)
    query_grad = jnp.zeros((rows, heads, DH), jnp.float32)
    partials = []
    for offset in range(REACH):
        keyed = split(memory[offset][0])
        valued = split(memory[offset][1])
        allowed = masks[offset]
        pair_scores = scores_of(queries, keyed)
        sigma = jax.nn.sigmoid(pair_scores)
        pair_weights = (sigma * pair_scores * allowed[None]).astype(jnp.bfloat16)
        weight_grad = jnp.einsum("qhd,khd->hqk", upper, valued, preferred_element_type=jnp.float32)
        score_grad = (
            weight_grad * allowed[None] * sigma * (1.0 + pair_scores * (1.0 - sigma))
        ).astype(jnp.bfloat16)
        score_grad, weights = (score_grad, pair_weights)
        query_grad = query_grad + jnp.einsum(
            "hqk,khd->qhd", score_grad, keyed, preferred_element_type=jnp.float32
        )
        key_part = jnp.einsum(
            "hqk,qhd->khd", score_grad, queries, preferred_element_type=jnp.float32
        ).reshape(rows, width)
        value_part = jnp.einsum(
            "hqk,qhd->khd", weights, upper, preferred_element_type=jnp.float32
        ).reshape(rows, width)
        partials.append((key_part, value_part))
    summed = partials[REACH - 1]
    for offset in range(REACH - 2, -1, -1):
        arrived = from_behind(summed, "blk", -1)
        summed = (arrived[0] + partials[offset][0], arrived[1] + partials[offset][1])
    key_total, value_total = summed
    query_out = (query_grad.reshape(rows, width) * scale).astype(jnp.bfloat16)
    key_out = (key_total * scale).astype(jnp.bfloat16)
    value_out = value_total.astype(jnp.bfloat16)
    return (query_out, key_out, value_out, gate_grad, w_grad)


def solution(mesh):
    in_specs = (
        P(("grp", "blk"), None),
        P(("grp", "blk"), None),
        P(("grp", "blk"), None),
        P(("grp", "blk"), None),
        P("grp"),
        P("blk", None),
        P(("grp", "blk"), None),
    )
    out_specs = (
        P(("grp", "blk"), None),
        P(("grp", "blk"), None),
        P(("grp", "blk"), None),
        P(("grp", "blk"), None),
        P(("grp", "blk"), None),
    )
    return jax.shard_map(body, mesh=mesh, in_specs=in_specs, out_specs=out_specs, check_vma=False)
```

profile of v0, /device:TPU:1, one launch (start us, length us, event | category | flops | bytes accessed | tf_op | source)
XLA Modules:
  0.0 809.0 jit_solution(13777400366180879938)
XLA Ops:
  9.1 4.5 collective-permute-start
  13.6 1.9 collective-permute-start.1
  20.0 4.3 collective-permute-start.3
  24.3 1.9 collective-permute-start.2
  27.9 4.3 collective-permute-start.5
  32.2 2.7 collective-permute-start.4
  37.3 1.3 collective-permute-done.4
  38.9 1.6 fusion.33
  41.0 2.8 fusion.18
  43.8 187.4 %all-gather.2.cloned.1.call-done = bf16[1024,1024]{1,0:T(8,128)(2,1)} async-done(((bf16[8,1024]{1,0:T(8,128)(2,1)}), bf16[1024,1024]{1,0:T(8,128)(2,1)}) %all-gather.2.cloned.1.call-update) | async-done | bytes 2097168 | tf_op jit(solution)/shard_map/all_gather | solution.py:79
  231.2 2.5 fusion.27
  235.6 1.3 fusion.12
  238.2 3.1 collective-permute-start.6
  241.4 1.3 fusion.31
  247.1 1.9 collective-permute-start.9
  249.8 1.9 add.197
  251.8 2.0 collective-permute-start.7
  255.0 1.2 copy.93
  256.2 2.1 collective-permute-done.9
  258.3 1.9 add.200
  260.2 1.9 collective-permute-start.10
  262.9 1.6 collective-permute-done.7
  265.6 1.9 collective-permute-start.8
  268.7 1.2 copy.95
  269.9 1.5 collective-permute-done.10
  271.4 1.9 add.201
  273.3 2.0 collective-permute-start.11
  275.7 1.2 copy.97
  278.4 1.8 multiply_convert_fusion.1
  280.2 4.4 collective-permute-done.11
  284.6 1.8 add_convert_fusion
  286.4 515.8 %reduce-scatter.2.cloned.1.call-done = f32[8,1024]{1,0:T(8,128)} async-done(((f32[1024,1024]{1,0:T(8,128)}), f32[8,1024]{1,0:T(8,128)}) %reduce-scatter.2.cloned.1.call-update) | async-done | bytes 32784 | tf_op jit(solution)/shard_map/reduce_scatter | solution.py:73
  (122 shorter events, 24.9 us)
Async XLA Ops:
  7.2 33.8 %copy-start = (bf16[128,1024]{1,0:T(8,128)(2,1)S(1)}, bf16[128,1024]{1,0:T(8,128)(2,1)}, u32[]{:S(2)}) copy-start(bf16[128,1024]{1,0:T(8,128)(2,1)} %param.13) | copy-start | bytes 786436
  7.2 11.6 %copy-start.29 = (bf16[128,1024]{1,0:T(8,128)(2,1)S(1)}, bf16[128,1024]{1,0:T(8,128)(2,1)}, u32[]{:S(2)}) copy-start(bf16[128,1024]{1,0:T(8,128)(2,1)} %param.9) | copy-start | bytes 786436
  7.2 224.1 %all-gather.2.cloned.1.call-start = ((), (), s32[]{:S(2)}) async-start(), calls=%async_computation.1 | async-start | bytes 2113536 | tf_op jit(solution)/shard_map/all_gather | solution.py:79
  7.9 794.3 %reduce-scatter.2.cloned.1.call-start = ((), (), s32[]{:S(2)}) async-start(), calls=%async_computation.2 | async-start | bytes 4227072 | tf_op jit(solution)/shard_map/reduce_scatter | solution.py:73
  9.1 15.2 %collective-permute-start = (bf16[128,1024]{0,1:T(8,128)(2,1)S(1)}, bf16[128,1024]{0,1:T(8,128)(2,1)S(1)}, u32[]{:S(2)}, u32[]{:S(2)}) collective-permute-start(bf16[128,1024]{0,1:T(8,128)(2,1)S(1)} %copy.110), channel_id=1, source_target_pairs={{0,4},{4,8},{8,12},{12,16},{16,20},{20,24},{24,28},{28,32},{32,36}... | collective-permute-start | bytes 786440 | tf_op jit(solution)/shard_map/ppermute | solution.py:13
  13.6 6.2 collective-permute-start.1
  18.8 16.4 %copy-start.27 = (f32[128,128]{1,0:T(8,128)}, f32[128,128]{1,0:T(8,128)S(1)}, u32[]{:S(2)}) copy-start(f32[128,128]{1,0:T(8,128)S(1)} %get-tuple-element.20) | copy-start | bytes 196612
  20.0 7.8 copy-start.18
  20.0 7.6 collective-permute-start.3
  24.3 7.9 collective-permute-start.2
  27.8 9.5 %copy-start.24 = (bf16[128,1024]{0,1:T(8,128)(2,1)}, bf16[128,1024]{0,1:T(8,128)(2,1)S(1)}, u32[]{:S(2)}) copy-start(bf16[128,1024]{0,1:T(8,128)(2,1)S(1)} %copy.63) | copy-start | bytes 786436
  27.9 9.3 %collective-permute-start.5 = (bf16[128,1024]{1,0:T(8,128)(2,1)S(1)}, bf16[128,1024]{1,0:T(8,128)(2,1)S(1)}, u32[]{:S(2)}, u32[]{:S(2)}) collective-permute-start(bf16[128,1024]{1,0:T(8,128)(2,1)S(1)} %collective-permute-done.3), channel_id=1, source_target_pairs={{0,4},{4,8},{8,12},{12,16},{16,20},{20,24},{24,28},{28,32},{32,36}... | collective-permute-start | bytes 786440 | tf_op jit(solution)/shard_map/ppermute | solution.py:13
  32.2 6.4 collective-permute-start.4
  237.2 5.5 copy-start.15
  238.2 4.4 copy-start.21
  238.2 4.5 copy-start.25
  238.2 4.5 copy-start.28
  238.2 11.6 %collective-permute-start.6 = (f32[128,1024]{1,0:T(8,128)}, f32[128,1024]{1,0:T(8,128)}, u32[]{:S(2)}, u32[]{:S(2)}) collective-permute-start(f32[128,1024]{1,0:T(8,128)} %copy.83), channel_id=1, source_target_pairs={{4,0},{8,4},{12,8},{16,12},{20,16},{24,20},{28,24},{32,28},{36,32}... | collective-permute-start | bytes 1572872 | tf_op jit(solution)/shard_map/ppermute | solution.py:13
  243.1 6.0 copy-start.4
  245.8 3.5 copy-start.2
  247.1 11.1 %collective-permute-start.9 = (f32[128,1024]{1,0:T(8,128)}, f32[128,1024]{1,0:T(8,128)}, u32[]{:S(2)}, u32[]{:S(2)}) collective-permute-start(f32[128,1024]{1,0:T(8,128)} %copy.91), channel_id=1, source_target_pairs={{4,0},{8,4},{12,8},{16,12},{20,16},{24,20},{28,24},{32,28},{36,32}... | collective-permute-start | bytes 1572872 | tf_op jit(solution)/shard_map/ppermute | solution.py:13
  249.5 4.3 copy-start.13
  249.5 4.3 copy-start.22
  251.8 10.3 %copy-start.7 = (bf16[8,128,128]{2,1,0:T(8,128)(2,1)S(1)}, bf16[8,128,128]{2,1,0:T(8,128)(2,1)}, u32[]{:S(2)}) copy-start(bf16[8,128,128]{2,1,0:T(8,128)(2,1)} %fusion.10) | copy-start | bytes 786436
  251.8 12.7 %collective-permute-start.7 = (f32[128,1024]{1,0:T(8,128)}, f32[128,1024]{1,0:T(8,128)}, u32[]{:S(2)}, u32[]{:S(2)}) collective-permute-start(f32[128,1024]{1,0:T(8,128)} %add.197), channel_id=1, source_target_pairs={{4,0},{8,4},{12,8},{16,12},{20,16},{24,20},{28,24},{32,28},{36,32}... | collective-permute-start | bytes 1572872 | tf_op jit(solution)/shard_map/ppermute | solution.py:13
  256.2 6.3 copy-start.5
  260.2 11.2 %collective-permute-start.10 = (f32[128,1024]{1,0:T(8,128)}, f32[128,1024]{1,0:T(8,128)}, u32[]{:S(2)}, u32[]{:S(2)}) collective-permute-start(f32[128,1024]{1,0:T(8,128)} %add.200), channel_id=1, source_target_pairs={{4,0},{8,4},{12,8},{16,12},{20,16},{24,20},{28,24},{32,28},{36,32}... | collective-permute-start | bytes 1572872 | tf_op jit(solution)/shard_map/ppermute | solution.py:13
  262.5 5.0 copy-start.10
  262.6 5.0 copy-start.23
  265.6 12.8 %collective-permute-start.8 = (f32[128,1024]{1,0:T(8,128)S(1)}, f32[128,1024]{1,0:T(8,128)}, u32[]{:S(2)}, u32[]{:S(2)}) collective-permute-start(f32[128,1024]{1,0:T(8,128)S(1)} %add.198), channel_id=1, source_target_pairs={{4,0},{8,4},{12,8},{16,12},{20,16},{24,20},{28,24},{32,28},{36,32}... | collective-permute-start | bytes 1572872 | tf_op jit(solution)/shard_map/ppermute | solution.py:13
  273.3 4.7 copy-start.3
  273.3 11.3 %collective-permute-start.11 = (f32[128,1024]{1,0:T(8,128)}, f32[128,1024]{1,0:T(8,128)}, u32[]{:S(2)}, u32[]{:S(2)}) collective-permute-start(f32[128,1024]{1,0:T(8,128)} %add.201), channel_id=1, source_target_pairs={{4,0},{8,4},{12,8},{16,12},{20,16},{24,20},{28,24},{32,28},{36,32}... | collective-permute-start | bytes 1572872 | tf_op jit(solution)/shard_map/ppermute | solution.py:13
  (13 other events, 20.1 us)
Sparse Core Ops, SparseCore 0:
  10.2 221.0 all-gather.1
  234.6 567.5 reduce-scatter.1
where the time goes:
time: 815 us; the launch traced here: 809 us
  waiting for transfers between devices  716 us (88%)
  starting transfers between devices  32.7 us (4%)
  matrix products  19.7 us (2%)
  between operations  14.8 us (2%)
  other arithmetic  13.4 us (2%)
  local copies, waits for them, and re-layouts  13 us (2%)
    reduce_scatter x1, waiting for transfers between devices, body(): lax.psum_scatter(jnp.einsum('tr,te->re', hidden, cotangent, preferred_ele...  516 us
    all_gather x1, waiting for transfers between devices, body(): full_weight = lax.all_gather(w_out, 'blk', axis=0, tiled=True)  187 us
    ppermute x12, starting transfers between devices, from_behind(): lax.ppermute(value, axis, [(source, source + steps) for source in range(f...  32.6 us
  transfers between devices with their start and end apart: 14, of which 8 were waited for; matrix products, arithmetic and copies ran while one was open for 5% of the time, Pallas kernels for 0%

commit v1 on v0

v1 whole, which is shorter than its diff:
```python
import jax
import jax.numpy as jnp
import numpy as np
from jax import lax
from jax.sharding import Mesh, PartitionSpec as P

DH = 128
REACH = 4
NY, NZ, NX, NC = 2, 8, 4, 2
BLK = ("y", "z", "x", "c")
ROW = ("x", "c")
COL = ("y", "z")


def shift(value, steps, sources=None):
    count = NY * NZ * NX * NC
    pairs = [(s, s + steps) for s in (sources or range(count)) if 0 <= s + steps < count]
    return lax.ppermute(value, BLK, pairs)


def ring(value, axis, size, steps):
    return lax.ppermute(value, axis, [(s, (s + steps) % size) for s in range(size)])


def swap(value):
    return ring(value, "c", NC, 1)


def body(query_rows, key_rows, value_rows, gate_rows, segment, w_out, cotangent):
    rows, width = query_rows.shape
    heads = width // DH
    scale = DH ** (-0.5)
    total = segment.shape[0]
    reach_rows = (REACH - 1) * rows
    core = lax.axis_index("c")
    xpos = lax.axis_index("x")
    device = lax.axis_index(BLK)
    own_start = device * rows
    local = jnp.arange(rows, dtype=jnp.int32)
    even = core == 0
    groups, members = NY * NZ, NX * NC
    part = rows // groups

    natural = np.arange(width)
    unit = w_out.shape[0]
    placed = (natural // unit % members) * (groups * unit) + natural // (unit * members) * unit + natural % unit
    to_placed = jnp.asarray(np.eye(width, dtype=np.float32)[:, np.argsort(placed)], jnp.bfloat16)

    def pair(mine, other):
        return jnp.where(even, mine, other), jnp.where(even, other, mine)

    kv = jnp.concatenate([key_rows, value_rows], 0)
    odd_sources = range(1, NY * NZ * NX * NC, 2)
    kv_chip = shift(kv, 2)
    kv_far = shift(kv, 3, odd_sources)
    qkv_sib = swap(jnp.concatenate([query_rows, kv], 0))
    q_sib, kv_sib = qkv_sib[:rows], qkv_sib[rows:]
    kv_cross = swap(kv_chip)
    memory = [
        kv,
        jnp.where(even, kv_cross, kv_sib),
        kv_chip,
        jnp.where(even, kv_far, kv_cross),
    ]

    rel = jnp.stack([cotangent] + [ring(cotangent, "x", NX, k) for k in range(1, NX)])
    rel_other = swap(rel)
    first, second = pair(rel, rel_other)
    cot_rel = jnp.stack([first, second], 1)
    order = (xpos - jnp.arange(NX)) % NX
    cot_abs = jnp.take(cot_rel, order, axis=0).reshape(members * rows, width)
    w_sub = lax.all_to_all(
        jnp.broadcast_to(w_out[None], (groups,) + w_out.shape), COL, 0, 0, tiled=True
    ).reshape(groups * unit, width)
    hg = jnp.einsum("te,de->td", cot_abs, w_sub, preferred_element_type=jnp.float32)
    hg = lax.all_to_all(hg.astype(jnp.bfloat16).reshape(members, rows, groups * unit), ROW, 0, 0, tiled=True)
    hg = hg.transpose(1, 0, 2).reshape(rows, width)
    hidden_grad = jnp.einsum("tp,dp->td", hg, to_placed, preferred_element_type=jnp.float32)

    def split(array):
        return array.reshape(rows, heads, DH)

    def segment_slice(start):
        return lax.dynamic_slice_in_dim(segment, jnp.clip(start, 0, total - rows), rows, 0)

    def block_mask(query_start, key_start):
        query_pos = query_start + local
        key_pos = key_start + local
        same = segment_slice(query_start)[:, None] == segment_slice(key_start)[None, :]
        valid = (
            (key_pos[None, :] <= query_pos[:, None])
            & (key_pos[None, :] >= 0)
            & (query_pos[:, None] < total)
            & (key_pos[None, :] >= query_pos[:, None] - reach_rows)
        )
        return (same & valid).astype(jnp.float32)

    def scores_of(queries, keyed):
        return (
            jnp.einsum("qhd,khd->hqk", queries, keyed, preferred_element_type=jnp.float32) * scale
        )

    queries = split(query_rows)
    attended = jnp.zeros((rows, heads, DH), jnp.float32)
    back = []
    for offset in range(REACH):
        keyed = split(memory[offset][:rows])
        valued = split(memory[offset][rows:])
        allowed = block_mask(own_start, own_start - offset * rows)
        scores = scores_of(queries, keyed)
        weights = (jax.nn.sigmoid(scores) * scores * allowed[None]).astype(jnp.bfloat16)
        attended = attended + jnp.einsum(
            "hqk,khd->qhd", weights, valued, preferred_element_type=jnp.float32
        )
        back.append((keyed, valued, allowed))
    attended = attended.reshape(rows, width)
    mean = jnp.mean(attended, axis=-1, keepdims=True)
    centred = attended - mean
    rstd = lax.rsqrt(jnp.mean(centred * centred, axis=-1, keepdims=True) + 1e-05)
    normed = centred * rstd
    gate = gate_rows.astype(jnp.float32)
    hidden = (normed * gate).astype(jnp.bfloat16)
    hidden = jnp.einsum("td,dp->tp", hidden, to_placed, preferred_element_type=jnp.float32)
    hidden = hidden.astype(jnp.bfloat16).reshape(rows, members, groups * unit).transpose(1, 0, 2)
    hidden_all = lax.all_to_all(hidden, ROW, 0, 0, tiled=True).reshape(members * rows, groups * unit)
    w_part = jnp.einsum("tr,te->re", hidden_all, cot_abs, preferred_element_type=jnp.float32)
    w_parts = lax.all_to_all(w_part.reshape(groups, unit, width), COL, 0, 0, tiled=True)
    w_grad = jnp.sum(w_parts, axis=0)

    gate_grad = (hidden_grad * normed).astype(jnp.bfloat16)
    normed_grad = hidden_grad * gate
    attended_grad = rstd * (
        normed_grad
        - jnp.mean(normed_grad, axis=-1, keepdims=True)
        - normed * jnp.mean(normed_grad * normed, axis=-1, keepdims=True)
    )
    upstream = attended_grad.astype(jnp.bfloat16)

    uq = jnp.concatenate([upstream, query_rows], 0)
    even_sources = range(0, NY * NZ * NX * NC, 2)
    uq_chip = shift(uq, -2)
    uq_far = shift(uq, -3, even_sources)
    u_sib = swap(upstream)
    uq_cross = swap(uq_chip)
    uq_sib = jnp.concatenate([u_sib, q_sib], 0)
    later = [
        uq,
        jnp.where(even, uq_sib, uq_cross),
        uq_chip,
        jnp.where(even, uq_cross, uq_far),
    ]

    upper = split(upstream)
    query_grad = jnp.zeros((rows, heads, DH), jnp.float32)
    key_total = jnp.zeros((rows, heads, DH), jnp.float32)
    value_total = jnp.zeros((rows, heads, DH), jnp.float32)

    def grads(pair_queries, pair_upper, keyed, valued, allowed):
        pair_scores = scores_of(pair_queries, keyed)
        sigma = jax.nn.sigmoid(pair_scores)
        weights = (sigma * pair_scores * allowed[None]).astype(jnp.bfloat16)
        weight_grad = jnp.einsum("qhd,khd->hqk", pair_upper, valued, preferred_element_type=jnp.float32)
        score_grad = (
            weight_grad * allowed[None] * sigma * (1.0 + pair_scores * (1.0 - sigma))
        ).astype(jnp.bfloat16)
        return weights, score_grad

    for offset in range(REACH):
        keyed, valued, allowed = back[offset]
        weights, score_grad = grads(queries, upper, keyed, valued, allowed)
        query_grad = query_grad + jnp.einsum(
            "hqk,khd->qhd", score_grad, keyed, preferred_element_type=jnp.float32
        )
        if offset:
            pair_upper = split(later[offset][:rows])
            pair_queries = split(later[offset][rows:])
            allowed = block_mask(own_start + offset * rows, own_start)
            keyed, valued, _ = back[0]
            weights, score_grad = grads(pair_queries, pair_upper, keyed, valued, allowed)
        else:
            pair_upper, pair_queries = upper, queries
        key_total = key_total + jnp.einsum(
            "hqk,qhd->khd", score_grad, pair_queries, preferred_element_type=jnp.float32
        )
        value_total = value_total + jnp.einsum(
            "hqk,qhd->khd", weights, pair_upper, preferred_element_type=jnp.float32
        )
    query_out = (query_grad.reshape(rows, width) * scale).astype(jnp.bfloat16)
    key_out = (key_total.reshape(rows, width) * scale).astype(jnp.bfloat16)
    value_out = value_total.reshape(rows, width).astype(jnp.bfloat16)
    return (query_out, key_out, value_out, gate_grad, w_grad)


def solution(mesh):
    fine = Mesh(
        mesh.devices.reshape(NY, NZ, NX, NC, mesh.devices.shape[1]), BLK + ("grp",)
    )
    every = ("grp",) + BLK
    rows = P(every, None)
    in_specs = (rows, rows, rows, rows, P("grp"), P(BLK, None), rows)
    return jax.shard_map(
        body, mesh=fine, in_specs=in_specs, out_specs=(rows,) * 5, check_vma=False
    )
```

time: 815 us -> 170 us (0.21)
  waiting for transfers between devices: 716 us -> 23.9 us
  starting transfers between devices: 32.7 us -> 64.5 us
  matrix products: 19.7 us -> 34.3 us
  between operations: 14.8 us -> 1.63 us
  local copies, waits for them, and re-layouts: 13 us -> 24.3 us
    reduce_scatter x1 -> x0, waiting for transfers between devices: 516 us -> none  [body(): lax.psum_scatter(jnp.einsum('tr,te->re', hidden, cotangent, preferred_ele...]
    all_gather x1 -> x0, waiting for transfers between devices: 187 us -> none  [body(): full_weight = lax.all_gather(w_out, 'blk', axis=0, tiled=True)]
    all_to_all x0 -> x4, starting transfers between devices: none -> 30.3 us  [the longest x1 13.6 us: body(): lax.all_to_all(jnp.broadcast_to(w_out[None], (groups,) + w_out.shape), CO...]
    all_to_all x0 -> x4, waiting for transfers between devices: none -> 10.7 us  [the longest x1 4.42 us: body(): lax.all_to_all(hidden, ROW, 0, 0, tiled=True)]
    dot_general x14 -> x13, matrix products: 13.9 us -> 18.8 us  [the longest x4 5.68 us: body(): jnp.einsum('hqk,qhd->khd', score_grad, pair_queries, preferred_element_ty...]
  transfers between devices with their start and end apart: 14 -> 16, of which waited for: 8 -> 5; matrix products, arithmetic and copies ran while one was open for 5% -> 34% of each run, Pallas kernels for 0% -> 0%
where the time goes in v1:
time: 170 us; the launch traced here: 168 us
  starting transfers between devices  64.5 us (38%)
  matrix products  34.3 us (20%)
  local copies, waits for them, and re-layouts  24.3 us (14%)
  waiting for transfers between devices  23.9 us (14%)
  other arithmetic  19.1 us (11%)
    ppermute x8, starting transfers between devices, ring(): lax.ppermute(value, axis, [(s, (s + steps) % size) for s in range(size)])  21.4 us
    all_to_all x1, starting transfers between devices, body(): lax.all_to_all(jnp.broadcast_to(w_out[None], (groups,) + w_out.shape), CO...  13.6 us
    ppermute x4, starting transfers between devices, shift(): return lax.ppermute(value, BLK, pairs)  12.8 us
    ppermute x4, waiting for transfers between devices, shift(): return lax.ppermute(value, BLK, pairs)  10.7 us
    dot_general x4, matrix products, body(): jnp.einsum('hqk,khd->qhd', score_grad, keyed, preferred_element_type=jnp....  8.56 us
    unnamed x112, local copies, waits for them, and re-layouts  7.6 us
    all_to_all x1, starting transfers between devices, body(): lax.all_to_all(hg.astype(jnp.bfloat16).reshape(members, rows, groups * un...  6.62 us
    dot_general x4, matrix products, body(): jnp.einsum('hqk,qhd->khd', score_grad, pair_queries, preferred_element_ty...  5.68 us
  transfers between devices with their start and end apart: 16, of which 5 were waited for; matrix products, arithmetic and copies ran while one was open for 34% of the time, Pallas kernels for 0%

profile of v1, /device:TPU:1, one launch (start us, length us, event | category | flops | bytes accessed | tf_op | source)
XLA Modules:
  0.0 167.9 jit_solution(4797555363970862274)
XLA Ops:
  4.0 4.9 %collective-permute-start = (bf16[256,1024]{1,0:T(8,128)(2,1)}, bf16[256,1024]{1,0:T(8,128)(2,1)}, u32[]{:S(2)}, u32[]{:S(2)}) collective-permute-start(bf16[256,1024]{1,0:T(8,128)(2,1)} %constant_dynamic-update-slice_fusion), channel_id=1, source_target_pairs={{0,8},{4,12},{8,16},{12,20},{16,24},{20,28},{24,32},{28,36},{32,40... | collective-permute-start | bytes 1572872 | tf_op jit(solution)/shard_map/ppermute | solution.py:18
  8.9 5.2 %collective-permute-start.3 = (bf16[256,1024]{1,0:T(8,128)(2,1)}, bf16[256,1024]{1,0:T(8,128)(2,1)}, u32[]{:S(2)}, u32[]{:S(2)}) collective-permute-start(bf16[256,1024]{1,0:T(8,128)(2,1)} %constant_dynamic-update-slice_fusion), channel_id=1, source_target_pairs={{4,16},{12,24},{20,32},{28,40},{36,48},{44,56},{52,64},{60,72},{68... | collective-permute-start | bytes 1572872 | tf_op jit(solution)/shard_map/ppermute | solution.py:18
  14.1 4.9 %collective-permute-start.6 = (bf16[128,1024]{1,0:T(8,128)(2,1)}, bf16[128,1024]{1,0:T(8,128)(2,1)S(1)}, u32[]{:S(2)}, u32[]{:S(2)}) collective-permute-start(bf16[128,1024]{1,0:T(8,128)(2,1)} %param.14), channel_id=1, source_target_pairs={{0,24},{8,0},{16,8},{24,16},{1,25},{9,1},{17,9},{25,17},{2,26},{10... | collective-permute-start | bytes 786440 | tf_op jit(solution)/shard_map/ppermute | solution.py:22
  19.0 2.1 %collective-permute-start.5 = (bf16[128,1024]{1,0:T(8,128)(2,1)}, bf16[128,1024]{1,0:T(8,128)(2,1)S(1)}, u32[]{:S(2)}, u32[]{:S(2)}) collective-permute-start(bf16[128,1024]{1,0:T(8,128)(2,1)} %param.14), channel_id=1, source_target_pairs={{0,16},{8,24},{16,0},{24,8},{1,17},{9,25},{17,1},{25,9},{2,18},{10... | collective-permute-start | bytes 786440 | tf_op jit(solution)/shard_map/ppermute | solution.py:22
  21.1 2.3 %collective-permute-start.4 = (bf16[128,1024]{1,0:T(8,128)(2,1)}, bf16[128,1024]{1,0:T(8,128)(2,1)S(1)}, u32[]{:S(2)}, u32[]{:S(2)}) collective-permute-start(bf16[128,1024]{1,0:T(8,128)(2,1)} %param.14), channel_id=1, source_target_pairs={{0,8},{8,16},{16,24},{24,0},{1,9},{9,17},{17,25},{25,1},{2,10},{10... | collective-permute-start | bytes 786440 | tf_op jit(solution)/shard_map/ppermute | solution.py:22
  32.6 1.9 %collective-permute-start.2 = (bf16[384,1024]{1,0:T(8,128)(2,1)S(1)}, bf16[384,1024]{1,0:T(8,128)(2,1)S(1)}, u32[]{:S(2)}, u32[]{:S(2)}) collective-permute-start(bf16[384,1024]{1,0:T(8,128)(2,1)S(1)} %pad_maximum_fusion.2), channel_id=1, source_target_pairs={{0,4},{4,0},{1,5},{5,1},{2,6},{6,2},{3,7},{7,3},{8,12},{12,8},{9,1... | collective-permute-start | bytes 2359304 | tf_op jit(solution)/shard_map/ppermute | solution.py:22
  34.6 2.5 %collective-permute-done.4 = bf16[128,1024]{1,0:T(8,128)(2,1)S(1)} collective-permute-done((bf16[128,1024]{1,0:T(8,128)(2,1)}, bf16[128,1024]{1,0:T(8,128)(2,1)S(1)}, u32[]{:S(2)}, u32[]{:S(2)}) %collective-permute-start.4) | collective-permute-done | bytes 262176 | tf_op jit(solution)/shard_map/ppermute | solution.py:22
  38.2 1.9 %collective-permute-start.7 = (bf16[4,128,1024]{2,1,0:T(8,128)(2,1)}, bf16[4,128,1024]{2,1,0:T(8,128)(2,1)}, u32[]{:S(2)}, u32[]{:S(2)}) collective-permute-start(bf16[4,128,1024]{2,1,0:T(8,128)(2,1)} %pad_maximum_fusion.1), channel_id=1, source_target_pairs={{0,4},{4,0},{1,5},{5,1},{2,6},{6,2},{3,7},{7,3},{8,12},{12,8},{9,1... | collective-permute-start | bytes 3145736 | tf_op jit(solution)/shard_map/ppermute | solution.py:22
  40.1 2.4 %collective-permute-start.1 = (bf16[256,1024]{1,0:T(8,128)(2,1)}, bf16[256,1024]{1,0:T(8,128)(2,1)}, u32[]{:S(2)}, u32[]{:S(2)}) collective-permute-start(bf16[256,1024]{1,0:T(8,128)(2,1)} %collective-permute-done), channel_id=1, source_target_pairs={{0,4},{4,0},{1,5},{5,1},{2,6},{6,2},{3,7},{7,3},{8,12},{12,8},{9,1... | collective-permute-start | bytes 1572872 | tf_op jit(solution)/shard_map/ppermute | solution.py:22
  44.9 2.3 %convolution_bitcast_fusion.9 = f32[128,8,128]{0,2,1:T(8,128)} fusion(bf16[128,8,128]{0,2,1:T(8,128)(2,1)} %bitcast.241, f32[8,128,128]{1,2,0:T(8,128)S(1)} %fusion.26, f32[128,128]{0,1:T(8,128)S(1)} %copy.84), kind=kOutput, calls=%fused_computation.12 | convolution fusion | flops 34340864 | bytes 1376256 | tf_op jit(solution)/shard_map/hqk,khd->qhd/dot_general | solution.py:112
  57.0 5.5 %all-to-all-start.2 = ((bf16[8,128,128]{2,1,0:T(8,128)(2,1)}), bf16[8,128,128]{2,1,0:T(8,128)(2,1)S(1)}, u32[]{:S(2)}, u32[]{:S(2)}) async-start(bf16[8,128,128]{2,1,0:T(8,128)(2,1)} %bitcast.210), calls=%async_computation.2 | async-start | bytes 524288 | tf_op jit(solution)/shard_map/all_to_all | solution.py:125
  64.6 4.4 %all-to-all-done.2 = bf16[8,128,128]{2,1,0:T(8,128)(2,1)S(1)} async-done(((bf16[8,128,128]{2,1,0:T(8,128)(2,1)}), bf16[8,128,128]{2,1,0:T(8,128)(2,1)S(1)}, u32[]{:S(2)}, u32[]{:S(2)}) %all-to-all-start.2) | async-done | bytes 262176 | tf_op jit(solution)/shard_map/all_to_all | solution.py:125
  69.8 13.6 %all-to-all-start = ((bf16[16,8,1024]{2,1,0:T(8,128)(2,1)}), bf16[16,8,1024]{2,1,0:T(8,128)(2,1)}, u32[]{:S(2)}, u32[]{:S(2)}) async-start(bf16[16,8,1024]{2,1,0:T(8,128)(2,1)} %broadcast_in_dim.14), calls=%async_computation | async-start | bytes 524288 | tf_op jit(solution)/shard_map/all_to_all | solution.py:72
  85.8 2.1 %gather_fusion = bf16[4,2,128,1024]{3,2,1,0:T(8,128)(2,1)} fusion(bf16[4,2,128,1024]{3,2,0,1:T(8,128)(2,1)S(1)} %pad_maximum_fusion, s32[1024]{0:T(1024)} %pad_clamp_fusion), kind=kCustom, calls=%fused_computation | custom fusion | bytes 4194320 | tf_op jit(solution)/shard_map/jit(_take)/gather | solution.py:71
  88.0 1.9 %broadcast_select_fusion = bf16[4,2,128,1024]{3,2,1,0:T(8,128)(2,1)S(1)} fusion(bf16[4,2,128,1024]{3,2,1,0:T(8,128)(2,1)} %gather_fusion, pred[4]{0:T(512)(128)(4,1)S(1)} %copy-done.51), kind=kLoop, calls=%fused_computation.2 | loop fusion | flops 1048576 | bytes 4194308 | tf_op jit(solution)/shard_map/jit(_take)/select_n | solution.py:71
  89.8 1.9 %all-to-all-done = bf16[16,8,1024]{2,1,0:T(8,128)(2,1)} async-done(((bf16[16,8,1024]{2,1,0:T(8,128)(2,1)}), bf16[16,8,1024]{2,1,0:T(8,128)(2,1)}, u32[]{:S(2)}, u32[]{:S(2)}) %all-to-all-start) | async-done | bytes 262176 | tf_op jit(solution)/shard_map/all_to_all | solution.py:72
  91.7 2.4 %convolution_convert_fusion.1 = bf16[1024,128]{1,0:T(8,128)(2,1)} fusion(bf16[1024,1024]{1,0:T(8,128)(2,1)S(1)} %bitcast.211, bf16[16,8,1024]{2,1,0:T(8,128)(2,1)} %all-to-all-done), kind=kOutput, calls=%fused_computation.70 | convolution fusion | flops 268566528 | bytes 2621440 | tf_op jit(solution)/shard_map/te,de->td/dot_general | solution.py:75
  94.1 1.8 %copy.94 = bf16[8,128,128]{1,2,0:T(8,128)(2,1)} copy(bf16[8,128,128]{2,1,0:T(8,128)(2,1)} %bitcast.219) | data formatting | bytes 524288 | tf_op jit(solution)/shard_map/reshape | solution.py:76
  95.9 6.6 %all-to-all-start.1 = ((bf16[8,128,128]{1,2,0:T(8,128)(2,1)}), bf16[8,128,128]{1,2,0:T(8,128)(2,1)}, u32[]{:S(2)}, u32[]{:S(2)}) async-start(bf16[8,128,128]{1,2,0:T(8,128)(2,1)} %copy.94), calls=%async_computation.1 | async-start | bytes 524288 | tf_op jit(solution)/shard_map/all_to_all | solution.py:76
  102.5 2.2 %fusion.78 = f32[16,8,1024]{2,1,0:T(8,128)} fusion(bf16[1024,1024,1]{1,0,2:T(8,128)(2,1)S(1)} %bitcast.212, bf16[128,1024]{1,0:T(8,128)(2,1)} %copy.123), kind=kOutput, calls=%fused_computation.139 | convolution fusion | flops 268435456 | bytes 2883584 | tf_op jit(solution)/shard_map/tr,te->re/dot_general | solution.py:126
  104.7 4.4 %all-to-all-done.1 = bf16[8,128,128]{1,2,0:T(8,128)(2,1)} async-done(((bf16[8,128,128]{1,2,0:T(8,128)(2,1)}), bf16[8,128,128]{1,2,0:T(8,128)(2,1)}, u32[]{:S(2)}, u32[]{:S(2)}) %all-to-all-start.1) | async-done | bytes 262176 | tf_op jit(solution)/shard_map/all_to_all | solution.py:76
  109.1 4.6 %all-to-all-start.3 = ((f32[16,8,1024]{2,1,0:T(8,128)}), f32[16,8,1024]{2,1,0:T(8,128)S(1)}, u32[]{:S(2)}, u32[]{:S(2)}) async-start(f32[16,8,1024]{2,1,0:T(8,128)} %fusion.78), calls=%async_computation.3 | async-start | bytes 1048576 | tf_op jit(solution)/shard_map/all_to_all | solution.py:127
  113.7 2.6 %fusion.101 = (f32[128]{0:T(128)S(1)}, f32[128]{0:T(128)S(1)}, f32[128,1024]{1,0:T(8,128)S(1)}) fusion(bf16[128,1024]{1,0:T(8,128)(2,1)S(1)} %copy-done.2, f32[128]{0:T(128)S(1)} %copy-done.49, f32[128,1024]{1,0:T(8,128)S(1)} %copy.95, f32[128]{0:T(128)S(1)} %copy-done.46, bf16[128,1024]{0,1:T(8,128)(2,1)} %bitcast.24, bf16[1024,1024]{1,0:T(8,128)(2,1)} %constant.103.clone), kind=kOutput, calls=%fused_computation.162 | convolution fusion | flops 269352704 | bytes 3672064 | tf_op jit(solution)/shard_map/tp,dp->td/dot_general | solution.py:78
  118.2 2.3 %convolution_bitcast_fusion.4 = f32[128,8,128]{0,2,1:T(8,128)} fusion(bf16[128,8,128]{0,2,1:T(8,128)(2,1)S(1)} %bitcast.226, bf16[128,8,128]{0,2,1:T(8,128)(2,1)S(1)} %bitcast.249, bf16[128,8,128]{0,2,1:T(8,128)(2,1)} %bitcast.246, f32[8,128,128]{1,2,0:T(8,128)S(1)} %copy-done.29, f32[128,128]{0,1:T(8,128)} %copy.92), kind=kOutput, calls=%fused_computation.7 | convolution fusion | flops 68419584 | bytes 1900544 | tf_op jit(solution)/shard_map/hqk,khd->qhd/dot_general | solution.py:171
  120.5 2.4 %convolution_bitcast_fusion.5 = f32[128,8,128]{0,2,1:T(8,128)} fusion(bf16[128,8,128]{0,2,1:T(8,128)(2,1)S(1)} %bitcast.222, bf16[128,8,128]{0,2,1:T(8,128)(2,1)} %bitcast.250, bf16[128,8,128]{0,2,1:T(8,128)(2,1)S(1)} %bitcast.242, f32[8,128,128]{1,2,0:T(8,128)S(1)} %copy-done.25, f32[128,128]{0,1:T(8,128)} %copy-done.39), kind=kOutput, calls=%fused_computation.8 | convolution fusion | flops 68419584 | bytes 1900544 | tf_op jit(solution)/shard_map/hqk,khd->qhd/dot_general | solution.py:171
  125.2 3.2 %collective-permute-start.8 = (bf16[128,1024]{1,0:T(8,128)(2,1)S(1)}, bf16[128,1024]{1,0:T(8,128)(2,1)}, u32[]{:S(2)}, u32[]{:S(2)}) collective-permute-start(bf16[128,1024]{1,0:T(8,128)(2,1)S(1)} %get-tuple-element.20), channel_id=1, source_target_pairs={{0,4},{4,0},{1,5},{5,1},{2,6},{6,2},{3,7},{7,3},{8,12},{12,8},{9,1... | collective-permute-start | bytes 786440 | tf_op jit(solution)/shard_map/ppermute | solution.py:22
  132.3 2.8 %fusion.36 = bf16[128,8,128]{0,2,1:T(8,128)(2,1)} fusion(f32[128,8,128]{0,2,1:T(8,128)} %convolution_bitcast_fusion.4, f32[128,8,128]{0,2,1:T(8,128)} %convolution_bitcast_fusion.5, f32[128,8,128]{0,2,1:T(8,128)} %convolution_bitcast_fusion.7, bf16[128,8,128]{0,2,1:T(8,128)(2,1)S(1)} %bitcast.224, bf16[128,8,128]{0,2,1:T(8,128)(2,1)} %bitcast.252, ...), kind=kOutput, calls=%fused_computation.68 | convolution fusion | flops 69074944 | bytes 3211264 | tf_op jit(solution)/shard_map/hqk,khd->qhd/dot_general | solution.py:171
  135.1 1.8 %copy.124 = bf16[128,1024]{1,0:T(8,128)(2,1)} copy(bf16[128,1024]{0,1:T(8,128)(2,1)} %bitcast.258) | data formatting | bytes 524288
  136.9 1.9 %fusion.130 = f32[8,128,128]{2,1,0:T(8,128)} fusion(bf16[128,8,128]{0,2,1:T(8,128)(2,1)S(1)} %bitcast.253, f32[8,128,128]{2,1,0:T(8,128)S(1)} %copy-done.23, f32[128,128]{1,0:T(8,128)} %copy-done.42), kind=kOutput, calls=%fused_computation.230 | convolution fusion | flops 34340864 | bytes 1376256 | tf_op jit(solution)/shard_map/hqk,qhd->khd/dot_general | solution.py:185
  139.1 10.7 %collective-permute-done.9 = bf16[256,1024]{1,0:T(8,128)(2,1)} collective-permute-done((bf16[256,1024]{1,0:T(8,128)(2,1)}, bf16[256,1024]{1,0:T(8,128)(2,1)}, u32[]{:S(2)}, u32[]{:S(2)}) %collective-permute-start.9) | collective-permute-done | bytes 524320 | tf_op jit(solution)/shard_map/ppermute | solution.py:18
  149.8 2.7 %collective-permute-start.10 = (bf16[256,1024]{1,0:T(8,128)(2,1)}, bf16[256,1024]{1,0:T(8,128)(2,1)}, u32[]{:S(2)}, u32[]{:S(2)}) collective-permute-start(bf16[256,1024]{1,0:T(8,128)(2,1)} %collective-permute-done.9), channel_id=1, source_target_pairs={{0,4},{4,0},{1,5},{5,1},{2,6},{6,2},{3,7},{7,3},{8,12},{12,8},{9,1... | collective-permute-start | bytes 1572872 | tf_op jit(solution)/shard_map/ppermute | solution.py:22
  160.0 2.3 %convolution_bitcast_fusion.1 = f32[128,8,128]{0,2,1:T(8,128)} fusion(bf16[128,8,128]{0,2,1:T(8,128)(2,1)S(1)} %bitcast.228, bf16[128,8,128]{0,2,1:T(8,128)(2,1)} %bitcast.254, f32[8,128,128]{2,1,0:T(8,128)S(1)} %convolution_multiply_fusion, f32[128,128]{1,0:T(8,128)S(1)} %get-tuple-element.50, bf16[128,1024]{1,0:T(8,128)(2,1)S(1)} %copy-done.6), kind=kOutput, calls=%fused_computation.4 | convolution fusion | flops 68419584 | bytes 1900544 | tf_op jit(solution)/shard_map/hqk,qhd->khd/dot_general | solution.py:182
  (201 shorter events, 51.9 us)
Async XLA Ops:
  0.6 24.8 %copy-start = (bf16[128,1024]{1,0:T(8,128)(2,1)S(1)}, bf16[128,1024]{1,0:T(8,128)(2,1)}, u32[]{:S(2)}) copy-start(bf16[128,1024]{1,0:T(8,128)(2,1)} %param.9) | copy-start | bytes 786436
  0.6 23.9 %copy-start.3 = (bf16[128,1024]{1,0:T(8,128)(2,1)S(1)}, bf16[128,1024]{1,0:T(8,128)(2,1)}, u32[]{:S(2)}) copy-start(bf16[128,1024]{1,0:T(8,128)(2,1)} %param.8) | copy-start | bytes 786436
  4.0 27.4 %copy-start.5 = (bf16[128,1024]{1,0:T(8,128)(2,1)S(1)}, bf16[128,1024]{1,0:T(8,128)(2,1)}, u32[]{:S(2)}) copy-start(bf16[128,1024]{1,0:T(8,128)(2,1)} %param.10) | copy-start | bytes 786436
  4.0 36.1 %collective-permute-start = (bf16[256,1024]{1,0:T(8,128)(2,1)}, bf16[256,1024]{1,0:T(8,128)(2,1)}, u32[]{:S(2)}, u32[]{:S(2)}) collective-permute-start(bf16[256,1024]{1,0:T(8,128)(2,1)} %constant_dynamic-update-slice_fusion), channel_id=1, source_target_pairs={{0,8},{4,12},{8,16},{12,20},{16,24},{20,28},{24,32},{28,36},{32,40... | collective-permute-start | bytes 1572872 | tf_op jit(solution)/shard_map/ppermute | solution.py:18
  8.9 38.3 %collective-permute-start.3 = (bf16[256,1024]{1,0:T(8,128)(2,1)}, bf16[256,1024]{1,0:T(8,128)(2,1)}, u32[]{:S(2)}, u32[]{:S(2)}) collective-permute-start(bf16[256,1024]{1,0:T(8,128)(2,1)} %constant_dynamic-update-slice_fusion), channel_id=1, source_target_pairs={{4,16},{12,24},{20,32},{28,40},{36,48},{44,56},{52,64},{60,72},{68... | collective-permute-start | bytes 1572872 | tf_op jit(solution)/shard_map/ppermute | solution.py:18
  14.1 18.5 %collective-permute-start.6 = (bf16[128,1024]{1,0:T(8,128)(2,1)}, bf16[128,1024]{1,0:T(8,128)(2,1)S(1)}, u32[]{:S(2)}, u32[]{:S(2)}) collective-permute-start(bf16[128,1024]{1,0:T(8,128)(2,1)} %param.14), channel_id=1, source_target_pairs={{0,24},{8,0},{16,8},{24,16},{1,25},{9,1},{17,9},{25,17},{2,26},{10... | collective-permute-start | bytes 786440 | tf_op jit(solution)/shard_map/ppermute | solution.py:22
  19.0 15.6 %collective-permute-start.5 = (bf16[128,1024]{1,0:T(8,128)(2,1)}, bf16[128,1024]{1,0:T(8,128)(2,1)S(1)}, u32[]{:S(2)}, u32[]{:S(2)}) collective-permute-start(bf16[128,1024]{1,0:T(8,128)(2,1)} %param.14), channel_id=1, source_target_pairs={{0,16},{8,24},{16,0},{24,8},{1,17},{9,25},{17,1},{25,9},{2,18},{10... | collective-permute-start | bytes 786440 | tf_op jit(solution)/shard_map/ppermute | solution.py:22
  21.1 15.9 %collective-permute-start.4 = (bf16[128,1024]{1,0:T(8,128)(2,1)}, bf16[128,1024]{1,0:T(8,128)(2,1)S(1)}, u32[]{:S(2)}, u32[]{:S(2)}) collective-permute-start(bf16[128,1024]{1,0:T(8,128)(2,1)} %param.14), channel_id=1, source_target_pairs={{0,8},{8,16},{16,24},{24,0},{1,9},{9,17},{17,25},{25,1},{2,10},{10... | collective-permute-start | bytes 786440 | tf_op jit(solution)/shard_map/ppermute | solution.py:22
  25.5 11.6 %copy-start.13 = (bf16[128,1024]{1,0:T(8,128)(2,1)S(1)}, bf16[128,1024]{1,0:T(8,128)(2,1)}, u32[]{:S(2)}) copy-start(bf16[128,1024]{1,0:T(8,128)(2,1)} %param.14) | copy-start | bytes 786436
  31.3 13.6 %copy-start.39 = (f32[128,128]{0,1:T(8,128)}, f32[128,128]{0,1:T(8,128)S(1)}, u32[]{:S(2)}) copy-start(f32[128,128]{0,1:T(8,128)S(1)} %copy.84) | copy-start | bytes 196612
  32.6 12.0 %copy-start.15 = (bf16[128,1024]{1,0:T(8,128)(2,1)}, bf16[128,1024]{1,0:T(8,128)(2,1)S(1)}, u32[]{:S(2)}) copy-start(bf16[128,1024]{1,0:T(8,128)(2,1)S(1)} %collective-permute-done.6) | copy-start | bytes 786436
  32.6 14.6 %collective-permute-start.2 = (bf16[384,1024]{1,0:T(8,128)(2,1)S(1)}, bf16[384,1024]{1,0:T(8,128)(2,1)S(1)}, u32[]{:S(2)}, u32[]{:S(2)}) collective-permute-start(bf16[384,1024]{1,0:T(8,128)(2,1)S(1)} %pad_maximum_fusion.2), channel_id=1, source_target_pairs={{0,4},{4,0},{1,5},{5,1},{2,6},{6,2},{3,7},{7,3},{8,12},{12,8},{9,1... | collective-permute-start | bytes 2359304 | tf_op jit(solution)/shard_map/ppermute | solution.py:22
  34.6 10.0 %copy-start.17 = (bf16[128,1024]{1,0:T(8,128)(2,1)}, bf16[128,1024]{1,0:T(8,128)(2,1)S(1)}, u32[]{:S(2)}) copy-start(bf16[128,1024]{1,0:T(8,128)(2,1)S(1)} %collective-permute-done.5) | copy-start | bytes 786436
  38.2 46.0 %collective-permute-start.7 = (bf16[4,128,1024]{2,1,0:T(8,128)(2,1)}, bf16[4,128,1024]{2,1,0:T(8,128)(2,1)}, u32[]{:S(2)}, u32[]{:S(2)}) collective-permute-start(bf16[4,128,1024]{2,1,0:T(8,128)(2,1)} %pad_maximum_fusion.1), channel_id=1, source_target_pairs={{0,4},{4,0},{1,5},{5,1},{2,6},{6,2},{3,7},{7,3},{8,12},{12,8},{9,1... | collective-permute-start | bytes 3145736 | tf_op jit(solution)/shard_map/ppermute | solution.py:22
  40.1 7.1 %collective-permute-start.1 = (bf16[256,1024]{1,0:T(8,128)(2,1)}, bf16[256,1024]{1,0:T(8,128)(2,1)}, u32[]{:S(2)}, u32[]{:S(2)}) collective-permute-start(bf16[256,1024]{1,0:T(8,128)(2,1)} %collective-permute-done), channel_id=1, source_target_pairs={{0,4},{4,0},{1,5},{5,1},{2,6},{6,2},{3,7},{7,3},{8,12},{12,8},{9,1... | collective-permute-start | bytes 1572872 | tf_op jit(solution)/shard_map/ppermute | solution.py:22
  55.6 13.4 %copy-start.43 = (bf16[8,1024]{1,0:T(8,128)(2,1)S(1)}, bf16[8,1024]{1,0:T(8,128)(2,1)}, u32[]{:S(2)}) copy-start(bf16[8,1024]{1,0:T(8,128)(2,1)} %param.13) | copy-start | bytes 49156
  56.2 28.0 %copy-start.14 = (bf16[128,1024]{1,0:T(8,128)(2,1)S(1)}, bf16[128,1024]{1,0:T(8,128)(2,1)}, u32[]{:S(2)}) copy-start(bf16[128,1024]{1,0:T(8,128)(2,1)} %param.14) | copy-start | bytes 786436
  56.2 28.0 %copy-start.16 = (bf16[128,1024]{1,0:T(8,128)(2,1)S(1)}, bf16[128,1024]{1,0:T(8,128)(2,1)}, u32[]{:S(2)}) copy-start(bf16[128,1024]{1,0:T(8,128)(2,1)} %copy-done.15) | copy-start | bytes 786436
  56.2 28.0 %copy-start.18 = (bf16[128,1024]{1,0:T(8,128)(2,1)S(1)}, bf16[128,1024]{1,0:T(8,128)(2,1)}, u32[]{:S(2)}) copy-start(bf16[128,1024]{1,0:T(8,128)(2,1)} %copy-done.17) | copy-start | bytes 786436
  56.2 28.0 %copy-start.20 = (bf16[128,1024]{1,0:T(8,128)(2,1)S(1)}, bf16[128,1024]{1,0:T(8,128)(2,1)}, u32[]{:S(2)}) copy-start(bf16[128,1024]{1,0:T(8,128)(2,1)} %copy-done.19) | copy-start | bytes 786436
  57.0 12.1 %all-to-all-start.2 = ((bf16[8,128,128]{2,1,0:T(8,128)(2,1)}), bf16[8,128,128]{2,1,0:T(8,128)(2,1)S(1)}, u32[]{:S(2)}, u32[]{:S(2)}) async-start(bf16[8,128,128]{2,1,0:T(8,128)(2,1)} %bitcast.210), calls=%async_computation.2 | async-start | bytes 524288 | tf_op jit(solution)/shard_map/all_to_all | solution.py:125
  69.8 21.9 %all-to-all-start = ((bf16[16,8,1024]{2,1,0:T(8,128)(2,1)}), bf16[16,8,1024]{2,1,0:T(8,128)(2,1)}, u32[]{:S(2)}, u32[]{:S(2)}) async-start(bf16[16,8,1024]{2,1,0:T(8,128)(2,1)} %broadcast_in_dim.14), calls=%async_computation | async-start | bytes 524288 | tf_op jit(solution)/shard_map/all_to_all | solution.py:72
  95.9 13.2 %all-to-all-start.1 = ((bf16[8,128,128]{1,2,0:T(8,128)(2,1)}), bf16[8,128,128]{1,2,0:T(8,128)(2,1)}, u32[]{:S(2)}, u32[]{:S(2)}) async-start(bf16[8,128,128]{1,2,0:T(8,128)(2,1)} %copy.94), calls=%async_computation.1 | async-start | bytes 524288 | tf_op jit(solution)/shard_map/all_to_all | solution.py:76
  102.5 11.2 %copy-start.46 = (f32[128]{0:T(128)S(1)}, f32[128]{0:T(128)}, u32[]{:S(2)}) copy-start(f32[128]{0:T(128)} %copy-done.45) | copy-start | bytes 1540
  102.5 11.2 %copy-start.49 = (f32[128]{0:T(128)S(1)}, f32[128]{0:T(128)}, u32[]{:S(2)}) copy-start(f32[128]{0:T(128)} %copy-done.48) | copy-start | bytes 1540
  109.1 46.5 %all-to-all-start.3 = ((f32[16,8,1024]{2,1,0:T(8,128)}), f32[16,8,1024]{2,1,0:T(8,128)S(1)}, u32[]{:S(2)}, u32[]{:S(2)}) async-start(f32[16,8,1024]{2,1,0:T(8,128)} %fusion.78), calls=%async_computation.3 | async-start | bytes 1048576 | tf_op jit(solution)/shard_map/all_to_all | solution.py:127
  122.9 9.4 %copy-start.10 = (bf16[128,1024]{0,1:T(8,128)(2,1)S(1)}, bf16[128,1024]{0,1:T(8,128)(2,1)}, u32[]{:S(2)}) copy-start(bf16[128,1024]{0,1:T(8,128)(2,1)} %copy-done.9) | copy-start | bytes 786436
  125.2 31.1 %collective-permute-start.8 = (bf16[128,1024]{1,0:T(8,128)(2,1)S(1)}, bf16[128,1024]{1,0:T(8,128)(2,1)}, u32[]{:S(2)}, u32[]{:S(2)}) collective-permute-start(bf16[128,1024]{1,0:T(8,128)(2,1)S(1)} %get-tuple-element.20), channel_id=1, source_target_pairs={{0,4},{4,0},{1,5},{5,1},{2,6},{6,2},{3,7},{7,3},{8,12},{12,8},{9,1... | collective-permute-start | bytes 786440 | tf_op jit(solution)/shard_map/ppermute | solution.py:22
  128.4 21.4 %collective-permute-start.9 = (bf16[256,1024]{1,0:T(8,128)(2,1)}, bf16[256,1024]{1,0:T(8,128)(2,1)}, u32[]{:S(2)}, u32[]{:S(2)}) collective-permute-start(bf16[256,1024]{1,0:T(8,128)(2,1)} %pad_maximum_fusion.3), channel_id=1, source_target_pairs={{8,0},{12,4},{16,8},{20,12},{24,16},{28,20},{32,24},{36,28},{40,32... | collective-permute-start | bytes 1572872 | tf_op jit(solution)/shard_map/ppermute | solution.py:18
  129.7 26.6 %collective-permute-start.11 = (bf16[256,1024]{1,0:T(8,128)(2,1)}, bf16[256,1024]{1,0:T(8,128)(2,1)}, u32[]{:S(2)}, u32[]{:S(2)}) collective-permute-start(bf16[256,1024]{1,0:T(8,128)(2,1)} %pad_maximum_fusion.3), channel_id=1, source_target_pairs={{16,4},{24,12},{32,20},{40,28},{48,36},{56,44},{64,52},{72,60},{80... | collective-permute-start | bytes 1572872 | tf_op jit(solution)/shard_map/ppermute | solution.py:18
  138.9 15.4 %copy-start.38 = (f32[128,128]{1,0:T(8,128)S(1)}, f32[128,128]{1,0:T(8,128)}, u32[]{:S(2)}) copy-start(f32[128,128]{1,0:T(8,128)} %get-tuple-element.49) | copy-start | bytes 196612
  149.8 6.5 %collective-permute-start.10 = (bf16[256,1024]{1,0:T(8,128)(2,1)}, bf16[256,1024]{1,0:T(8,128)(2,1)}, u32[]{:S(2)}, u32[]{:S(2)}) collective-permute-start(bf16[256,1024]{1,0:T(8,128)(2,1)} %collective-permute-done.9), channel_id=1, source_target_pairs={{0,4},{4,0},{1,5},{5,1},{2,6},{6,2},{3,7},{7,3},{8,12},{12,8},{9,1... | collective-permute-start | bytes 1572872 | tf_op jit(solution)/shard_map/ppermute | solution.py:22
  (39 other events, 112.5 us)

commit v2 on v1

v2 whole, which is shorter than its diff:
```python
import functools

import jax
import jax.numpy as jnp
import numpy as np
from jax import lax
from jax.experimental import pallas as pl
from jax.experimental.pallas import tpu as pltpu
from jax.sharding import Mesh, PartitionSpec as P

DH = 128
REACH = 4
NY, NZ, NX, NC = 2, 8, 4, 2
COUNT = NY * NZ * NX * NC
BLK = ("y", "z", "x", "c")
ROW = ("x", "c")
COL = ("y", "z")
GROUPS, MEMBERS = NY * NZ, NX * NC
F32, BF16 = jnp.float32, jnp.bfloat16
SCALE = DH ** (-0.5)


def shift(value, steps, sources=None):
    pairs = [(s, s + steps) for s in (sources or range(COUNT)) if 0 <= s + steps < COUNT]
    return lax.ppermute(value, BLK, pairs)


def ring(value, axis, size, steps):
    return lax.ppermute(value, axis, [(s, (s + steps) % size) for s in range(size)])


def swap(value):
    return ring(value, "c", NC, 1)


def dot(a, b, contract):
    return lax.dot_general(a, b, ((contract[:1], contract[1:]), ((), ())), preferred_element_type=F32)


def sigmoid(s):
    return 0.5 * jnp.tanh(0.5 * s) + 0.5


class Loader:
    def __init__(self, sems):
        self.sems, self.used = sems, 0

    def start(self, source, target):
        copy = pltpu.make_async_copy(source, target, self.sems.at[self.used])
        self.used += 1
        copy.start()
        return copy

    def choose(self, condition, source, otherwise, target):
        sem = self.sems.at[self.used]
        self.used += 1

        @pl.when(condition)
        def _():
            pltpu.make_async_copy(source, target, sem).start()

        @pl.when(jnp.logical_not(condition))
        def _():
            pltpu.make_async_copy(otherwise, target, sem).start()

        return pltpu.make_async_copy(source, target, sem)


def allowed_pairs(segs, block, direction):
    rows = segs.shape[1]
    last = segs.shape[0] - 1
    own = jnp.broadcast_to(segs[pl.ds(block, 1), :].astype(F32), (rows, rows)).T
    line = lax.broadcasted_iota(jnp.int32, (rows, rows), 0)
    lane = lax.broadcasted_iota(jnp.int32, (rows, rows), 1)
    masks = []
    for offset in range(REACH):
        there = jnp.clip(block + direction * offset, 0, last)
        mask = own == segs[pl.ds(there, 1), :].astype(F32)
        ahead = direction * (lane - line)
        if offset == 0:
            mask = mask & (ahead >= 0)
        if offset == REACH - 1:
            mask = mask & (ahead <= 0)
        masks.append(mask)
    return jnp.concatenate(masks, 1)


def load_memory(load, even, kv, sib, chip, cross, far, kb, vb):
    rows = kv.shape[0] // 2
    copies = []
    for half, buffer in ((0, kb), (1, vb)):
        part = pl.ds(half * rows, rows)
        slot = lambda o: buffer.at[pl.ds(o * rows, rows), :]
        copies.append(load.start(kv.at[part, :], slot(0)))
        copies.append(load.choose(even, cross.at[part, :], sib.at[part, :], slot(1)))
        copies.append(load.start(chip.at[part, :], slot(2)))
        copies.append(load.choose(even, far.at[part, :], cross.at[part, :], slot(3)))
    return copies


def forward_kernel(
    info, seg, q, kv, sib, chip, cross, far, gate, perm,
    normed_o, rstd_o, hidden_o,
    segs, qb, kb, vb, gb, pb, att, sems,
):
    load = Loader(sems)
    even = info[1] == 0
    first = [load.start(seg, segs), load.start(q, qb)]
    first += load_memory(load, even, kv, sib, chip, cross, far, kb, vb)
    later = [load.start(gate, gb), load.start(perm, pb)]
    for copy in first:
        copy.wait()
    width = qb.shape[1]
    allowed = allowed_pairs(segs, info[0], -1)
    for h in range(width // DH):
        at = pl.ds(h * DH, DH)
        s = dot(qb[:, at], kb[:, at], (1, 1)) * SCALE
        weights = jnp.where(allowed, s * sigmoid(s), 0.0).astype(BF16)
        att[:, at] = dot(weights, vb[:, at], (1, 0))
    attended = att[...]
    mean = jnp.mean(attended, axis=1, keepdims=True)
    centred = attended - mean
    rstd = lax.rsqrt(jnp.mean(centred * centred, axis=1, keepdims=True) + 1e-05)
    normed = centred * rstd
    normed_o[...] = normed
    rstd_o[...] = jnp.broadcast_to(rstd, rstd_o.shape)
    for copy in later:
        copy.wait()
    hidden = (normed * gb[...].astype(F32)).astype(BF16)
    placed = dot(hidden, pb[...], (1, 0)).astype(BF16)
    for k in range(hidden_o.shape[0]):
        hidden_o[k] = placed[:, k * DH:(k + 1) * DH]


def columns_kernel(info, rel, other, w_sub, out):
    rows = out.shape[1]
    for who, block in ((0, rel), (1, other)):
        product = dot(block[...], w_sub[...], (1, 1)).astype(BF16)
        for r in range(NX):
            x = lax.rem(info[2] - r + NX, NX)
            c = info[1] if who == 0 else 1 - info[1]
            out[x * NC + c] = product[r * rows:(r + 1) * rows]


def weight_kernel(info, rel, other, hidden, out):
    total = None
    for who, block in ((0, rel), (1, other)):
        pieces = []
        for r in range(NX):
            x = lax.rem(info[2] - r + NX, NX)
            c = info[1] if who == 0 else 1 - info[1]
            pieces.append(hidden[x * NC + c])
        product = dot(jnp.concatenate(pieces, 0), block[...], (0, 0))
        total = product if total is None else total + product
    out[...] = total


def upstream_kernel(hg, normed, rstd, gate, q, perm, gate_o, uq_o):
    rows = q.shape[0]
    placed = jnp.concatenate([hg[k] for k in range(hg.shape[0])], 1)
    hidden_grad = dot(placed, perm[...], (1, 1))
    n = normed[...]
    gate_o[...] = (hidden_grad * n).astype(BF16)
    normed_grad = hidden_grad * gate[...].astype(F32)
    inner = (
        normed_grad
        - jnp.mean(normed_grad, axis=1, keepdims=True)
        - n * jnp.mean(normed_grad * n, axis=1, keepdims=True)
    )
    uq_o[:rows] = (rstd[:, :1] * inner).astype(BF16)
    uq_o[rows:] = q[...]


def query_kernel(
    info, seg, uq, kv, sib, chip, cross, far,
    query_o,
    segs, ub, kb, vb, sems,
):
    load = Loader(sems)
    even = info[1] == 0
    copies = [load.start(seg, segs), load.start(uq, ub)]
    copies += load_memory(load, even, kv, sib, chip, cross, far, kb, vb)
    for copy in copies:
        copy.wait()
    rows, width = query_o.shape
    allowed = allowed_pairs(segs, info[0], -1)
    for h in range(width // DH):
        at = pl.ds(h * DH, DH)
        keyed = kb[:, at]
        s = dot(ub[rows:, at], keyed, (1, 1)) * SCALE
        sigma = sigmoid(s)
        weight_grad = dot(ub[:rows, at], vb[:, at], (1, 1))
        score_grad = jnp.where(allowed, weight_grad * sigma * (1.0 + s * (1.0 - sigma)), 0.0)
        query_o[:, at] = (dot(score_grad.astype(BF16), keyed, (1, 0)) * SCALE).astype(BF16)


def memory_kernel(
    info, seg, kv, uq, sib, chip, cross, far,
    key_o, value_o,
    segs, kvb, ub, qb, sems,
):
    load = Loader(sems)
    even = info[1] == 0
    rows, width = key_o.shape
    copies = [load.start(seg, segs), load.start(kv, kvb)]
    for half, buffer in ((0, ub), (1, qb)):
        part = pl.ds(half * rows, rows)
        slot = lambda o: buffer.at[pl.ds(o * rows, rows), :]
        copies.append(load.start(uq.at[part, :], slot(0)))
        copies.append(load.choose(even, sib.at[part, :], cross.at[part, :], slot(1)))
        copies.append(load.start(chip.at[part, :], slot(2)))
        copies.append(load.choose(even, cross.at[part, :], far.at[part, :], slot(3)))
    for copy in copies:
        copy.wait()
    allowed = allowed_pairs(segs, info[0], 1)
    for h in range(width // DH):
        at = pl.ds(h * DH, DH)
        queries, upper = qb[:, at], ub[:, at]
        s = dot(kvb[:rows, at], queries, (1, 1)) * SCALE
        sigma = sigmoid(s)
        weights = jnp.where(allowed, s * sigma, 0.0).astype(BF16)
        weight_grad = dot(kvb[rows:, at], upper, (1, 1))
        score_grad = jnp.where(allowed, weight_grad * sigma * (1.0 + s * (1.0 - sigma)), 0.0)
        key_o[:, at] = (dot(score_grad.astype(BF16), queries, (1, 0)) * SCALE).astype(BF16)
        value_o[:, at] = dot(weights, upper, (1, 0)).astype(BF16)


def call(kernel, out_shape, kinds, scratch=(), cost=None):
    place = {"s": pltpu.SMEM, "v": pltpu.VMEM, "a": pl.ANY}
    outs = jax.tree.map(lambda _: pl.BlockSpec(memory_space=pltpu.VMEM), out_shape)
    return pl.pallas_call(
        kernel,
        out_shape=out_shape,
        in_specs=[pl.BlockSpec(memory_space=place[kind]) for kind in kinds],
        out_specs=outs,
        scratch_shapes=list(scratch),
        compiler_params=pltpu.CompilerParams(vmem_limit_bytes=40 * 1024 * 1024),
        cost_estimate=cost,
    )


def body(query_rows, key_rows, value_rows, gate_rows, segment, w_out, cotangent):
    rows, width = query_rows.shape
    device = lax.axis_index(BLK)
    info = jnp.stack([device, lax.axis_index("c"), lax.axis_index("x")]).astype(jnp.int32)
    seg = segment.reshape(-1, rows)
    unit = w_out.shape[0]
    span = REACH * rows

    natural = np.arange(width)
    placed = (natural // unit % MEMBERS) * (GROUPS * unit) + natural // (unit * MEMBERS) * unit + natural % unit
    perm = jnp.asarray(np.eye(width, dtype=np.float32)[:, np.argsort(placed)], BF16)

    def like(*shape, dtype=BF16):
        return jax.ShapeDtypeStruct(shape, dtype)

    def scratch(*shape, dtype=BF16):
        return pltpu.VMEM(shape, dtype)

    def cost(flops, size):
        return pl.CostEstimate(flops=flops, bytes_accessed=size, transcendentals=0)

    seg_scratch = scratch(*seg.shape, dtype=jnp.int32)
    sems = lambda n: pltpu.SemaphoreType.DMA((n,))

    kv = jnp.concatenate([key_rows, value_rows], 0)
    kv_chip = shift(kv, 2)
    kv_far = shift(kv, 3, range(1, COUNT, 2))
    kv_sib = swap(kv)
    kv_cross = swap(kv_chip)
    memory = (kv, kv_sib, kv_chip, kv_cross, kv_far)

    rel = jnp.concatenate([cotangent] + [ring(cotangent, "x", NX, k) for k in range(1, NX)], 0)
    other = swap(rel)
    w_sub = lax.all_to_all(
        jnp.broadcast_to(w_out[None], (GROUPS,) + w_out.shape), COL, 0, 0, tiled=True
    ).reshape(GROUPS * unit, width)
    hg = call(columns_kernel, like(MEMBERS, rows, GROUPS * unit), "svvv", cost=cost(268435456, 2 << 20))(
        info, rel, other, w_sub
    )
    hg = lax.all_to_all(hg, ROW, 0, 0, tiled=True)

    normed, rstd, hidden = call(
        forward_kernel,
        (like(rows, width, dtype=F32), like(rows, 128, dtype=F32), like(MEMBERS, rows, GROUPS * unit)),
        "s" + "a" * 9,
        [
            seg_scratch, scratch(rows, width), scratch(span, width), scratch(span, width),
            scratch(rows, width), scratch(width, width), scratch(rows, width, dtype=F32), sems(12),
        ],
        cost(536870912, 6 << 20),
    )(info, seg, query_rows, *memory, gate_rows, perm)

    hidden_all = lax.all_to_all(hidden, ROW, 0, 0, tiled=True)
    w_part = call(weight_kernel, like(GROUPS * unit, width, dtype=F32), "svvv", cost=cost(268435456, 3 << 20))(
        info, rel, other, hidden_all
    )
    w_parts = lax.all_to_all(w_part.reshape(GROUPS, unit, width), COL, 0, 0, tiled=True)
    w_grad = jnp.sum(w_parts, axis=0)

    gate_grad, uq = call(upstream_kernel, (like(rows, width), like(2 * rows, width)), "vvvvvv", cost=cost(268435456, 4 << 20))(
        hg, normed, rstd, gate_rows, query_rows, perm
    )

    uq_chip = shift(uq, -2)
    uq_far = shift(uq, -3, range(0, COUNT, 2))
    uq_sib = swap(uq)
    uq_cross = swap(uq_chip)

    query_grad = call(
        query_kernel,
        like(rows, width),
        "s" + "a" * 7,
        [seg_scratch, scratch(2 * rows, width), scratch(span, width), scratch(span, width), sems(10)],
        cost(536870912, 5 << 20),
    )(info, seg, uq, *memory)
    key_grad, value_grad = call(
        memory_kernel,
        (like(rows, width), like(rows, width)),
        "s" + "a" * 7,
        [seg_scratch, scratch(2 * rows, width), scratch(span, width), scratch(span, width), sems(10)],
        cost(671088640, 5 << 20),
    )(info, seg, kv, uq, uq_sib, uq_chip, uq_cross, uq_far)
    return (query_grad, key_grad, value_grad, gate_grad, w_grad)


def solution(mesh):
    fine = Mesh(
        mesh.devices.reshape(NY, NZ, NX, NC, mesh.devices.shape[1]), BLK + ("grp",)
    )
    every = ("grp",) + BLK
    rows = P(every, None)
    in_specs = (rows, rows, rows, rows, P("grp"), P(BLK, None), rows)
    return jax.shard_map(
        body, mesh=fine, in_specs=in_specs, out_specs=(rows,) * 5, check_vma=False
    )
```

time: 170 us -> 125 us (0.74)
  matrix products: 34.3 us -> 0 us
  Pallas kernels: 0 us -> 22.6 us
  other arithmetic: 19.1 us -> 1.77 us
  local copies, waits for them, and re-layouts: 24.3 us -> 10.8 us
  waiting for transfers between devices: 23.9 us -> 13.5 us
  starting transfers between devices: 64.5 us -> 74.3 us
    dot_general x28 -> x0, matrix products: 34.3 us -> none  [the longest x4 8.56 us: body(): jnp.einsum('hqk,khd->qhd', score_grad, keyed, preferred_element_type=jnp....]
    pallas_call x0 -> x6, Pallas kernels: none -> 22.6 us  [the longest x1 5.47 us: body(): call(memory_kernel, (like(rows, width), like(rows, width)), 's' + 'a' * 7...]
    ppermute x4, waiting for transfers between devices: 10.7 us -> 0.01 us  [shift(): return lax.ppermute(value, BLK, pairs)]
    ppermute x8, starting transfers between devices: 21.4 us -> 28 us  [ring(): lax.ppermute(value, axis, [(s, (s + steps) % size) for s in range(size)])]
    all_to_all x4, starting transfers between devices: 30.3 us -> 36.9 us  [the longest x1 11.9 us: body(): lax.all_to_all(w_part.reshape(GROUPS, unit, width), COL, 0, 0, tiled=True)]
    reshape x11 -> x0, local copies, waits for them, and re-layouts: 5.82 us -> none  [the longest x8 2.03 us: split(): return array.reshape(rows, heads, DH)]
    select_n x4 -> x0, other arithmetic: 4.85 us -> none  [the longest x2 1.86 us: body(): cot_abs = jnp.take(cot_rel, order, axis=0).reshape(members * rows, width)]
    slice x13 -> x0, local copies, waits for them, and re-layouts: 4.66 us -> none  [the longest x3 1.88 us: body(): valued = split(memory[offset][rows:])]
  transfers between devices with their start and end apart: 16 -> 16, of which waited for: 5 -> 2; matrix products, arithmetic and copies ran while one was open for 34% -> 5% of each run, Pallas kernels for 0% -> 14%
where the time goes in v2:
time: 125 us; the launch traced here: 124 us
  starting transfers between devices  74.3 us (59%)
  Pallas kernels  22.6 us (18%)
  waiting for transfers between devices  13.5 us (11%)
  local copies, waits for them, and re-layouts  10.8 us (9%)
  other arithmetic  1.77 us (1%)
    ppermute x8, starting transfers between devices, ring(): lax.ppermute(value, axis, [(s, (s + steps) % size) for s in range(size)])  28 us
    all_to_all x1, starting transfers between devices, body(): lax.all_to_all(w_part.reshape(GROUPS, unit, width), COL, 0, 0, tiled=True)  11.9 us
    all_to_all x1, starting transfers between devices, body(): lax.all_to_all(jnp.broadcast_to(w_out[None], (GROUPS,) + w_out.shape), CO...  11.1 us
    all_to_all x1, waiting for transfers between devices, body(): lax.all_to_all(w_part.reshape(GROUPS, unit, width), COL, 0, 0, tiled=True)  10.3 us
    ppermute x4, starting transfers between devices, shift(): return lax.ppermute(value, BLK, pairs)  9.38 us
    unnamed x34, local copies, waits for them, and re-layouts  9.3 us
    all_to_all x1, starting transfers between devices, body(): hg = lax.all_to_all(hg, ROW, 0, 0, tiled=True)  9.02 us
    pallas_call x1, Pallas kernels, body(): call(memory_kernel, (like(rows, width), like(rows, width)), 's' + 'a' * 7...  5.47 us
  transfers between devices with their start and end apart: 16, of which 2 were waited for; matrix products, arithmetic and copies ran while one was open for 5% of the time, Pallas kernels for 14%

profile of v2, /device:TPU:1, one launch (start us, length us, event | category | flops | bytes accessed | tf_op | source)
XLA Modules:
  0.0 123.9 jit_solution(1318778135126283682)
XLA Ops:
  0.7 4.1 %collective-permute-start = (bf16[128,1024]{1,0:T(8,128)(2,1)}, bf16[128,1024]{1,0:T(8,128)(2,1)S(1)}, u32[]{:S(2)}, u32[]{:S(2)}) collective-permute-start(bf16[128,1024]{1,0:T(8,128)(2,1)} %param.14), channel_id=1, source_target_pairs={{0,8},{8,16},{16,24},{24,0},{1,9},{9,17},{17,25},{25,1},{2,10},{10... | collective-permute-start | bytes 786440 | tf_op jit(solution)/shard_map/ppermute | solution.py:29
  4.8 4.4 %collective-permute-start.1 = (bf16[128,1024]{1,0:T(8,128)(2,1)}, bf16[128,1024]{1,0:T(8,128)(2,1)S(1)}, u32[]{:S(2)}, u32[]{:S(2)}) collective-permute-start(bf16[128,1024]{1,0:T(8,128)(2,1)} %param.14), channel_id=1, source_target_pairs={{0,16},{8,24},{16,0},{24,8},{1,17},{9,25},{17,1},{25,9},{2,18},{10... | collective-permute-start | bytes 786440 | tf_op jit(solution)/shard_map/ppermute | solution.py:29
  9.1 3.1 %collective-permute-start.2 = (bf16[128,1024]{1,0:T(8,128)(2,1)}, bf16[128,1024]{1,0:T(8,128)(2,1)S(1)}, u32[]{:S(2)}, u32[]{:S(2)}) collective-permute-start(bf16[128,1024]{1,0:T(8,128)(2,1)} %param.14), channel_id=1, source_target_pairs={{0,24},{8,0},{16,8},{24,16},{1,25},{9,1},{17,9},{25,17},{2,26},{10... | collective-permute-start | bytes 786440 | tf_op jit(solution)/shard_map/ppermute | solution.py:29
  12.2 1.7 %constant_dynamic-update-slice_fusion.3 = bf16[512,1024]{1,0:T(8,128)(2,1)} fusion(bf16[128,1024]{1,0:T(8,128)(2,1)} %param.14), kind=kLoop, calls=%fused_computation.3 | loop fusion | bytes 524288
  14.6 3.1 %collective-permute-done.1 = bf16[128,1024]{1,0:T(8,128)(2,1)S(1)} collective-permute-done((bf16[128,1024]{1,0:T(8,128)(2,1)}, bf16[128,1024]{1,0:T(8,128)(2,1)S(1)}, u32[]{:S(2)}, u32[]{:S(2)}) %collective-permute-start.1) | collective-permute-done | bytes 262176 | tf_op jit(solution)/shard_map/ppermute | solution.py:29
  17.7 0.7 constant_dynamic-update-slice_fusion.1
  19.2 7.3 %collective-permute-start.3 = (bf16[512,1024]{1,0:T(8,128)(2,1)}, bf16[512,1024]{1,0:T(8,128)(2,1)}, u32[]{:S(2)}, u32[]{:S(2)}) collective-permute-start(bf16[512,1024]{1,0:T(8,128)(2,1)} %constant_dynamic-update-slice_fusion.rel), channel_id=1, source_target_pairs={{0,4},{4,0},{1,5},{5,1},{2,6},{6,2},{3,7},{7,3},{8,12},{12,8},{9,1... | collective-permute-start | bytes 3145736 | tf_op jit(solution)/shard_map/ppermute | solution.py:29
  26.7 2.1 %collective-permute-start.5 = (bf16[256,1024]{1,0:T(8,128)(2,1)S(1)}, bf16[256,1024]{1,0:T(8,128)(2,1)S(1)}, u32[]{:S(2)}, u32[]{:S(2)}) collective-permute-start(bf16[256,1024]{1,0:T(8,128)(2,1)S(1)} %constant_dynamic-update-slice_fusion.4.kv), channel_id=1, source_target_pairs={{0,8},{4,12},{8,16},{12,20},{16,24},{20,28},{24,32},{28,36},{32,40... | collective-permute-start | bytes 1572872 | tf_op jit(solution)/shard_map/ppermute | solution.py:25
  29.5 11.1 %all-to-all-start = ((bf16[16,8,1024]{2,1,0:T(8,128)(2,1)}), bf16[16,8,1024]{2,1,0:T(8,128)(2,1)}, u32[]{:S(2)}, u32[]{:S(2)}) async-start(bf16[16,8,1024]{2,1,0:T(8,128)(2,1)} %broadcast_in_dim.2), calls=%async_computation | async-start | bytes 524288 | tf_op jit(solution)/shard_map/all_to_all | solution.py:275
  40.6 4.6 %collective-permute-start.7 = (bf16[256,1024]{1,0:T(8,128)(2,1)S(1)}, bf16[256,1024]{1,0:T(8,128)(2,1)}, u32[]{:S(2)}, u32[]{:S(2)}) collective-permute-start(bf16[256,1024]{1,0:T(8,128)(2,1)S(1)} %constant_dynamic-update-slice_fusion.4.kv), channel_id=1, source_target_pairs={{4,16},{12,24},{20,32},{28,40},{36,48},{44,56},{52,64},{60,72},{68... | collective-permute-start | bytes 1572872 | tf_op jit(solution)/shard_map/ppermute | solution.py:25
  45.2 1.9 %collective-permute-start.4 = (bf16[256,1024]{1,0:T(8,128)(2,1)S(1)}, bf16[256,1024]{1,0:T(8,128)(2,1)}, u32[]{:S(2)}, u32[]{:S(2)}) collective-permute-start(bf16[256,1024]{1,0:T(8,128)(2,1)S(1)} %constant_dynamic-update-slice_fusion.4.kv), channel_id=1, source_target_pairs={{0,4},{4,0},{1,5},{5,1},{2,6},{6,2},{3,7},{7,3},{8,12},{12,8},{9,1... | collective-permute-start | bytes 1572872 | tf_op jit(solution)/shard_map/ppermute | solution.py:29
  47.2 2.4 %collective-permute-start.6 = (bf16[256,1024]{1,0:T(8,128)(2,1)S(1)}, bf16[256,1024]{1,0:T(8,128)(2,1)}, u32[]{:S(2)}, u32[]{:S(2)}) collective-permute-start(bf16[256,1024]{1,0:T(8,128)(2,1)S(1)} %collective-permute-done.5.chip), channel_id=1, source_target_pairs={{0,4},{4,0},{1,5},{5,1},{2,6},{6,2},{3,7},{7,3},{8,12},{12,8},{9,1... | collective-permute-start | bytes 1572872 | tf_op jit(solution)/shard_map/ppermute | solution.py:29
  49.7 2.3 %shard_map.119 = bf16[8,128,128]{2,1,0:T(8,128)(2,1)S(1)} custom-call(s32[3]{0:T(128)S(1)} %pad_add_fusion.info, bf16[512,1024]{1,0:T(8,128)(2,1)} %constant_dynamic-update-slice_fusion.rel, bf16[512,1024]{1,0:T(8,128)(2,1)} %collective-permute-done.3.other, bf16[128,1024]{1,0:T(8,128)(2,1)} %bitcast.4.w_sub), custom_call_target="tpu_custom_call" | custom-call | flops 268435456 | bytes 2097152 | tf_op jit(solution)/shard_map/pallas_call | solution.py:278
  52.7 9.0 %all-to-all-start.1 = ((bf16[8,128,128]{2,1,0:T(8,128)(2,1)}), bf16[8,128,128]{2,1,0:T(8,128)(2,1)}, u32[]{:S(2)}, u32[]{:S(2)}) async-start(bf16[8,128,128]{2,1,0:T(8,128)(2,1)} %copy-done.7), calls=%async_computation.1 | async-start | bytes 524288 | tf_op jit(solution)/shard_map/all_to_all | solution.py:281
  61.8 0.9 copy-done.5
  62.7 4.5 %shard_map.120 = (f32[128,1024]{1,0:T(8,128)S(1)}, f32[128,128]{1,0:T(8,128)S(1)}, bf16[8,128,128]{2,1,0:T(8,128)(2,1)S(1)}) custom-call(s32[3]{0:T(128)S(1)} %pad_add_fusion.info, s32[128,128]{1,0:T(8,128)S(1)} %bitcast.6, bf16[128,1024]{1,0:T(8,128)(2,1)S(1)} %copy-done.3, bf16[256,1024]{1,0:T(8,128)(2,1)S(1)} %constant_dynamic-update-slice_fusion.4.kv, ...), custom_call_target="tpu_custom_call" | custom-call | flops 536870912 | bytes 6291456 | tf_op jit(solution)/shard_map/pallas_call | solution.py:283
  67.2 0.8 copy-done.9
  68.7 4.8 %all-to-all-start.2 = ((bf16[8,128,128]{2,1,0:T(8,128)(2,1)}), bf16[8,128,128]{2,1,0:T(8,128)(2,1)S(1)}, u32[]{:S(2)}, u32[]{:S(2)}) async-start(bf16[8,128,128]{2,1,0:T(8,128)(2,1)} %copy-done.11), calls=%async_computation.2 | async-start | bytes 524288 | tf_op jit(solution)/shard_map/all_to_all | solution.py:294
  73.5 0.9 copy-done.4
  74.5 0.9 copy-done.6
  75.4 1.0 copy-done.10
  76.5 2.5 %shard_map.121 = (bf16[128,1024]{1,0:T(8,128)(2,1)}, bf16[256,1024]{1,0:T(8,128)(2,1)S(1)}) custom-call(bf16[8,128,128]{2,1,0:T(8,128)(2,1)} %all-to-all-done.1.hg, f32[128,1024]{1,0:T(8,128)S(1)} %copy-done.10, f32[128,128]{1,0:T(8,128)S(1)} %get-tuple-element.13.rstd, bf16[128,1024]{1,0:T(8,128)(2,1)S(1)} %copy-done.6, bf16[128,1024]{1,0:T(8,128)(2,1)S(1)} %copy-done.4, ...), custom_call_target="tpu_custom_call" | custom-call | flops 268435456 | bytes 4194304 | tf_op jit(solution)/shard_map/pallas_call | solution.py:301
  79.0 1.4 %collective-permute-start.9 = (bf16[256,1024]{1,0:T(8,128)(2,1)S(1)}, bf16[256,1024]{1,0:T(8,128)(2,1)}, u32[]{:S(2)}, u32[]{:S(2)}) collective-permute-start(bf16[256,1024]{1,0:T(8,128)(2,1)S(1)} %get-tuple-element.14.uq), channel_id=1, source_target_pairs={{8,0},{12,4},{16,8},{20,12},{24,16},{28,20},{32,24},{36,28},{40,32... | collective-permute-start | bytes 1572872 | tf_op jit(solution)/shard_map/ppermute | solution.py:25
  80.4 2.9 %shard_map.124 = f32[128,1024]{1,0:T(8,128)} custom-call(s32[3]{0:T(128)S(1)} %pad_add_fusion.info, bf16[512,1024]{1,0:T(8,128)(2,1)} %constant_dynamic-update-slice_fusion.rel, bf16[512,1024]{1,0:T(8,128)(2,1)} %collective-permute-done.3.other, bf16[8,128,128]{2,1,0:T(8,128)(2,1)S(1)} %all-to-all-done.2.hidden), custom_call_target="tpu_custom_call" | custom-call | flops 268435456 | bytes 3145728 | tf_op jit(solution)/shard_map/pallas_call | solution.py:295
  83.3 11.9 %all-to-all-start.3 = ((f32[16,8,1024]{2,1,0:T(8,128)}), f32[16,8,1024]{2,1,0:T(8,128)}, u32[]{:S(2)}, u32[]{:S(2)}) async-start(f32[16,8,1024]{2,1,0:T(8,128)} %bitcast.5), calls=%async_computation.3 | async-start | bytes 1048576 | tf_op jit(solution)/shard_map/all_to_all | solution.py:298
  95.2 1.3 %collective-permute-start.11 = (bf16[256,1024]{1,0:T(8,128)(2,1)S(1)}, bf16[256,1024]{1,0:T(8,128)(2,1)}, u32[]{:S(2)}, u32[]{:S(2)}) collective-permute-start(bf16[256,1024]{1,0:T(8,128)(2,1)S(1)} %get-tuple-element.14.uq), channel_id=1, source_target_pairs={{16,4},{24,12},{32,20},{40,28},{48,36},{56,44},{64,52},{72,60},{80... | collective-permute-start | bytes 1572872 | tf_op jit(solution)/shard_map/ppermute | solution.py:25
  96.5 3.0 %collective-permute-start.8 = (bf16[256,1024]{1,0:T(8,128)(2,1)S(1)}, bf16[256,1024]{1,0:T(8,128)(2,1)}, u32[]{:S(2)}, u32[]{:S(2)}) collective-permute-start(bf16[256,1024]{1,0:T(8,128)(2,1)S(1)} %get-tuple-element.14.uq), channel_id=1, source_target_pairs={{0,4},{4,0},{1,5},{5,1},{2,6},{6,2},{3,7},{7,3},{8,12},{12,8},{9,1... | collective-permute-start | bytes 1572872 | tf_op jit(solution)/shard_map/ppermute | solution.py:29
  99.5 1.9 %collective-permute-start.10 = (bf16[256,1024]{1,0:T(8,128)(2,1)}, bf16[256,1024]{1,0:T(8,128)(2,1)}, u32[]{:S(2)}, u32[]{:S(2)}) collective-permute-start(bf16[256,1024]{1,0:T(8,128)(2,1)} %collective-permute-done.9.chip), channel_id=1, source_target_pairs={{0,4},{4,0},{1,5},{5,1},{2,6},{6,2},{3,7},{7,3},{8,12},{12,8},{9,1... | collective-permute-start | bytes 1572872 | tf_op jit(solution)/shard_map/ppermute | solution.py:29
  101.4 5.0 %shard_map.122 = bf16[128,1024]{1,0:T(8,128)(2,1)} custom-call(s32[3]{0:T(128)S(1)} %pad_add_fusion.info, s32[128,128]{1,0:T(8,128)S(1)} %bitcast.7, bf16[256,1024]{1,0:T(8,128)(2,1)S(1)} %get-tuple-element.14.uq, bf16[256,1024]{1,0:T(8,128)(2,1)S(1)} %constant_dynamic-update-slice_fusion.4.kv, bf16[256,1024]{1,0:T(8,128)(2,1)} %collective-permute-done.4.sib, ...), custom_call_target="tpu_custom_call" | custom-call | flops 536870912 | bytes 5242880 | tf_op jit(solution)/shard_map/pallas_call | solution.py:310
  106.4 10.3 %all-to-all-done.3 = f32[16,8,1024]{2,1,0:T(8,128)} async-done(((f32[16,8,1024]{2,1,0:T(8,128)}), f32[16,8,1024]{2,1,0:T(8,128)}, u32[]{:S(2)}, u32[]{:S(2)}) %all-to-all-start.3) | async-done | bytes 524320 | tf_op jit(solution)/shard_map/all_to_all | solution.py:298
  116.7 1.7 %reduce_sum.9 = f32[8,1024]{1,0:T(8,128)} reduce(f32[16,8,1024]{2,1,0:T(8,128)} %all-to-all-done.3, f32[]{:T(128)} %constant.28.clone.1), dimensions={0}, to_apply=%region_0.0 | reduce | flops 122880 | bytes 557060 | tf_op jit(solution)/shard_map/reduce_sum | solution.py:299
  118.4 5.5 %shard_map.123 = (bf16[128,1024]{1,0:T(8,128)(2,1)}, bf16[128,1024]{1,0:T(8,128)(2,1)}) custom-call(s32[3]{0:T(128)S(1)} %pad_add_fusion.info, s32[128,128]{1,0:T(8,128)S(1)} %bitcast.8, bf16[256,1024]{1,0:T(8,128)(2,1)S(1)} %constant_dynamic-update-slice_fusion.4.kv, bf16[256,1024]{1,0:T(8,128)(2,1)S(1)} %get-tuple-element.14.uq, ...), custom_call_target="tpu_custom_call" | custom-call | flops 671088640 | bytes 5242880 | tf_op jit(solution)/shard_map/pallas_call | solution.py:317
  (45 shorter events, 3.8 us)
Async XLA Ops:
  0.6 25.9 %copy-start.12 = (bf16[128,1024]{1,0:T(8,128)(2,1)S(1)}, bf16[128,1024]{1,0:T(8,128)(2,1)}, u32[]{:S(2)}) copy-start(bf16[128,1024]{1,0:T(8,128)(2,1)} %param.9) | copy-start | bytes 786436
  0.6 25.9 %copy-start.13 = (bf16[128,1024]{1,0:T(8,128)(2,1)S(1)}, bf16[128,1024]{1,0:T(8,128)(2,1)}, u32[]{:S(2)}) copy-start(bf16[128,1024]{1,0:T(8,128)(2,1)} %param.10) | copy-start | bytes 786436
  0.7 28.1 %copy-start.14 = (bf16[8,1024]{1,0:T(8,128)(2,1)S(1)}, bf16[8,1024]{1,0:T(8,128)(2,1)}, u32[]{:S(2)}) copy-start(bf16[8,1024]{1,0:T(8,128)(2,1)} %param.13) | copy-start | bytes 49156
  0.7 13.2 %collective-permute-start = (bf16[128,1024]{1,0:T(8,128)(2,1)}, bf16[128,1024]{1,0:T(8,128)(2,1)S(1)}, u32[]{:S(2)}, u32[]{:S(2)}) collective-permute-start(bf16[128,1024]{1,0:T(8,128)(2,1)} %param.14), channel_id=1, source_target_pairs={{0,8},{8,16},{16,24},{24,0},{1,9},{9,17},{17,25},{25,1},{2,10},{10... | collective-permute-start | bytes 786440 | tf_op jit(solution)/shard_map/ppermute | solution.py:29
  4.8 13.0 %collective-permute-start.1 = (bf16[128,1024]{1,0:T(8,128)(2,1)}, bf16[128,1024]{1,0:T(8,128)(2,1)S(1)}, u32[]{:S(2)}, u32[]{:S(2)}) collective-permute-start(bf16[128,1024]{1,0:T(8,128)(2,1)} %param.14), channel_id=1, source_target_pairs={{0,16},{8,24},{16,0},{24,8},{1,17},{9,25},{17,1},{25,9},{2,18},{10... | collective-permute-start | bytes 786440 | tf_op jit(solution)/shard_map/ppermute | solution.py:29
  9.1 9.4 %collective-permute-start.2 = (bf16[128,1024]{1,0:T(8,128)(2,1)}, bf16[128,1024]{1,0:T(8,128)(2,1)S(1)}, u32[]{:S(2)}, u32[]{:S(2)}) collective-permute-start(bf16[128,1024]{1,0:T(8,128)(2,1)} %param.14), channel_id=1, source_target_pairs={{0,24},{8,0},{16,8},{24,16},{1,25},{9,1},{17,9},{25,17},{2,26},{10... | collective-permute-start | bytes 786440 | tf_op jit(solution)/shard_map/ppermute | solution.py:29
  19.2 30.5 %collective-permute-start.3 = (bf16[512,1024]{1,0:T(8,128)(2,1)}, bf16[512,1024]{1,0:T(8,128)(2,1)}, u32[]{:S(2)}, u32[]{:S(2)}) collective-permute-start(bf16[512,1024]{1,0:T(8,128)(2,1)} %constant_dynamic-update-slice_fusion.rel), channel_id=1, source_target_pairs={{0,4},{4,0},{1,5},{5,1},{2,6},{6,2},{3,7},{7,3},{8,12},{12,8},{9,1... | collective-permute-start | bytes 3145736 | tf_op jit(solution)/shard_map/ppermute | solution.py:29
  26.6 35.1 %copy-start = (bf16[1024,1024]{1,0:T(8,128)(2,1)S(1)}, bf16[1024,1024]{1,0:T(8,128)(2,1)}, u32[]{:S(2)}) copy-start(bf16[1024,1024]{1,0:T(8,128)(2,1)} %constant.29.clone.perm) | copy-start | bytes 6291460
  26.6 35.1 %copy-start.3 = (bf16[128,1024]{1,0:T(8,128)(2,1)S(1)}, bf16[128,1024]{1,0:T(8,128)(2,1)}, u32[]{:S(2)}) copy-start(bf16[128,1024]{1,0:T(8,128)(2,1)} %q.3) | copy-start | bytes 786436
  26.6 35.1 %copy-start.8 = (s32[16384]{0:T(1024)S(1)}, s32[16384]{0:T(1024)}, u32[]{:S(2)}) copy-start(s32[16384]{0:T(1024)} %param.12) | copy-start | bytes 196612
  26.7 20.5 %collective-permute-start.5 = (bf16[256,1024]{1,0:T(8,128)(2,1)S(1)}, bf16[256,1024]{1,0:T(8,128)(2,1)S(1)}, u32[]{:S(2)}, u32[]{:S(2)}) collective-permute-start(bf16[256,1024]{1,0:T(8,128)(2,1)S(1)} %constant_dynamic-update-slice_fusion.4.kv), channel_id=1, source_target_pairs={{0,8},{4,12},{8,16},{12,20},{16,24},{20,28},{24,32},{28,36},{32,40... | collective-permute-start | bytes 1572872 | tf_op jit(solution)/shard_map/ppermute | solution.py:25
  29.5 20.2 %all-to-all-start = ((bf16[16,8,1024]{2,1,0:T(8,128)(2,1)}), bf16[16,8,1024]{2,1,0:T(8,128)(2,1)}, u32[]{:S(2)}, u32[]{:S(2)}) async-start(bf16[16,8,1024]{2,1,0:T(8,128)(2,1)} %broadcast_in_dim.2), calls=%async_computation | async-start | bytes 524288 | tf_op jit(solution)/shard_map/all_to_all | solution.py:275
  40.6 21.1 %collective-permute-start.7 = (bf16[256,1024]{1,0:T(8,128)(2,1)S(1)}, bf16[256,1024]{1,0:T(8,128)(2,1)}, u32[]{:S(2)}, u32[]{:S(2)}) collective-permute-start(bf16[256,1024]{1,0:T(8,128)(2,1)S(1)} %constant_dynamic-update-slice_fusion.4.kv), channel_id=1, source_target_pairs={{4,16},{12,24},{20,32},{28,40},{36,48},{44,56},{52,64},{60,72},{68... | collective-permute-start | bytes 1572872 | tf_op jit(solution)/shard_map/ppermute | solution.py:25
  45.2 16.5 %collective-permute-start.4 = (bf16[256,1024]{1,0:T(8,128)(2,1)S(1)}, bf16[256,1024]{1,0:T(8,128)(2,1)}, u32[]{:S(2)}, u32[]{:S(2)}) collective-permute-start(bf16[256,1024]{1,0:T(8,128)(2,1)S(1)} %constant_dynamic-update-slice_fusion.4.kv), channel_id=1, source_target_pairs={{0,4},{4,0},{1,5},{5,1},{2,6},{6,2},{3,7},{7,3},{8,12},{12,8},{9,1... | collective-permute-start | bytes 1572872 | tf_op jit(solution)/shard_map/ppermute | solution.py:29
  47.2 20.0 %copy-start.1 = (bf16[256,1024]{1,0:T(8,128)(2,1)}, bf16[256,1024]{1,0:T(8,128)(2,1)S(1)}, u32[]{:S(2)}) copy-start(bf16[256,1024]{1,0:T(8,128)(2,1)S(1)} %collective-permute-done.5.chip) | copy-start | bytes 1572868
  47.2 14.6 %collective-permute-start.6 = (bf16[256,1024]{1,0:T(8,128)(2,1)S(1)}, bf16[256,1024]{1,0:T(8,128)(2,1)}, u32[]{:S(2)}, u32[]{:S(2)}) collective-permute-start(bf16[256,1024]{1,0:T(8,128)(2,1)S(1)} %collective-permute-done.5.chip), channel_id=1, source_target_pairs={{0,4},{4,0},{1,5},{5,1},{2,6},{6,2},{3,7},{7,3},{8,12},{12,8},{9,1... | collective-permute-start | bytes 1572872 | tf_op jit(solution)/shard_map/ppermute | solution.py:29
  52.0 0.7 copy-start.7
  52.7 16.0 %all-to-all-start.1 = ((bf16[8,128,128]{2,1,0:T(8,128)(2,1)}), bf16[8,128,128]{2,1,0:T(8,128)(2,1)}, u32[]{:S(2)}, u32[]{:S(2)}) async-start(bf16[8,128,128]{2,1,0:T(8,128)(2,1)} %copy-done.7), calls=%async_computation.1 | async-start | bytes 524288 | tf_op jit(solution)/shard_map/all_to_all | solution.py:281
  61.8 1.0 copy-start.5
  67.2 0.8 copy-start.9
  68.0 0.7 copy-start.11
  68.7 11.7 %all-to-all-start.2 = ((bf16[8,128,128]{2,1,0:T(8,128)(2,1)}), bf16[8,128,128]{2,1,0:T(8,128)(2,1)S(1)}, u32[]{:S(2)}, u32[]{:S(2)}) async-start(bf16[8,128,128]{2,1,0:T(8,128)(2,1)} %copy-done.11), calls=%async_computation.2 | async-start | bytes 524288 | tf_op jit(solution)/shard_map/all_to_all | solution.py:294
  73.5 0.9 copy-start.4
  74.5 0.9 copy-start.6
  75.4 1.0 copy-start.10
  79.0 22.4 %copy-start.2 = (bf16[256,1024]{1,0:T(8,128)(2,1)S(1)}, bf16[256,1024]{1,0:T(8,128)(2,1)}, u32[]{:S(2)}) copy-start(bf16[256,1024]{1,0:T(8,128)(2,1)} %copy-done.1) | copy-start | bytes 1572868
  79.0 20.5 %collective-permute-start.9 = (bf16[256,1024]{1,0:T(8,128)(2,1)S(1)}, bf16[256,1024]{1,0:T(8,128)(2,1)}, u32[]{:S(2)}, u32[]{:S(2)}) collective-permute-start(bf16[256,1024]{1,0:T(8,128)(2,1)S(1)} %get-tuple-element.14.uq), channel_id=1, source_target_pairs={{8,0},{12,4},{16,8},{20,12},{24,16},{28,20},{32,24},{36,28},{40,32... | collective-permute-start | bytes 1572872 | tf_op jit(solution)/shard_map/ppermute | solution.py:25
  83.3 33.5 %all-to-all-start.3 = ((f32[16,8,1024]{2,1,0:T(8,128)}), f32[16,8,1024]{2,1,0:T(8,128)}, u32[]{:S(2)}, u32[]{:S(2)}) async-start(f32[16,8,1024]{2,1,0:T(8,128)} %bitcast.5), calls=%async_computation.3 | async-start | bytes 1048576 | tf_op jit(solution)/shard_map/all_to_all | solution.py:298
  95.2 23.2 %collective-permute-start.11 = (bf16[256,1024]{1,0:T(8,128)(2,1)S(1)}, bf16[256,1024]{1,0:T(8,128)(2,1)}, u32[]{:S(2)}, u32[]{:S(2)}) collective-permute-start(bf16[256,1024]{1,0:T(8,128)(2,1)S(1)} %get-tuple-element.14.uq), channel_id=1, source_target_pairs={{16,4},{24,12},{32,20},{40,28},{48,36},{56,44},{64,52},{72,60},{80... | collective-permute-start | bytes 1572872 | tf_op jit(solution)/shard_map/ppermute | solution.py:25
  96.5 21.9 %collective-permute-start.8 = (bf16[256,1024]{1,0:T(8,128)(2,1)S(1)}, bf16[256,1024]{1,0:T(8,128)(2,1)}, u32[]{:S(2)}, u32[]{:S(2)}) collective-permute-start(bf16[256,1024]{1,0:T(8,128)(2,1)S(1)} %get-tuple-element.14.uq), channel_id=1, source_target_pairs={{0,4},{4,0},{1,5},{5,1},{2,6},{6,2},{3,7},{7,3},{8,12},{12,8},{9,1... | collective-permute-start | bytes 1572872 | tf_op jit(solution)/shard_map/ppermute | solution.py:29
  99.5 18.9 %collective-permute-start.10 = (bf16[256,1024]{1,0:T(8,128)(2,1)}, bf16[256,1024]{1,0:T(8,128)(2,1)}, u32[]{:S(2)}, u32[]{:S(2)}) collective-permute-start(bf16[256,1024]{1,0:T(8,128)(2,1)} %collective-permute-done.9.chip), channel_id=1, source_target_pairs={{0,4},{4,0},{1,5},{5,1},{2,6},{6,2},{3,7},{7,3},{8,12},{12,8},{9,1... | collective-permute-start | bytes 1572872 | tf_op jit(solution)/shard_map/ppermute | solution.py:29

commit v3 on v2

v3 whole, which is shorter than its diff:
```python
import jax
import jax.numpy as jnp
import numpy as np
from jax import lax
from jax.experimental import pallas as pl
from jax.experimental.pallas import tpu as pltpu
from jax.sharding import Mesh, PartitionSpec as P

DH = 128
REACH = 4
NY, NZ, NX, NC = 2, 8, 4, 2
COUNT = NY * NZ * NX * NC
BLK = ("y", "z", "x", "c")
PLANE = ("y", "x")
CHIPS = NY * NZ * NX
F32, BF16 = jnp.float32, jnp.bfloat16
SCALE = DH ** (-0.5)
VMEM_LIMIT = 20 * 1024 * 1024


def shift(value, steps, sources=None):
    pairs = [(s, s + steps) for s in (sources or range(COUNT)) if 0 <= s + steps < COUNT]
    return lax.ppermute(value, BLK, pairs)


def ring(value, axis, size, steps):
    return lax.ppermute(value, axis, [(s, (s + steps) % size) for s in range(size)])


def swap(value):
    return ring(value, "c", NC, 1)


def dot(a, b, contract):
    return lax.dot_general(a, b, ((contract[:1], contract[1:]), ((), ())), preferred_element_type=F32)


def sigmoid(s):
    return 0.5 * jnp.tanh(0.5 * s) + 0.5


class Loader:
    def __init__(self, sems):
        self.sems, self.used = sems, 0

    def start(self, source, target):
        copy = pltpu.make_async_copy(source, target, self.sems.at[self.used])
        self.used += 1
        copy.start()
        return copy

    def choose(self, condition, source, otherwise, target):
        sem = self.sems.at[self.used]
        self.used += 1

        @pl.when(condition)
        def _():
            pltpu.make_async_copy(source, target, sem).start()

        @pl.when(jnp.logical_not(condition))
        def _():
            pltpu.make_async_copy(otherwise, target, sem).start()

        return pltpu.make_async_copy(source, target, sem)


def allowed_pairs(segs, block, direction):
    rows = segs.shape[1]
    last = segs.shape[0] - 1
    own = jnp.broadcast_to(segs[pl.ds(block, 1), :].astype(F32), (rows, rows)).T
    line = lax.broadcasted_iota(jnp.int32, (rows, rows), 0)
    lane = lax.broadcasted_iota(jnp.int32, (rows, rows), 1)
    masks = []
    for offset in range(REACH):
        there = jnp.clip(block + direction * offset, 0, last)
        mask = own == segs[pl.ds(there, 1), :].astype(F32)
        ahead = direction * (lane - line)
        if offset == 0:
            mask = mask & (ahead >= 0)
        if offset == REACH - 1:
            mask = mask & (ahead <= 0)
        masks.append(mask)
    return jnp.concatenate(masks, 1)


def load_memory(load, even, kv, k_pair, v_pair, chip, cross, far, kb, vb):
    rows = kv.shape[0] // 2
    copies = []
    for half, pair, buffer in ((0, k_pair, kb), (1, v_pair, vb)):
        part = pl.ds(half * rows, rows)
        slot = lambda o: buffer.at[pl.ds(o * rows, rows), :]
        copies.append(load.start(kv.at[part, :], slot(0)))
        copies.append(load.choose(even, cross.at[part, :], pair.at[pl.ds(0, rows), :], slot(1)))
        copies.append(load.start(chip.at[part, :], slot(2)))
        copies.append(load.choose(even, far.at[part, :], cross.at[part, :], slot(3)))
    return copies


def forward_kernel(
    info, seg, q, kv, k_pair, v_pair, chip, cross, far, gate, perm,
    normed_o, rstd_o, hidden_o,
    segs, qb, kb, vb, gb, pb, att, sems,
):
    load = Loader(sems)
    even = info[1] == 0
    first = [load.start(seg, segs), load.start(q, qb)]
    first += load_memory(load, even, kv, k_pair, v_pair, chip, cross, far, kb, vb)
    later = [load.start(gate, gb), load.start(perm, pb)]
    for copy in first:
        copy.wait()
    width = qb.shape[1]
    allowed = allowed_pairs(segs, info[0], -1)
    for h in range(width // DH):
        at = pl.ds(h * DH, DH)
        s = dot(qb[:, at], kb[:, at], (1, 1)) * SCALE
        weights = jnp.where(allowed, s * sigmoid(s), 0.0).astype(BF16)
        att[:, at] = dot(weights, vb[:, at], (1, 0))
    attended = att[...]
    mean = jnp.mean(attended, axis=1, keepdims=True)
    centred = attended - mean
    rstd = lax.rsqrt(jnp.mean(centred * centred, axis=1, keepdims=True) + 1e-05)
    normed = centred * rstd
    normed_o[...] = normed
    rstd_o[...] = jnp.broadcast_to(rstd, rstd_o.shape)
    for copy in later:
        copy.wait()
    hidden = (normed * gb[...].astype(F32)).astype(BF16)
    hidden_o[...] = dot(hidden, pb[...], (1, 0)).astype(BF16)


def columns_kernel(info, cot, w_sub, mine_o, sent_o, wb, sems):
    load = Loader(sems)
    rows, half = mine_o.shape
    step = half // 4
    chunks = [pl.ds(i * step, step) for i in range(half // step)]
    copies = [load.start(w_sub.at[chunk, :], wb.at[chunk, :]) for chunk in chunks]
    core = info[1]
    own = pl.ds(pl.multiple_of(core * rows, rows), rows)
    other = pl.ds(pl.multiple_of((1 - core) * rows, rows), rows)
    for chunk, copy in zip(chunks, copies):
        copy.wait()
        mine_o[:, chunk] = dot(cot[own, :], wb[chunk, :], (1, 1))
        sent_o[:, chunk] = dot(cot[other, :], wb[chunk, :], (1, 1))


def weight_kernel(info, hidden, cot, out):
    half = out.shape[0]
    columns = hidden[:, pl.ds(pl.multiple_of(info[1] * half, half), half)]
    out[...] = dot(columns, cot[...], (0, 0)).astype(BF16)


def upstream_kernel(info, mine, both, normed, rstd, gate, perm, gate_o, upper_o):
    rows = mine.shape[0]
    own = mine[...]
    even = info[1] == 0
    first = jnp.where(even, own, both[:rows])
    second = jnp.where(even, both[rows:], own)
    placed = jnp.concatenate([first, second], 1)
    high = placed.astype(BF16)
    low = (placed - high.astype(F32)).astype(BF16)
    hidden_grad = dot(high, perm[...], (1, 1)) + dot(low, perm[...], (1, 1))
    n = normed[...]
    gate_o[...] = (hidden_grad * n).astype(BF16)
    normed_grad = hidden_grad * gate[...].astype(F32)
    inner = (
        normed_grad
        - jnp.mean(normed_grad, axis=1, keepdims=True)
        - n * jnp.mean(normed_grad * n, axis=1, keepdims=True)
    )
    upper_o[...] = (rstd[:, :1] * inner).astype(BF16)


def query_kernel(
    info, seg, q, u, kv, k_pair, v_pair, chip, cross, far,
    query_o,
    segs, qb, ub, kb, vb, sems,
):
    load = Loader(sems)
    even = info[1] == 0
    copies = [load.start(seg, segs), load.start(q, qb), load.start(u, ub)]
    copies += load_memory(load, even, kv, k_pair, v_pair, chip, cross, far, kb, vb)
    for copy in copies:
        copy.wait()
    width = query_o.shape[1]
    allowed = allowed_pairs(segs, info[0], -1)
    for h in range(width // DH):
        at = pl.ds(h * DH, DH)
        keyed = kb[:, at]
        s = dot(qb[:, at], keyed, (1, 1)) * SCALE
        sigma = sigmoid(s)
        weight_grad = dot(ub[:, at], vb[:, at], (1, 1))
        score_grad = jnp.where(allowed, weight_grad * sigma * (1.0 + s * (1.0 - sigma)), 0.0)
        query_o[:, at] = (dot(score_grad.astype(BF16), keyed, (1, 0)) * SCALE).astype(BF16)


def memory_kernel(
    info, seg, kv, q, q_pair, q_chip, q_chips, q_far, u, u_pair, u_chip, u_chips, u_far,
    key_o, value_o,
    segs, kvb, qb, ub, sems,
):
    load = Loader(sems)
    even = info[1] == 0
    rows, width = key_o.shape
    copies = [load.start(seg, segs), load.start(kv, kvb)]
    slot = lambda buffer, o: buffer.at[pl.ds(o * rows, rows), :]
    first, second = pl.ds(0, rows), pl.ds(rows, rows)
    for buffer, own, pair, chip, chips, far in (
        (qb, q, q_pair, q_chip, q_chips, q_far),
        (ub, u, u_pair, u_chip, u_chips, u_far),
    ):
        copies.append(load.start(own, slot(buffer, 0)))
        copies.append(load.choose(even, pair.at[second, :], chips.at[first, :], slot(buffer, 1)))
        copies.append(load.start(chip, slot(buffer, 2)))
        copies.append(load.choose(even, chips.at[second, :], far, slot(buffer, 3)))
    for copy in copies:
        copy.wait()
    allowed = allowed_pairs(segs, info[0], 1)
    for h in range(width // DH):
        at = pl.ds(h * DH, DH)
        queries, upper = qb[:, at], ub[:, at]
        s = dot(kvb[:rows, at], queries, (1, 1)) * SCALE
        sigma = sigmoid(s)
        weights = jnp.where(allowed, s * sigma, 0.0).astype(BF16)
        weight_grad = dot(kvb[rows:, at], upper, (1, 1))
        score_grad = jnp.where(allowed, weight_grad * sigma * (1.0 + s * (1.0 - sigma)), 0.0)
        key_o[:, at] = (dot(score_grad.astype(BF16), queries, (1, 0)) * SCALE).astype(BF16)
        value_o[:, at] = dot(weights, upper, (1, 0)).astype(BF16)


def sum_kernel(parts, out):
    total = parts[0].astype(F32)
    for i in range(1, parts.shape[0]):
        total += parts[i].astype(F32)
    out[...] = total


def pack_kernel(key, value, out, sems):
    load = Loader(sems)
    rows = key.shape[0]
    copies = [load.start(key, out.at[pl.ds(0, rows), :]), load.start(value, out.at[pl.ds(rows, rows), :])]
    for copy in copies:
        copy.wait()


def call(kernel, out_shape, kinds, scratch=(), work=1000):
    place = {"s": pltpu.SMEM, "v": pltpu.VMEM, "a": pl.ANY, "h": pltpu.HBM}
    return pl.pallas_call(
        kernel,
        out_shape=out_shape,
        in_specs=[pl.BlockSpec(memory_space=place[kind]) for kind in kinds],
        out_specs=jax.tree.map(lambda _: pl.BlockSpec(memory_space=pltpu.VMEM), out_shape),
        scratch_shapes=list(scratch),
        compiler_params=pltpu.CompilerParams(vmem_limit_bytes=VMEM_LIMIT),
        cost_estimate=pl.CostEstimate(flops=work, bytes_accessed=1000, transcendentals=0),
    )


def body(query_rows, key_rows, value_rows, gate_rows, segment, w_out, cotangent):
    rows, width = query_rows.shape
    device = lax.axis_index(BLK)
    info = jnp.stack([device, lax.axis_index("c"), lax.axis_index("x")]).astype(jnp.int32)
    seg = segment.reshape(-1, rows)
    unit = w_out.shape[0]
    span = REACH * rows

    natural = np.arange(width)
    holder = natural // unit
    core, x, z, y = holder % NC, holder // NC % NX, holder // (NC * NX) % NZ, holder // (NC * NX * NZ)
    placed = (((core * NY + y) * NX + x) * NZ + z) * unit + natural % unit
    perm = jnp.asarray(np.eye(width, dtype=np.float32)[:, np.argsort(placed)], BF16)

    def like(*shape, dtype=BF16):
        return jax.ShapeDtypeStruct(shape, dtype)

    def scratch(*shape, dtype=BF16):
        return pltpu.VMEM(shape, dtype)

    seg_scratch = scratch(*seg.shape, dtype=jnp.int32)
    sems = lambda n: pltpu.SemaphoreType.DMA((n,))

    def pair(rows_of):
        return lax.all_gather(rows_of, "c", axis=0, tiled=True)

    def ahead(rows_of):
        return shift(rows_of, -2), shift(rows_of, -3, range(0, COUNT, 2))

    kv = call(pack_kernel, like(2 * rows, width), "hh", [sems(2)])(key_rows, value_rows)
    w_line = lax.all_to_all(
        jnp.broadcast_to(w_out[None], (NZ,) + w_out.shape), "z", 0, 0, tiled=True
    ).reshape(NZ * unit, width)
    kv_chip = shift(kv, 2)
    cot, k_pair, v_pair = pair(cotangent), pair(key_rows), pair(value_rows)
    kv_far = shift(kv, 3, range(1, COUNT, 2))
    q_chip, q_far = ahead(query_rows)
    kv_chip, kv_far, w_line, cot, k_pair, v_pair, q_chip, q_far = lax.optimization_barrier(
        (kv_chip, kv_far, w_line, cot, k_pair, v_pair, q_chip, q_far)
    )
    w_sub = lax.all_to_all(
        jnp.broadcast_to(w_line[None], (NY * NX,) + w_line.shape), PLANE, 0, 0, tiled=True
    ).reshape(CHIPS * unit, width)
    kv_cross = swap(kv_chip)
    memory = (kv, k_pair, v_pair, kv_chip, kv_cross, kv_far)

    normed, rstd, hidden = call(
        forward_kernel,
        (like(rows, width, dtype=F32), like(rows, 128, dtype=F32), like(rows, width)),
        "shhahhhhhhh",
        [
            seg_scratch, scratch(rows, width), scratch(span, width), scratch(span, width),
            scratch(rows, width), scratch(width, width), scratch(rows, width, dtype=F32), sems(12),
        ],
    )(info, seg, query_rows, *memory, gate_rows, perm)
    mine, sent = call(
        columns_kernel,
        (like(rows, CHIPS * unit, dtype=F32),) * 2,
        "svh",
        [scratch(CHIPS * unit, width), sems(4)],
    )(info, cot, w_sub)
    gate_grad, upper = call(upstream_kernel, (like(rows, width), like(rows, width)), "svvvvvv")(
        info, mine, pair(sent), normed, rstd, gate_rows, perm
    )

    u_chip, u_far = ahead(upper)
    u_pair = pair(upper)

    hidden, q_chip, q_far = lax.optimization_barrier((hidden, q_chip, q_far))
    q_pair, q_chips = pair(query_rows), pair(q_chip)
    w_part = call(weight_kernel, like(CHIPS * unit, width), "svv")(info, pair(hidden), cot)
    w_parts = lax.all_to_all(w_part.reshape(NY * NX, NZ * unit, width), PLANE, 0, 0, tiled=True)
    w_parts, _ = lax.optimization_barrier((w_parts, u_pair))
    w_sum = call(sum_kernel, like(NZ * unit, width, dtype=F32), "v")(w_parts).reshape(NZ, unit, width)
    w_line = lax.all_to_all(w_sum, "z", 0, 0, tiled=True)
    upper_late, _ = lax.optimization_barrier((upper, w_sum))
    query_grad = call(
        query_kernel,
        like(rows, width),
        "s" + "a" * 9,
        [
            seg_scratch, scratch(rows, width), scratch(rows, width), scratch(span, width), scratch(span, width),
            sems(11),
        ],
        20_000_000_000,
    )(info, seg, query_rows, upper_late, *memory)
    u_chip, _ = lax.optimization_barrier((u_chip, query_grad))
    u_chips = pair(u_chip)
    key_grad, value_grad = call(
        memory_kernel,
        (like(rows, width), like(rows, width)),
        "s" + "a" * 12,
        [seg_scratch, scratch(2 * rows, width), scratch(span, width), scratch(span, width), sems(10)],
        20_000_000_000,
    )(
        info, seg, kv, query_rows, q_pair, q_chip, q_chips, q_far,
        upper, u_pair, u_chip, u_chips, u_far,
    )
    w_line, _ = lax.optimization_barrier((w_line, key_grad))
    w_grad = call(sum_kernel, like(unit, width, dtype=F32), "v")(w_line)
    return (query_grad, key_grad, value_grad, gate_grad, w_grad)


def solution(mesh):
    fine = Mesh(
        mesh.devices.reshape(NY, NZ, NX, NC, mesh.devices.shape[1]), BLK + ("grp",)
    )
    every = ("grp",) + BLK
    rows = P(every, None)
    in_specs = (rows, rows, rows, rows, P("grp"), P(BLK, None), rows)
    return jax.shard_map(
        body, mesh=fine, in_specs=in_specs, out_specs=(rows,) * 5, check_vma=False
    )
```

time: 125 us -> 122 us (0.976)
  blocking collectives: 0 us -> 28.5 us
  starting transfers between devices: 74.3 us -> 54.5 us
  waiting for transfers between devices: 13.5 us -> 1.8 us
  Pallas kernels: 22.6 us -> 24.3 us
  other arithmetic: 1.77 us -> 0.08 us
    all_gather x0 -> x9, blocking collectives: none -> 28.5 us  [pair(): return lax.all_gather(rows_of, 'c', axis=0, tiled=True)]
    ppermute x8 -> x1, starting transfers between devices: 28 us -> 2.86 us  [ring(): lax.ppermute(value, axis, [(s, (s + steps) % size) for s in range(size)])]
    all_to_all x4, waiting for transfers between devices: 10.3 us -> 0.01 us  [the longest x1 0.01 us: body(): lax.all_to_all(jnp.broadcast_to(w_out[None], (NZ,) + w_out.shape), 'z', 0...]
    ppermute x4 -> x6, starting transfers between devices: 9.38 us -> 15.2 us  [shift(): return lax.ppermute(value, BLK, pairs)]
    broadcast_in_dim x1 -> x2, local copies, waits for them, and re-layouts: 0.73 us -> 3.4 us  [the longest x1 2.01 us: body(): jnp.broadcast_to(w_line[None], (NY * NX,) + w_line.shape)]
    pallas_call x5 -> x8, Pallas kernels: 18.1 us -> 19.9 us  [the longest x1 5.41 us: body(): call(memory_kernel, (like(rows, width), like(rows, width)), 's' + 'a' * 1...]
    reduce_sum x1 -> x0, other arithmetic: 1.69 us -> none  [body(): w_grad = jnp.sum(w_parts, axis=0)]
    unnamed x34, local copies, waits for them, and re-layouts: 9.3 us -> 7.72 us
  transfers between devices with their start and end apart: 16 -> 11, of which waited for: 2 -> 1; matrix products, arithmetic and copies ran while one was open for 5% -> 1% of each run, Pallas kernels for 14% -> 20%
where the time goes in v3:
time: 122 us; the launch traced here: 121 us
  starting transfers between devices  54.5 us (45%)
  blocking collectives  28.5 us (23%)
  Pallas kernels  24.3 us (20%)
  local copies, waits for them, and re-layouts  11.1 us (9%)
  waiting for transfers between devices  1.8 us (1%)
    all_gather x9, blocking collectives, pair(): return lax.all_gather(rows_of, 'c', axis=0, tiled=True)  28.5 us
    ppermute x6, starting transfers between devices, shift(): return lax.ppermute(value, BLK, pairs)  15.2 us
    all_to_all x1, starting transfers between devices, body(): lax.all_to_all(jnp.broadcast_to(w_out[None], (NZ,) + w_out.shape), 'z', 0...  13.9 us
    all_to_all x1, starting transfers between devices, body(): w_line = lax.all_to_all(w_sum, 'z', 0, 0, tiled=True)  10.3 us
    unnamed x34, local copies, waits for them, and re-layouts  7.72 us
    all_to_all x1, starting transfers between devices, body(): lax.all_to_all(jnp.broadcast_to(w_line[None], (NY * NX,) + w_line.shape),...  6.77 us
    all_to_all x1, starting transfers between devices, body(): lax.all_to_all(w_part.reshape(NY * NX, NZ * unit, width), PLANE, 0, 0, ti...  5.43 us
    pallas_call x1, Pallas kernels, body(): call(memory_kernel, (like(rows, width), like(rows, width)), 's' + 'a' * 1...  5.41 us
  transfers between devices with their start and end apart: 11, of which 1 were waited for; matrix products, arithmetic and copies ran while one was open for 1% of the time, Pallas kernels for 20%

profile of v3, /device:TPU:1, one launch (start us, length us, event | category | flops | bytes accessed | tf_op | source)
XLA Modules:
  0.0 121.1 jit_solution(345410839529382540)
XLA Ops:
  2.6 4.7 %collective-permute-start = (bf16[256,1024]{1,0:T(8,128)(2,1)S(1)}, bf16[256,1024]{1,0:T(8,128)(2,1)}, u32[]{:S(2)}, u32[]{:S(2)}) collective-permute-start(bf16[256,1024]{1,0:T(8,128)(2,1)S(1)} %shard_map.119.kv), channel_id=1, source_target_pairs={{0,8},{4,12},{8,16},{12,20},{16,24},{20,28},{24,32},{28,36},{32,40... | collective-permute-start | bytes 1572872 | tf_op jit(solution)/shard_map/ppermute | solution.py:23
  7.3 5.2 %collective-permute-start.1 = (bf16[256,1024]{1,0:T(8,128)(2,1)S(1)}, bf16[256,1024]{1,0:T(8,128)(2,1)}, u32[]{:S(2)}, u32[]{:S(2)}) collective-permute-start(bf16[256,1024]{1,0:T(8,128)(2,1)S(1)} %shard_map.119.kv), channel_id=1, source_target_pairs={{4,16},{12,24},{20,32},{28,40},{36,48},{44,56},{52,64},{60,72},{68... | collective-permute-start | bytes 1572872 | tf_op jit(solution)/shard_map/ppermute | solution.py:23
  12.6 1.3 %collective-permute-start.2 = (bf16[128,1024]{1,0:T(8,128)(2,1)}, bf16[128,1024]{1,0:T(8,128)(2,1)}, u32[]{:S(2)}, u32[]{:S(2)}) collective-permute-start(bf16[128,1024]{1,0:T(8,128)(2,1)} %q.5), channel_id=1, source_target_pairs={{8,0},{12,4},{16,8},{20,12},{24,16},{28,20},{32,24},{36,28},{40,32... | collective-permute-start | bytes 786440 | tf_op jit(solution)/shard_map/ppermute | solution.py:23
  13.9 1.3 %collective-permute-start.3 = (bf16[128,1024]{1,0:T(8,128)(2,1)}, bf16[128,1024]{1,0:T(8,128)(2,1)}, u32[]{:S(2)}, u32[]{:S(2)}) collective-permute-start(bf16[128,1024]{1,0:T(8,128)(2,1)} %q.5), channel_id=1, source_target_pairs={{16,4},{24,12},{32,20},{40,28},{48,36},{56,44},{64,52},{72,60},{80... | collective-permute-start | bytes 786440 | tf_op jit(solution)/shard_map/ppermute | solution.py:23
  15.2 1.4 %broadcast_in_dim.4 = bf16[8,8,1024]{2,1,0:T(8,128)(2,1)} broadcast(bf16[8,1024]{1,0:T(8,128)(2,1)} %param.13), dimensions={1,2} | broadcast | bytes 147456 | tf_op jit(solution)/shard_map/broadcast_in_dim | solution.py:289
  16.5 13.9 %all-to-all-start = ((bf16[8,8,1024]{2,1,0:T(8,128)(2,1)}), bf16[8,8,1024]{2,1,0:T(8,128)(2,1)}, u32[]{:S(2)}, u32[]{:S(2)}) async-start(bf16[8,8,1024]{2,1,0:T(8,128)(2,1)} %broadcast_in_dim.4), calls=%async_computation | async-start | bytes 262144 | tf_op jit(solution)/shard_map/all_to_all | solution.py:288
  30.4 4.2 %all_gather.28.k_pair = bf16[256,1024]{1,0:T(8,128)(2,1)} all-gather(bf16[128,1024]{1,0:T(8,128)(2,1)S(1)} %copy-done.9), channel_id=1, replica_groups=mesh['y'=2,'z'=8,'x'=4,'c'=2,'grp'=4] {'c'}, dimensions={0}, use_global_device_ids=true | all-gather | bytes 786432 | tf_op jit(solution)/shard_map/all_gather | solution.py:282
  34.6 2.3 %all_gather.29.v_pair = bf16[256,1024]{1,0:T(8,128)(2,1)} all-gather(bf16[128,1024]{1,0:T(8,128)(2,1)S(1)} %copy-done.10), channel_id=1, replica_groups=mesh['y'=2,'z'=8,'x'=4,'c'=2,'grp'=4] {'c'}, dimensions={0}, use_global_device_ids=true | all-gather | bytes 786432 | tf_op jit(solution)/shard_map/all_gather | solution.py:282
  36.9 2.5 %all_gather.27.cot = bf16[256,1024]{1,0:T(8,128)(2,1)S(1)} all-gather(bf16[128,1024]{1,0:T(8,128)(2,1)} %param.14), channel_id=1, replica_groups=mesh['y'=2,'z'=8,'x'=4,'c'=2,'grp'=4] {'c'}, dimensions={0}, use_global_device_ids=true | all-gather | bytes 786432 | tf_op jit(solution)/shard_map/all_gather | solution.py:282
  39.5 2.0 %broadcast_in_dim.5 = bf16[8,64,1024]{2,1,0:T(8,128)(2,1)} broadcast(bf16[64,1024]{1,0:T(8,128)(2,1)} %bitcast.4), dimensions={1,2} | broadcast | bytes 1179648 | tf_op jit(solution)/shard_map/broadcast_in_dim | solution.py:299
  41.5 6.8 %all-to-all-start.1 = ((bf16[8,64,1024]{2,1,0:T(8,128)(2,1)}), bf16[8,64,1024]{2,1,0:T(8,128)(2,1)}, u32[]{:S(2)}, u32[]{:S(2)}) async-start(bf16[8,64,1024]{2,1,0:T(8,128)(2,1)} %broadcast_in_dim.5), calls=%async_computation.1 | async-start | bytes 2097152 | tf_op jit(solution)/shard_map/all_to_all | solution.py:298
  48.3 2.9 %collective-permute-start.4 = (bf16[256,1024]{1,0:T(8,128)(2,1)}, bf16[256,1024]{1,0:T(8,128)(2,1)}, u32[]{:S(2)}, u32[]{:S(2)}) collective-permute-start(bf16[256,1024]{1,0:T(8,128)(2,1)} %collective-permute-done.chip), channel_id=1, source_target_pairs={{0,4},{4,0},{1,5},{5,1},{2,6},{6,2},{3,7},{7,3},{8,12},{12,8},{9,1... | collective-permute-start | bytes 1572872 | tf_op jit(solution)/shard_map/ppermute | solution.py:27
  51.2 1.8 %collective-permute-done.4.cross = bf16[256,1024]{1,0:T(8,128)(2,1)} collective-permute-done((bf16[256,1024]{1,0:T(8,128)(2,1)}, bf16[256,1024]{1,0:T(8,128)(2,1)}, u32[]{:S(2)}, u32[]{:S(2)}) %collective-permute-start.4) | collective-permute-done | bytes 524320 | tf_op jit(solution)/shard_map/ppermute | solution.py:27
  53.0 1.0 copy-done.2
  54.0 1.0 copy-done.4
  56.0 4.5 %shard_map.121 = (f32[128,1024]{1,0:T(8,128)S(1)}, f32[128,128]{1,0:T(8,128)S(1)}, bf16[128,1024]{1,0:T(8,128)(2,1)S(1)}) custom-call(s32[3]{0:T(128)S(1)} %pad_add_fusion.info, s32[128,128]{1,0:T(8,128)S(1)} %bitcast.9, bf16[128,1024]{1,0:T(8,128)(2,1)S(1)} %copy-done.7, bf16[256,1024]{1,0:T(8,128)(2,1)S(1)} %shard_map.119.kv, ...), custom_call_target="tpu_custom_call" | custom-call | flops 1000 | bytes 1000 | tf_op jit(solution)/shard_map/pallas_call | solution.py:304
  61.3 2.3 %all_gather.31.hidden = bf16[256,1024]{1,0:T(8,128)(2,1)S(1)} all-gather(bf16[128,1024]{1,0:T(8,128)(2,1)S(1)} %get-tuple-element.43), channel_id=1, replica_groups=mesh['y'=2,'z'=8,'x'=4,'c'=2,'grp'=4] {'c'}, dimensions={0}, use_global_device_ids=true | all-gather | bytes 786432 | tf_op jit(solution)/shard_map/all_gather | solution.py:282
  65.6 5.4 %all-to-all-start.2 = ((bf16[8,64,1024]{2,1,0:T(8,128)(2,1)}), bf16[8,64,1024]{2,1,0:T(8,128)(2,1)}, u32[]{:S(2)}, u32[]{:S(2)}) async-start(bf16[8,64,1024]{2,1,0:T(8,128)(2,1)} %bitcast.8), calls=%async_computation.2 | async-start | bytes 2097152 | tf_op jit(solution)/shard_map/all_to_all | solution.py:329
  71.0 4.5 %all_gather.33.q_pair = bf16[256,1024]{1,0:T(8,128)(2,1)} all-gather(bf16[128,1024]{1,0:T(8,128)(2,1)} %q.5), channel_id=1, replica_groups=mesh['y'=2,'z'=8,'x'=4,'c'=2,'grp'=4] {'c'}, dimensions={0}, use_global_device_ids=true | all-gather | bytes 786432 | tf_op jit(solution)/shard_map/all_gather | solution.py:282
  75.5 3.8 %all_gather.34.q_chips = bf16[256,1024]{1,0:T(8,128)(2,1)} all-gather(bf16[128,1024]{1,0:T(8,128)(2,1)} %collective-permute-done.2.q_chip), channel_id=1, replica_groups=mesh['y'=2,'z'=8,'x'=4,'c'=2,'grp'=4] {'c'}, dimensions={0}, use_global_device_ids=true | all-gather | bytes 786432 | tf_op jit(solution)/shard_map/all_gather | solution.py:282
  79.3 2.8 %shard_map.120 = (f32[128,512]{1,0:T(8,128)S(1)}, f32[128,512]{1,0:T(8,128)S(1)}) custom-call(s32[3]{0:T(128)S(1)} %pad_add_fusion.info, bf16[256,1024]{1,0:T(8,128)(2,1)S(1)} %all_gather.27.cot, bf16[512,1024]{1,0:T(8,128)(2,1)} %bitcast.5.w_sub), custom_call_target="tpu_custom_call" | custom-call | flops 1000 | bytes 1000 | tf_op jit(solution)/shard_map/pallas_call | solution.py:313
  82.1 2.2 %all_gather.30.both = f32[256,512]{1,0:T(8,128)S(1)} all-gather(f32[128,512]{1,0:T(8,128)S(1)} %get-tuple-element.32), channel_id=1, replica_groups=mesh['y'=2,'z'=8,'x'=4,'c'=2,'grp'=4] {'c'}, dimensions={0}, use_global_device_ids=true | all-gather | bytes 786432 | tf_op jit(solution)/shard_map/all_gather | solution.py:282
  84.3 2.9 %shard_map.122 = (bf16[128,1024]{1,0:T(8,128)(2,1)}, bf16[128,1024]{1,0:T(8,128)(2,1)}) custom-call(s32[3]{0:T(128)S(1)} %pad_add_fusion.info, f32[128,512]{1,0:T(8,128)S(1)} %get-tuple-element.31.mine, f32[256,512]{1,0:T(8,128)S(1)} %all_gather.30.both, f32[128,1024]{1,0:T(8,128)S(1)} %copy-done.15, f32[128,128]{1,0:T(8,128)S(1)} %get-tuple-element.38.rstd, ...), custom_call_target="tpu_custom_call" | custom-call | flops 1000 | bytes 1000 | tf_op jit(solution)/shard_map/pallas_call | solution.py:319
  87.1 1.4 %collective-permute-start.5 = (bf16[128,1024]{1,0:T(8,128)(2,1)}, bf16[128,1024]{1,0:T(8,128)(2,1)}, u32[]{:S(2)}, u32[]{:S(2)}) collective-permute-start(bf16[128,1024]{1,0:T(8,128)(2,1)} %get-tuple-element.45.u), channel_id=1, source_target_pairs={{8,0},{12,4},{16,8},{20,12},{24,16},{28,20},{32,24},{36,28},{40,32... | collective-permute-start | bytes 786440 | tf_op jit(solution)/shard_map/ppermute | solution.py:23
  88.6 1.3 %collective-permute-start.6 = (bf16[128,1024]{1,0:T(8,128)(2,1)}, bf16[128,1024]{1,0:T(8,128)(2,1)}, u32[]{:S(2)}, u32[]{:S(2)}) collective-permute-start(bf16[128,1024]{1,0:T(8,128)(2,1)} %get-tuple-element.45.u), channel_id=1, source_target_pairs={{16,4},{24,12},{32,20},{40,28},{48,36},{56,44},{64,52},{72,60},{80... | collective-permute-start | bytes 786440 | tf_op jit(solution)/shard_map/ppermute | solution.py:23
  89.9 4.1 %all_gather.32.u_pair = bf16[256,1024]{1,0:T(8,128)(2,1)} all-gather(bf16[128,1024]{1,0:T(8,128)(2,1)} %get-tuple-element.45.u), channel_id=1, replica_groups=mesh['y'=2,'z'=8,'x'=4,'c'=2,'grp'=4] {'c'}, dimensions={0}, use_global_device_ids=true | all-gather | bytes 786432 | tf_op jit(solution)/shard_map/all_gather | solution.py:282
  94.0 2.1 %shard_map.124 = f32[64,1024]{1,0:T(8,128)} custom-call(bf16[8,64,1024]{2,1,0:T(8,128)(2,1)} %all-to-all-done.2.parts), custom_call_target="tpu_custom_call" | custom-call | flops 1000 | bytes 1000 | tf_op jit(solution)/shard_map/pallas_call | solution.py:331
  96.0 10.3 %all-to-all-start.3 = ((f32[8,8,1024]{2,1,0:T(8,128)}), f32[8,8,1024]{2,1,0:T(8,128)S(1)}, u32[]{:S(2)}, u32[]{:S(2)}) async-start(f32[8,8,1024]{2,1,0:T(8,128)} %bitcast.7), calls=%async_computation.3 | async-start | bytes 524288 | tf_op jit(solution)/shard_map/all_to_all | solution.py:332
  106.3 1.0 copy-done.5
  107.4 5.1 %shard_map.125 = bf16[128,1024]{1,0:T(8,128)(2,1)} custom-call(s32[3]{0:T(128)S(1)} %pad_add_fusion.info, s32[128,128]{1,0:T(8,128)S(1)} %bitcast.10, bf16[128,1024]{1,0:T(8,128)(2,1)S(1)} %copy-done.8, bf16[128,1024]{1,0:T(8,128)(2,1)} %get-tuple-element.45.u, bf16[256,1024]{1,0:T(8,128)(2,1)S(1)} %shard_map.119.kv, bf16[256,1024]{1,0:T(8,128)(2,1)S(1)} %copy-done.3, ...), custom_call_target="tpu_custom_call" | custom-call | flops 20000000000 | bytes 1000 | tf_op jit(solution)/shard_map/pallas_call | solution.py:334
  112.5 2.6 %all_gather.35.u_chips = bf16[256,1024]{1,0:T(8,128)(2,1)S(1)} all-gather(bf16[128,1024]{1,0:T(8,128)(2,1)} %collective-permute-done.5.u_chip), channel_id=1, replica_groups=mesh['y'=2,'z'=8,'x'=4,'c'=2,'grp'=4] {'c'}, dimensions={0}, use_global_device_ids=true | all-gather | bytes 786432 | tf_op jit(solution)/shard_map/all_gather | solution.py:282
  115.1 5.4 %shard_map.126 = (bf16[128,1024]{1,0:T(8,128)(2,1)}, bf16[128,1024]{1,0:T(8,128)(2,1)}) custom-call(s32[3]{0:T(128)S(1)} %pad_add_fusion.info, s32[128,128]{1,0:T(8,128)S(1)} %bitcast.11, bf16[256,1024]{1,0:T(8,128)(2,1)S(1)} %shard_map.119.kv, bf16[128,1024]{1,0:T(8,128)(2,1)S(1)} %copy-done.8, bf16[256,1024]{1,0:T(8,128)(2,1)S(1)} %copy-done.11, ...), custom_call_target="tpu_custom_call" | custom-call | flops 20000000000 | bytes 1000 | tf_op jit(solution)/shard_map/pallas_call | solution.py:346
  (45 shorter events, 6.4 us)
Async XLA Ops:
  0.6 1.0 copy-start.9
  1.6 0.9 copy-start.10
  2.6 36.9 %collective-permute-start = (bf16[256,1024]{1,0:T(8,128)(2,1)S(1)}, bf16[256,1024]{1,0:T(8,128)(2,1)}, u32[]{:S(2)}, u32[]{:S(2)}) collective-permute-start(bf16[256,1024]{1,0:T(8,128)(2,1)S(1)} %shard_map.119.kv), channel_id=1, source_target_pairs={{0,8},{4,12},{8,16},{12,20},{16,24},{20,28},{24,32},{28,36},{32,40... | collective-permute-start | bytes 1572872 | tf_op jit(solution)/shard_map/ppermute | solution.py:23
  7.3 32.1 %collective-permute-start.1 = (bf16[256,1024]{1,0:T(8,128)(2,1)S(1)}, bf16[256,1024]{1,0:T(8,128)(2,1)}, u32[]{:S(2)}, u32[]{:S(2)}) collective-permute-start(bf16[256,1024]{1,0:T(8,128)(2,1)S(1)} %shard_map.119.kv), channel_id=1, source_target_pairs={{4,16},{12,24},{20,32},{28,40},{36,48},{44,56},{52,64},{60,72},{68... | collective-permute-start | bytes 1572872 | tf_op jit(solution)/shard_map/ppermute | solution.py:23
  12.6 26.9 %collective-permute-start.2 = (bf16[128,1024]{1,0:T(8,128)(2,1)}, bf16[128,1024]{1,0:T(8,128)(2,1)}, u32[]{:S(2)}, u32[]{:S(2)}) collective-permute-start(bf16[128,1024]{1,0:T(8,128)(2,1)} %q.5), channel_id=1, source_target_pairs={{8,0},{12,4},{16,8},{20,12},{24,16},{28,20},{32,24},{36,28},{40,32... | collective-permute-start | bytes 786440 | tf_op jit(solution)/shard_map/ppermute | solution.py:23
  13.9 25.6 %collective-permute-start.3 = (bf16[128,1024]{1,0:T(8,128)(2,1)}, bf16[128,1024]{1,0:T(8,128)(2,1)}, u32[]{:S(2)}, u32[]{:S(2)}) collective-permute-start(bf16[128,1024]{1,0:T(8,128)(2,1)} %q.5), channel_id=1, source_target_pairs={{16,4},{24,12},{32,20},{40,28},{48,36},{56,44},{64,52},{72,60},{80... | collective-permute-start | bytes 786440 | tf_op jit(solution)/shard_map/ppermute | solution.py:23
  16.5 22.9 %all-to-all-start = ((bf16[8,8,1024]{2,1,0:T(8,128)(2,1)}), bf16[8,8,1024]{2,1,0:T(8,128)(2,1)}, u32[]{:S(2)}, u32[]{:S(2)}) async-start(bf16[8,8,1024]{2,1,0:T(8,128)(2,1)} %broadcast_in_dim.4), calls=%async_computation | async-start | bytes 262144 | tf_op jit(solution)/shard_map/all_to_all | solution.py:288
  36.9 16.1 %copy-start = (bf16[1024,1024]{1,0:T(8,128)(2,1)S(1)}, bf16[1024,1024]{1,0:T(8,128)(2,1)}, u32[]{:S(2)}) copy-start(bf16[1024,1024]{1,0:T(8,128)(2,1)} %constant.27.clone.perm) | copy-start | bytes 6291460
  36.9 16.1 %copy-start.6 = (bf16[128,1024]{1,0:T(8,128)(2,1)S(1)}, bf16[128,1024]{1,0:T(8,128)(2,1)}, u32[]{:S(2)}) copy-start(bf16[128,1024]{1,0:T(8,128)(2,1)} %gate.3) | copy-start | bytes 786436
  36.9 16.1 %copy-start.16 = (s32[16384]{0:T(1024)S(1)}, s32[16384]{0:T(1024)}, u32[]{:S(2)}) copy-start(s32[16384]{0:T(1024)} %param.12) | copy-start | bytes 196612
  41.5 24.1 %all-to-all-start.1 = ((bf16[8,64,1024]{2,1,0:T(8,128)(2,1)}), bf16[8,64,1024]{2,1,0:T(8,128)(2,1)}, u32[]{:S(2)}, u32[]{:S(2)}) async-start(bf16[8,64,1024]{2,1,0:T(8,128)(2,1)} %broadcast_in_dim.5), calls=%async_computation.1 | async-start | bytes 2097152 | tf_op jit(solution)/shard_map/all_to_all | solution.py:298
  48.3 4.7 %collective-permute-start.4 = (bf16[256,1024]{1,0:T(8,128)(2,1)}, bf16[256,1024]{1,0:T(8,128)(2,1)}, u32[]{:S(2)}, u32[]{:S(2)}) collective-permute-start(bf16[256,1024]{1,0:T(8,128)(2,1)} %collective-permute-done.chip), channel_id=1, source_target_pairs={{0,4},{4,0},{1,5},{5,1},{2,6},{6,2},{3,7},{7,3},{8,12},{12,8},{9,1... | collective-permute-start | bytes 1572872 | tf_op jit(solution)/shard_map/ppermute | solution.py:27
  53.0 1.0 copy-start.2
  54.0 1.0 copy-start.4
  55.1 0.9 copy-start.7
  60.5 0.8 copy-start.14
  64.6 1.0 copy-start.1
  65.6 28.4 %all-to-all-start.2 = ((bf16[8,64,1024]{2,1,0:T(8,128)(2,1)}), bf16[8,64,1024]{2,1,0:T(8,128)(2,1)}, u32[]{:S(2)}, u32[]{:S(2)}) async-start(bf16[8,64,1024]{2,1,0:T(8,128)(2,1)} %bitcast.8), calls=%async_computation.2 | async-start | bytes 2097152 | tf_op jit(solution)/shard_map/all_to_all | solution.py:329
  71.0 13.3 %copy-start.15 = (f32[128,1024]{1,0:T(8,128)S(1)}, f32[128,1024]{1,0:T(8,128)}, u32[]{:S(2)}) copy-start(f32[128,1024]{1,0:T(8,128)} %copy-done.14) | copy-start | bytes 1572868
  87.1 19.2 %copy-start.3 = (bf16[256,1024]{1,0:T(8,128)(2,1)S(1)}, bf16[256,1024]{1,0:T(8,128)(2,1)}, u32[]{:S(2)}) copy-start(bf16[256,1024]{1,0:T(8,128)(2,1)} %all_gather.28.k_pair) | copy-start | bytes 1572868
  87.1 19.2 %copy-start.8 = (bf16[128,1024]{1,0:T(8,128)(2,1)S(1)}, bf16[128,1024]{1,0:T(8,128)(2,1)}, u32[]{:S(2)}) copy-start(bf16[128,1024]{1,0:T(8,128)(2,1)} %q.5) | copy-start | bytes 786436
  87.1 25.3 %collective-permute-start.5 = (bf16[128,1024]{1,0:T(8,128)(2,1)}, bf16[128,1024]{1,0:T(8,128)(2,1)}, u32[]{:S(2)}, u32[]{:S(2)}) collective-permute-start(bf16[128,1024]{1,0:T(8,128)(2,1)} %get-tuple-element.45.u), channel_id=1, source_target_pairs={{8,0},{12,4},{16,8},{20,12},{24,16},{28,20},{32,24},{36,28},{40,32... | collective-permute-start | bytes 786440 | tf_op jit(solution)/shard_map/ppermute | solution.py:23
  88.6 26.5 %collective-permute-start.6 = (bf16[128,1024]{1,0:T(8,128)(2,1)}, bf16[128,1024]{1,0:T(8,128)(2,1)}, u32[]{:S(2)}, u32[]{:S(2)}) collective-permute-start(bf16[128,1024]{1,0:T(8,128)(2,1)} %get-tuple-element.45.u), channel_id=1, source_target_pairs={{16,4},{24,12},{32,20},{40,28},{48,36},{56,44},{64,52},{72,60},{80... | collective-permute-start | bytes 786440 | tf_op jit(solution)/shard_map/ppermute | solution.py:23
  96.0 24.5 %all-to-all-start.3 = ((f32[8,8,1024]{2,1,0:T(8,128)}), f32[8,8,1024]{2,1,0:T(8,128)S(1)}, u32[]{:S(2)}, u32[]{:S(2)}) async-start(f32[8,8,1024]{2,1,0:T(8,128)} %bitcast.7), calls=%async_computation.3 | async-start | bytes 524288 | tf_op jit(solution)/shard_map/all_to_all | solution.py:332
  106.3 1.0 copy-start.5
  107.4 7.7 %copy-start.11 = (bf16[256,1024]{1,0:T(8,128)(2,1)S(1)}, bf16[256,1024]{1,0:T(8,128)(2,1)}, u32[]{:S(2)}) copy-start(bf16[256,1024]{1,0:T(8,128)(2,1)} %all_gather.33.q_pair) | copy-start | bytes 1572868
  107.4 7.7 %copy-start.12 = (bf16[256,1024]{1,0:T(8,128)(2,1)S(1)}, bf16[256,1024]{1,0:T(8,128)(2,1)}, u32[]{:S(2)}) copy-start(bf16[256,1024]{1,0:T(8,128)(2,1)} %all_gather.34.q_chips) | copy-start | bytes 1572868
  107.4 7.7 %copy-start.13 = (bf16[256,1024]{1,0:T(8,128)(2,1)S(1)}, bf16[256,1024]{1,0:T(8,128)(2,1)}, u32[]{:S(2)}) copy-start(bf16[256,1024]{1,0:T(8,128)(2,1)} %all_gather.32.u_pair) | copy-start | bytes 1572868

commit v4 on v3

--- a/solution.py
+++ b/solution.py
@@ -16,6 +16,8 @@
 F32, BF16 = jnp.float32, jnp.bfloat16
 SCALE = DH ** (-0.5)
 VMEM_LIMIT = 20 * 1024 * 1024
+LARGE_LIMIT = 58 * 1024 * 1024
+HEADS_TOGETHER = 2
 
 
 def shift(value, steps, sources=None):
@@ -83,6 +85,11 @@
     return jnp.concatenate(masks, 1)
 
 
+def head_groups(width):
+    heads = [pl.ds(h * DH, DH) for h in range(width // DH)]
+    return [heads[i:i + HEADS_TOGETHER] for i in range(0, len(heads), HEADS_TOGETHER)]
+
+
 def load_memory(load, even, kv, k_pair, v_pair, chip, cross, far, kb, vb):
     rows = kv.shape[0] // 2
     copies = []
@@ -110,11 +117,11 @@
         copy.wait()
     width = qb.shape[1]
     allowed = allowed_pairs(segs, info[0], -1)
-    for h in range(width // DH):
-        at = pl.ds(h * DH, DH)
-        s = dot(qb[:, at], kb[:, at], (1, 1)) * SCALE
-        weights = jnp.where(allowed, s * sigmoid(s), 0.0).astype(BF16)
-        att[:, at] = dot(weights, vb[:, at], (1, 0))
+    for at in head_groups(width):
+        scores = [dot(qb[:, h], kb[:, h], (1, 1)) * SCALE for h in at]
+        weights = [jnp.where(allowed, s * sigmoid(s), 0.0).astype(BF16) for s in scores]
+        for h, w in zip(at, weights):
+            att[:, h] = dot(w, vb[:, h], (1, 0))
     attended = att[...]
     mean = jnp.mean(attended, axis=1, keepdims=True)
     centred = attended - mean
@@ -183,14 +190,16 @@
         copy.wait()
     width = query_o.shape[1]
     allowed = allowed_pairs(segs, info[0], -1)
-    for h in range(width // DH):
-        at = pl.ds(h * DH, DH)
-        keyed = kb[:, at]
-        s = dot(qb[:, at], keyed, (1, 1)) * SCALE
-        sigma = sigmoid(s)
-        weight_grad = dot(ub[:, at], vb[:, at], (1, 1))
-        score_grad = jnp.where(allowed, weight_grad * sigma * (1.0 + s * (1.0 - sigma)), 0.0)
-        query_o[:, at] = (dot(score_grad.astype(BF16), keyed, (1, 0)) * SCALE).astype(BF16)
+    for at in head_groups(width):
+        scores = [dot(qb[:, h], kb[:, h], (1, 1)) * SCALE for h in at]
+        weight_grads = [dot(ub[:, h], vb[:, h], (1, 1)) for h in at]
+        score_grads = []
+        for s, weight_grad in zip(scores, weight_grads):
+            sigma = sigmoid(s)
+            grad = jnp.where(allowed, weight_grad * (sigma * (1.0 + s * (1.0 - sigma))), 0.0)
+            score_grads.append(grad.astype(BF16))
+        for h, grad in zip(at, score_grads):
+            query_o[:, h] = (dot(grad, kb[:, h], (1, 0)) * SCALE).astype(BF16)
 
 
 def memory_kernel(
@@ -215,16 +224,18 @@
     for copy in copies:
         copy.wait()
     allowed = allowed_pairs(segs, info[0], 1)
-    for h in range(width // DH):
-        at = pl.ds(h * DH, DH)
-        queries, upper = qb[:, at], ub[:, at]
-        s = dot(kvb[:rows, at], queries, (1, 1)) * SCALE
-        sigma = sigmoid(s)
-        weights = jnp.where(allowed, s * sigma, 0.0).astype(BF16)
-        weight_grad = dot(kvb[rows:, at], upper, (1, 1))
-        score_grad = jnp.where(allowed, weight_grad * sigma * (1.0 + s * (1.0 - sigma)), 0.0)
-        key_o[:, at] = (dot(score_grad.astype(BF16), queries, (1, 0)) * SCALE).astype(BF16)
-        value_o[:, at] = dot(weights, upper, (1, 0)).astype(BF16)
+    for at in head_groups(width):
+        scores = [dot(kvb[:rows, h], qb[:, h], (1, 1)) * SCALE for h in at]
+        weight_grads = [dot(kvb[rows:, h], ub[:, h], (1, 1)) for h in at]
+        weights, score_grads = [], []
+        for s, weight_grad in zip(scores, weight_grads):
+            sigma = sigmoid(s)
+            weights.append(jnp.where(allowed, s * sigma, 0.0).astype(BF16))
+            grad = jnp.where(allowed, weight_grad * (sigma * (1.0 + s * (1.0 - sigma))), 0.0)
+            score_grads.append(grad.astype(BF16))
+        for h, w, grad in zip(at, weights, score_grads):
+            key_o[:, h] = (dot(grad, qb[:, h], (1, 0)) * SCALE).astype(BF16)
+            value_o[:, h] = dot(w, ub[:, h], (1, 0)).astype(BF16)
 
 
 def sum_kernel(parts, out):
@@ -242,7 +253,7 @@
         copy.wait()
 
 
-def call(kernel, out_shape, kinds, scratch=(), work=1000):
+def call(kernel, out_shape, kinds, scratch=(), work=1000, limit=VMEM_LIMIT):
     place = {"s": pltpu.SMEM, "v": pltpu.VMEM, "a": pl.ANY, "h": pltpu.HBM}
     return pl.pallas_call(
         kernel,
@@ -250,7 +261,7 @@
         in_specs=[pl.BlockSpec(memory_space=place[kind]) for kind in kinds],
         out_specs=jax.tree.map(lambda _: pl.BlockSpec(memory_space=pltpu.VMEM), out_shape),
         scratch_shapes=list(scratch),
-        compiler_params=pltpu.CompilerParams(vmem_limit_bytes=VMEM_LIMIT),
+        compiler_params=pltpu.CompilerParams(vmem_limit_bytes=limit),
         cost_estimate=pl.CostEstimate(flops=work, bytes_accessed=1000, transcendentals=0),
     )
 
@@ -309,6 +320,7 @@
             seg_scratch, scratch(rows, width), scratch(span, width), scratch(span, width),
             scratch(rows, width), scratch(width, width), scratch(rows, width, dtype=F32), sems(12),
         ],
+        limit=LARGE_LIMIT,
     )(info, seg, query_rows, *memory, gate_rows, perm)
     mine, sent = call(
         columns_kernel,
@@ -324,9 +336,10 @@
     u_pair = pair(upper)
 
     hidden, q_chip, q_far = lax.optimization_barrier((hidden, q_chip, q_far))
-    q_pair, q_chips = pair(query_rows), pair(q_chip)
     w_part = call(weight_kernel, like(CHIPS * unit, width), "svv")(info, pair(hidden), cot)
     w_parts = lax.all_to_all(w_part.reshape(NY * NX, NZ * unit, width), PLANE, 0, 0, tiled=True)
+    q_late, q_chip_late, _ = lax.optimization_barrier((query_rows, q_chip, u_pair))
+    q_pair, q_chips = pair(q_late), pair(q_chip_late)
     w_parts, _ = lax.optimization_barrier((w_parts, u_pair))
     w_sum = call(sum_kernel, like(NZ * unit, width, dtype=F32), "v")(w_parts).reshape(NZ, unit, width)
     w_line = lax.all_to_all(w_sum, "z", 0, 0, tiled=True)
@@ -340,6 +353,7 @@
             sems(11),
         ],
         20_000_000_000,
+        LARGE_LIMIT,
     )(info, seg, query_rows, upper_late, *memory)
     u_chip, _ = lax.optimization_barrier((u_chip, query_grad))
     u_chips = pair(u_chip)

time: 122 us -> 113 us (0.926)
  blocking collectives: 28.5 us -> 23.3 us
  local copies, waits for them, and re-layouts: 11.1 us -> 8.58 us
  starting transfers between devices: 54.5 us -> 52.5 us
    all_gather x9, blocking collectives: 28.5 us -> 23.3 us  [pair(): return lax.all_gather(rows_of, 'c', axis=0, tiled=True)]
    unnamed x34 -> x46, local copies, waits for them, and re-layouts: 7.72 us -> 5.98 us
  transfers between devices with their start and end apart: 11 -> 11, of which waited for: 1 -> 2; matrix products, arithmetic and copies ran while one was open for 1% -> 2% of each run, Pallas kernels for 20% -> 20%
where the time goes in v4:
time: 113 us; the launch traced here: 112 us
  starting transfers between devices  52.5 us (46%)
  Pallas kernels  23.5 us (21%)
  blocking collectives  23.3 us (21%)
  local copies, waits for them, and re-layouts  8.58 us (8%)
  waiting for transfers between devices  2.26 us (2%)
    all_gather x9, blocking collectives, pair(): return lax.all_gather(rows_of, 'c', axis=0, tiled=True)  23.3 us
    ppermute x6, starting transfers between devices, shift(): return lax.ppermute(value, BLK, pairs)  14.5 us
    all_to_all x1, starting transfers between devices, body(): lax.all_to_all(jnp.broadcast_to(w_out[None], (NZ,) + w_out.shape), 'z', 0...  13.9 us
    all_to_all x1, starting transfers between devices, body(): w_line = lax.all_to_all(w_sum, 'z', 0, 0, tiled=True)  11.1 us
    all_to_all x1, starting transfers between devices, body(): lax.all_to_all(jnp.broadcast_to(w_line[None], (NY * NX,) + w_line.shape),...  6.77 us
    unnamed x46, local copies, waits for them, and re-layouts  5.98 us
    pallas_call x1, Pallas kernels, body(): call(forward_kernel, (like(rows, width, dtype=F32), like(rows, 128, dtype...  5.16 us
    pallas_call x1, Pallas kernels, body(): call(query_kernel, like(rows, width), 's' + 'a' * 9, [seg_scratch, scratc...  5.09 us
  transfers between devices with their start and end apart: 11, of which 2 were waited for; matrix products, arithmetic and copies ran while one was open for 2% of the time, Pallas kernels for 20%

profile of v4, /device:TPU:1, one launch (start us, length us, event | category | flops | bytes accessed | tf_op | source)
XLA Modules:
  0.0 111.7 jit_solution(5359322417423701965)
XLA Ops:
  2.6 4.1 %collective-permute-start = (bf16[256,1024]{1,0:T(8,128)(2,1)S(1)}, bf16[256,1024]{1,0:T(8,128)(2,1)S(1)}, u32[]{:S(2)}, u32[]{:S(2)}) collective-permute-start(bf16[256,1024]{1,0:T(8,128)(2,1)S(1)} %shard_map.119.kv), channel_id=1, source_target_pairs={{0,8},{4,12},{8,16},{12,20},{16,24},{20,28},{24,32},{28,36},{32,40... | collective-permute-start | bytes 1572872 | tf_op jit(solution)/shard_map/ppermute | solution.py:25
  6.7 5.2 %collective-permute-start.1 = (bf16[256,1024]{1,0:T(8,128)(2,1)S(1)}, bf16[256,1024]{1,0:T(8,128)(2,1)S(1)}, u32[]{:S(2)}, u32[]{:S(2)}) collective-permute-start(bf16[256,1024]{1,0:T(8,128)(2,1)S(1)} %shard_map.119.kv), channel_id=1, source_target_pairs={{4,16},{12,24},{20,32},{28,40},{36,48},{44,56},{52,64},{60,72},{68... | collective-permute-start | bytes 1572872 | tf_op jit(solution)/shard_map/ppermute | solution.py:25
  11.9 1.3 %collective-permute-start.2 = (bf16[128,1024]{1,0:T(8,128)(2,1)}, bf16[128,1024]{1,0:T(8,128)(2,1)S(1)}, u32[]{:S(2)}, u32[]{:S(2)}) collective-permute-start(bf16[128,1024]{1,0:T(8,128)(2,1)} %q.5), channel_id=1, source_target_pairs={{8,0},{12,4},{16,8},{20,12},{24,16},{28,20},{32,24},{36,28},{40,32... | collective-permute-start | bytes 786440 | tf_op jit(solution)/shard_map/ppermute | solution.py:25
  13.2 1.3 %collective-permute-start.3 = (bf16[128,1024]{1,0:T(8,128)(2,1)}, bf16[128,1024]{1,0:T(8,128)(2,1)S(1)}, u32[]{:S(2)}, u32[]{:S(2)}) collective-permute-start(bf16[128,1024]{1,0:T(8,128)(2,1)} %q.5), channel_id=1, source_target_pairs={{16,4},{24,12},{32,20},{40,28},{48,36},{56,44},{64,52},{72,60},{80... | collective-permute-start | bytes 786440 | tf_op jit(solution)/shard_map/ppermute | solution.py:25
  14.5 1.4 %broadcast_in_dim.4 = bf16[8,8,1024]{2,1,0:T(8,128)(2,1)} broadcast(bf16[8,1024]{1,0:T(8,128)(2,1)} %param.13), dimensions={1,2} | broadcast | bytes 147456 | tf_op jit(solution)/shard_map/broadcast_in_dim | solution.py:300
  15.9 13.9 %all-to-all-start = ((bf16[8,8,1024]{2,1,0:T(8,128)(2,1)}), bf16[8,8,1024]{2,1,0:T(8,128)(2,1)S(1)}, u32[]{:S(2)}, u32[]{:S(2)}) async-start(bf16[8,8,1024]{2,1,0:T(8,128)(2,1)} %broadcast_in_dim.4), calls=%async_computation | async-start | bytes 262144 | tf_op jit(solution)/shard_map/all_to_all | solution.py:299
  29.8 5.2 %all_gather.28.k_pair = bf16[256,1024]{1,0:T(8,128)(2,1)} all-gather(bf16[128,1024]{1,0:T(8,128)(2,1)} %key.1), channel_id=1, replica_groups=mesh['y'=2,'z'=8,'x'=4,'c'=2,'grp'=4] {'c'}, dimensions={0}, use_global_device_ids=true | all-gather | bytes 786432 | tf_op jit(solution)/shard_map/all_gather | solution.py:293
  35.0 2.3 %all_gather.29.v_pair = bf16[256,1024]{1,0:T(8,128)(2,1)} all-gather(bf16[128,1024]{1,0:T(8,128)(2,1)S(1)} %copy-done.11), channel_id=1, replica_groups=mesh['y'=2,'z'=8,'x'=4,'c'=2,'grp'=4] {'c'}, dimensions={0}, use_global_device_ids=true | all-gather | bytes 786432 | tf_op jit(solution)/shard_map/all_gather | solution.py:293
  37.3 2.2 %all_gather.27.cot = bf16[256,1024]{1,0:T(8,128)(2,1)S(1)} all-gather(bf16[128,1024]{1,0:T(8,128)(2,1)S(1)} %copy-done.22), channel_id=1, replica_groups=mesh['y'=2,'z'=8,'x'=4,'c'=2,'grp'=4] {'c'}, dimensions={0}, use_global_device_ids=true | all-gather | bytes 786432 | tf_op jit(solution)/shard_map/all_gather | solution.py:293
  39.5 1.2 %broadcast_in_dim.5 = bf16[8,64,1024]{2,1,0:T(8,128)(2,1)} broadcast(bf16[64,1024]{1,0:T(8,128)(2,1)S(1)} %bitcast.13), dimensions={1,2} | broadcast | bytes 1179648 | tf_op jit(solution)/shard_map/broadcast_in_dim | solution.py:310
  40.8 6.8 %all-to-all-start.1 = ((bf16[8,64,1024]{2,1,0:T(8,128)(2,1)}), bf16[8,64,1024]{2,1,0:T(8,128)(2,1)S(1)}, u32[]{:S(2)}, u32[]{:S(2)}) async-start(bf16[8,64,1024]{2,1,0:T(8,128)(2,1)} %broadcast_in_dim.5), calls=%async_computation.1 | async-start | bytes 2097152 | tf_op jit(solution)/shard_map/all_to_all | solution.py:309
  47.5 1.9 %collective-permute-start.4 = (bf16[256,1024]{1,0:T(8,128)(2,1)S(1)}, bf16[256,1024]{1,0:T(8,128)(2,1)S(1)}, u32[]{:S(2)}, u32[]{:S(2)}) collective-permute-start(bf16[256,1024]{1,0:T(8,128)(2,1)S(1)} %collective-permute-done.chip), channel_id=1, source_target_pairs={{0,4},{4,0},{1,5},{5,1},{2,6},{6,2},{3,7},{7,3},{8,12},{12,8},{9,1... | collective-permute-start | bytes 1572872 | tf_op jit(solution)/shard_map/ppermute | solution.py:29
  50.1 1.2 %collective-permute-done.4.cross = bf16[256,1024]{1,0:T(8,128)(2,1)S(1)} collective-permute-done((bf16[256,1024]{1,0:T(8,128)(2,1)S(1)}, bf16[256,1024]{1,0:T(8,128)(2,1)S(1)}, u32[]{:S(2)}, u32[]{:S(2)}) %collective-permute-start.4) | collective-permute-done | bytes 524320 | tf_op jit(solution)/shard_map/ppermute | solution.py:29
  52.1 5.2 %shard_map.121 = (f32[128,1024]{1,0:T(8,128)}, f32[128,128]{1,0:T(8,128)}, bf16[128,1024]{1,0:T(8,128)(2,1)}) custom-call(s32[3]{0:T(128)} %pad_add_fusion.info, s32[128,128]{1,0:T(8,128)} %bitcast.10, bf16[128,1024]{1,0:T(8,128)(2,1)} %q.5, bf16[256,1024]{1,0:T(8,128)(2,1)} %copy-done.4, bf16[256,1024]{1,0:T(8,128)(2,1)} %all_gather.28.k_pair, ...), custom_call_target="tpu_custom_call" | custom-call | flops 1000 | bytes 1000 | tf_op jit(solution)/shard_map/pallas_call | solution.py:315
  57.3 2.4 %all_gather.31.hidden = bf16[256,1024]{1,0:T(8,128)(2,1)S(1)} all-gather(bf16[128,1024]{1,0:T(8,128)(2,1)} %get-tuple-element.45), channel_id=1, replica_groups=mesh['y'=2,'z'=8,'x'=4,'c'=2,'grp'=4] {'c'}, dimensions={0}, use_global_device_ids=true | all-gather | bytes 786432 | tf_op jit(solution)/shard_map/all_gather | solution.py:293
  59.7 1.0 shard_map.123
  61.7 1.0 all-to-all-done.1
  63.7 4.4 %all-to-all-start.2 = ((bf16[8,64,1024]{2,1,0:T(8,128)(2,1)}), bf16[8,64,1024]{2,1,0:T(8,128)(2,1)}, u32[]{:S(2)}, u32[]{:S(2)}) async-start(bf16[8,64,1024]{2,1,0:T(8,128)(2,1)} %bitcast.8), calls=%async_computation.2 | async-start | bytes 2097152 | tf_op jit(solution)/shard_map/all_to_all | solution.py:340
  68.1 1.2 %copy-done.3 = bf16[8,64,1024]{2,1,0:T(8,128)(2,1)S(1)} copy-done((bf16[8,64,1024]{2,1,0:T(8,128)(2,1)S(1)}, bf16[8,64,1024]{2,1,0:T(8,128)(2,1)}, u32[]{:S(2)}) %copy-start.3) | copy-done | bytes 1048600
  69.4 1.9 %shard_map.120 = (f32[128,512]{1,0:T(8,128)S(1)}, f32[128,512]{1,0:T(8,128)S(1)}) custom-call(s32[3]{0:T(128)S(1)} %copy-done.17, bf16[256,1024]{1,0:T(8,128)(2,1)S(1)} %all_gather.27.cot, bf16[512,1024]{1,0:T(8,128)(2,1)S(1)} %bitcast.9), custom_call_target="tpu_custom_call" | custom-call | flops 1000 | bytes 1000 | tf_op jit(solution)/shard_map/pallas_call | solution.py:325
  71.3 2.2 %all_gather.30.both = f32[256,512]{1,0:T(8,128)S(1)} all-gather(f32[128,512]{1,0:T(8,128)S(1)} %get-tuple-element.34), channel_id=1, replica_groups=mesh['y'=2,'z'=8,'x'=4,'c'=2,'grp'=4] {'c'}, dimensions={0}, use_global_device_ids=true | all-gather | bytes 786432 | tf_op jit(solution)/shard_map/all_gather | solution.py:293
  73.5 2.7 %shard_map.122 = (bf16[128,1024]{1,0:T(8,128)(2,1)}, bf16[128,1024]{1,0:T(8,128)(2,1)S(1)}) custom-call(s32[3]{0:T(128)S(1)} %copy-done.17, f32[128,512]{1,0:T(8,128)S(1)} %get-tuple-element.33.mine, f32[256,512]{1,0:T(8,128)S(1)} %all_gather.30.both, f32[128,1024]{1,0:T(8,128)S(1)} %copy-done.12, f32[128,128]{1,0:T(8,128)S(1)} %copy-done.16, ...), custom_call_target="tpu_custom_call" | custom-call | flops 1000 | bytes 1000 | tf_op jit(solution)/shard_map/pallas_call | solution.py:331
  76.2 1.3 %collective-permute-start.5 = (bf16[128,1024]{1,0:T(8,128)(2,1)S(1)}, bf16[128,1024]{1,0:T(8,128)(2,1)S(1)}, u32[]{:S(2)}, u32[]{:S(2)}) collective-permute-start(bf16[128,1024]{1,0:T(8,128)(2,1)S(1)} %get-tuple-element.47.u), channel_id=1, source_target_pairs={{8,0},{12,4},{16,8},{20,12},{24,16},{28,20},{32,24},{36,28},{40,32... | collective-permute-start | bytes 786440 | tf_op jit(solution)/shard_map/ppermute | solution.py:25
  77.5 1.3 %collective-permute-start.6 = (bf16[128,1024]{1,0:T(8,128)(2,1)S(1)}, bf16[128,1024]{1,0:T(8,128)(2,1)}, u32[]{:S(2)}, u32[]{:S(2)}) collective-permute-start(bf16[128,1024]{1,0:T(8,128)(2,1)S(1)} %get-tuple-element.47.u), channel_id=1, source_target_pairs={{16,4},{24,12},{32,20},{40,28},{48,36},{56,44},{64,52},{72,60},{80... | collective-permute-start | bytes 786440 | tf_op jit(solution)/shard_map/ppermute | solution.py:25
  78.8 2.3 %all_gather.32.u_pair = bf16[256,1024]{1,0:T(8,128)(2,1)S(1)} all-gather(bf16[128,1024]{1,0:T(8,128)(2,1)S(1)} %get-tuple-element.47.u), channel_id=1, replica_groups=mesh['y'=2,'z'=8,'x'=4,'c'=2,'grp'=4] {'c'}, dimensions={0}, use_global_device_ids=true | all-gather | bytes 786432 | tf_op jit(solution)/shard_map/all_gather | solution.py:293
  81.1 2.2 %all_gather.33.q_pair = bf16[256,1024]{1,0:T(8,128)(2,1)S(1)} all-gather(bf16[128,1024]{1,0:T(8,128)(2,1)S(1)} %copy-done.7), channel_id=1, replica_groups=mesh['y'=2,'z'=8,'x'=4,'c'=2,'grp'=4] {'c'}, dimensions={0}, use_global_device_ids=true | all-gather | bytes 786432 | tf_op jit(solution)/shard_map/all_gather | solution.py:293
  83.3 2.2 %all_gather.34.q_chips = bf16[256,1024]{1,0:T(8,128)(2,1)S(1)} all-gather(bf16[128,1024]{1,0:T(8,128)(2,1)S(1)} %collective-permute-done.2.q_chip), channel_id=1, replica_groups=mesh['y'=2,'z'=8,'x'=4,'c'=2,'grp'=4] {'c'}, dimensions={0}, use_global_device_ids=true | all-gather | bytes 786432 | tf_op jit(solution)/shard_map/all_gather | solution.py:293
  85.4 2.1 %shard_map.124 = f32[64,1024]{1,0:T(8,128)} custom-call(bf16[8,64,1024]{2,1,0:T(8,128)(2,1)} %all-to-all-done.2.parts), custom_call_target="tpu_custom_call" | custom-call | flops 1000 | bytes 1000 | tf_op jit(solution)/shard_map/pallas_call | solution.py:344
  87.5 11.1 %all-to-all-start.3 = ((f32[8,8,1024]{2,1,0:T(8,128)}), f32[8,8,1024]{2,1,0:T(8,128)S(1)}, u32[]{:S(2)}, u32[]{:S(2)}) async-start(f32[8,8,1024]{2,1,0:T(8,128)} %bitcast.7), calls=%async_computation.3 | async-start | bytes 524288 | tf_op jit(solution)/shard_map/all_to_all | solution.py:345
  98.6 5.1 %shard_map.125 = bf16[128,1024]{1,0:T(8,128)(2,1)} custom-call(s32[3]{0:T(128)} %pad_add_fusion.info, s32[128,128]{1,0:T(8,128)} %bitcast.11, bf16[128,1024]{1,0:T(8,128)(2,1)} %q.5, bf16[128,1024]{1,0:T(8,128)(2,1)} %copy-done.13, bf16[256,1024]{1,0:T(8,128)(2,1)} %copy-done.4, bf16[256,1024]{1,0:T(8,128)(2,1)} %all_gather.28.k_pair, ...), custom_call_target="tpu_custom_call" | custom-call | flops 20000000000 | bytes 1000 | tf_op jit(solution)/shard_map/pallas_call | solution.py:347
  103.7 2.5 %all_gather.35.u_chips = bf16[256,1024]{1,0:T(8,128)(2,1)S(1)} all-gather(bf16[128,1024]{1,0:T(8,128)(2,1)S(1)} %collective-permute-done.5.u_chip), channel_id=1, replica_groups=mesh['y'=2,'z'=8,'x'=4,'c'=2,'grp'=4] {'c'}, dimensions={0}, use_global_device_ids=true | all-gather | bytes 786432 | tf_op jit(solution)/shard_map/all_gather | solution.py:293
  106.2 4.8 %shard_map.126 = (bf16[128,1024]{1,0:T(8,128)(2,1)}, bf16[128,1024]{1,0:T(8,128)(2,1)}) custom-call(s32[3]{0:T(128)S(1)} %copy-done.18, s32[128,128]{1,0:T(8,128)S(1)} %bitcast.12, bf16[256,1024]{1,0:T(8,128)(2,1)S(1)} %copy-done.5, bf16[128,1024]{1,0:T(8,128)(2,1)S(1)} %copy-done.8, bf16[256,1024]{1,0:T(8,128)(2,1)S(1)} %all_gather.33.q_pair, ...), custom_call_target="tpu_custom_call" | custom-call | flops 20000000000 | bytes 1000 | tf_op jit(solution)/shard_map/pallas_call | solution.py:360
  (57 shorter events, 6.1 us)
Async XLA Ops:
  0.6 1.0 copy-start.9
  2.5 32.5 %copy-start.11 = (bf16[128,1024]{1,0:T(8,128)(2,1)S(1)}, bf16[128,1024]{1,0:T(8,128)(2,1)}, u32[]{:S(2)}) copy-start(bf16[128,1024]{1,0:T(8,128)(2,1)} %value.1) | copy-start | bytes 786436
  2.5 34.8 %copy-start.22 = (bf16[128,1024]{1,0:T(8,128)(2,1)S(1)}, bf16[128,1024]{1,0:T(8,128)(2,1)}, u32[]{:S(2)}) copy-start(bf16[128,1024]{1,0:T(8,128)(2,1)} %param.14) | copy-start | bytes 786436
  2.6 38.2 %copy-start.4 = (bf16[256,1024]{1,0:T(8,128)(2,1)}, bf16[256,1024]{1,0:T(8,128)(2,1)S(1)}, u32[]{:S(2)}) copy-start(bf16[256,1024]{1,0:T(8,128)(2,1)S(1)} %shard_map.119.kv) | copy-start | bytes 1572868
  2.6 36.9 %collective-permute-start = (bf16[256,1024]{1,0:T(8,128)(2,1)S(1)}, bf16[256,1024]{1,0:T(8,128)(2,1)S(1)}, u32[]{:S(2)}, u32[]{:S(2)}) collective-permute-start(bf16[256,1024]{1,0:T(8,128)(2,1)S(1)} %shard_map.119.kv), channel_id=1, source_target_pairs={{0,8},{4,12},{8,16},{12,20},{16,24},{20,28},{24,32},{28,36},{32,40... | collective-permute-start | bytes 1572872 | tf_op jit(solution)/shard_map/ppermute | solution.py:25
  6.7 32.8 %collective-permute-start.1 = (bf16[256,1024]{1,0:T(8,128)(2,1)S(1)}, bf16[256,1024]{1,0:T(8,128)(2,1)S(1)}, u32[]{:S(2)}, u32[]{:S(2)}) collective-permute-start(bf16[256,1024]{1,0:T(8,128)(2,1)S(1)} %shard_map.119.kv), channel_id=1, source_target_pairs={{4,16},{12,24},{20,32},{28,40},{36,48},{44,56},{52,64},{60,72},{68... | collective-permute-start | bytes 1572872 | tf_op jit(solution)/shard_map/ppermute | solution.py:25
  11.9 27.6 %collective-permute-start.2 = (bf16[128,1024]{1,0:T(8,128)(2,1)}, bf16[128,1024]{1,0:T(8,128)(2,1)S(1)}, u32[]{:S(2)}, u32[]{:S(2)}) collective-permute-start(bf16[128,1024]{1,0:T(8,128)(2,1)} %q.5), channel_id=1, source_target_pairs={{8,0},{12,4},{16,8},{20,12},{24,16},{28,20},{32,24},{36,28},{40,32... | collective-permute-start | bytes 786440 | tf_op jit(solution)/shard_map/ppermute | solution.py:25
  13.2 26.3 %collective-permute-start.3 = (bf16[128,1024]{1,0:T(8,128)(2,1)}, bf16[128,1024]{1,0:T(8,128)(2,1)S(1)}, u32[]{:S(2)}, u32[]{:S(2)}) collective-permute-start(bf16[128,1024]{1,0:T(8,128)(2,1)} %q.5), channel_id=1, source_target_pairs={{16,4},{24,12},{32,20},{40,28},{48,36},{56,44},{64,52},{72,60},{80... | collective-permute-start | bytes 786440 | tf_op jit(solution)/shard_map/ppermute | solution.py:25
  15.9 23.6 %all-to-all-start = ((bf16[8,8,1024]{2,1,0:T(8,128)(2,1)}), bf16[8,8,1024]{2,1,0:T(8,128)(2,1)S(1)}, u32[]{:S(2)}, u32[]{:S(2)}) async-start(bf16[8,8,1024]{2,1,0:T(8,128)(2,1)} %broadcast_in_dim.4), calls=%async_computation | async-start | bytes 262144 | tf_op jit(solution)/shard_map/all_to_all | solution.py:299
  39.5 11.8 %copy-start.19 = (bf16[256,1024]{1,0:T(8,128)(2,1)}, bf16[256,1024]{1,0:T(8,128)(2,1)S(1)}, u32[]{:S(2)}) copy-start(bf16[256,1024]{1,0:T(8,128)(2,1)S(1)} %collective-permute-done.chip) | copy-start | bytes 1572868
  39.5 1.2 %copy-start.20 = (bf16[256,1024]{1,0:T(8,128)(2,1)}, bf16[256,1024]{1,0:T(8,128)(2,1)S(1)}, u32[]{:S(2)}) copy-start(bf16[256,1024]{1,0:T(8,128)(2,1)S(1)} %collective-permute-done.1.far) | copy-start | bytes 1572868
  40.8 22.0 %all-to-all-start.1 = ((bf16[8,64,1024]{2,1,0:T(8,128)(2,1)}), bf16[8,64,1024]{2,1,0:T(8,128)(2,1)S(1)}, u32[]{:S(2)}, u32[]{:S(2)}) async-start(bf16[8,64,1024]{2,1,0:T(8,128)(2,1)} %broadcast_in_dim.5), calls=%async_computation.1 | async-start | bytes 2097152 | tf_op jit(solution)/shard_map/all_to_all | solution.py:309
  47.5 3.8 %collective-permute-start.4 = (bf16[256,1024]{1,0:T(8,128)(2,1)S(1)}, bf16[256,1024]{1,0:T(8,128)(2,1)S(1)}, u32[]{:S(2)}, u32[]{:S(2)}) collective-permute-start(bf16[256,1024]{1,0:T(8,128)(2,1)S(1)} %collective-permute-done.chip), channel_id=1, source_target_pairs={{0,4},{4,0},{1,5},{5,1},{2,6},{6,2},{3,7},{7,3},{8,12},{12,8},{9,1... | collective-permute-start | bytes 1572872 | tf_op jit(solution)/shard_map/ppermute | solution.py:29
  52.1 7.6 %copy-start.17 = (s32[3]{0:T(128)S(1)}, s32[3]{0:T(128)}, u32[]{:S(2)}) copy-start(s32[3]{0:T(128)} %pad_add_fusion.info) | copy-start | bytes 40
  60.7 1.0 copy-start.1
  62.7 1.0 copy-start.2
  63.7 9.7 %copy-start = (bf16[1024,1024]{1,0:T(8,128)(2,1)S(1)}, bf16[1024,1024]{1,0:T(8,128)(2,1)}, u32[]{:S(2)}) copy-start(bf16[1024,1024]{1,0:T(8,128)(2,1)} %constant.27.clone.perm) | copy-start | bytes 6291460
  63.7 21.7 %all-to-all-start.2 = ((bf16[8,64,1024]{2,1,0:T(8,128)(2,1)}), bf16[8,64,1024]{2,1,0:T(8,128)(2,1)}, u32[]{:S(2)}, u32[]{:S(2)}) async-start(bf16[8,64,1024]{2,1,0:T(8,128)(2,1)} %bitcast.8), calls=%async_computation.2 | async-start | bytes 2097152 | tf_op jit(solution)/shard_map/all_to_all | solution.py:340
  68.1 1.2 %copy-start.3 = (bf16[8,64,1024]{2,1,0:T(8,128)(2,1)S(1)}, bf16[8,64,1024]{2,1,0:T(8,128)(2,1)}, u32[]{:S(2)}) copy-start(bf16[8,64,1024]{2,1,0:T(8,128)(2,1)} %copy-done.2) | copy-start | bytes 3145732
  69.4 4.1 %copy-start.6 = (bf16[128,1024]{1,0:T(8,128)(2,1)S(1)}, bf16[128,1024]{1,0:T(8,128)(2,1)}, u32[]{:S(2)}) copy-start(bf16[128,1024]{1,0:T(8,128)(2,1)} %gate.3) | copy-start | bytes 786436
  69.4 4.1 %copy-start.12 = (f32[128,1024]{1,0:T(8,128)S(1)}, f32[128,1024]{1,0:T(8,128)}, u32[]{:S(2)}) copy-start(f32[128,1024]{1,0:T(8,128)} %get-tuple-element.39.normed) | copy-start | bytes 1572868
  69.4 4.1 %copy-start.16 = (f32[128,128]{1,0:T(8,128)S(1)}, f32[128,128]{1,0:T(8,128)}, u32[]{:S(2)}) copy-start(f32[128,128]{1,0:T(8,128)} %get-tuple-element.40.rstd) | copy-start | bytes 196612
  73.5 7.6 %copy-start.7 = (bf16[128,1024]{1,0:T(8,128)(2,1)S(1)}, bf16[128,1024]{1,0:T(8,128)(2,1)}, u32[]{:S(2)}) copy-start(bf16[128,1024]{1,0:T(8,128)(2,1)} %q.5) | copy-start | bytes 786436
  76.2 11.3 %copy-start.13 = (bf16[128,1024]{1,0:T(8,128)(2,1)}, bf16[128,1024]{1,0:T(8,128)(2,1)S(1)}, u32[]{:S(2)}) copy-start(bf16[128,1024]{1,0:T(8,128)(2,1)S(1)} %get-tuple-element.47.u) | copy-start | bytes 786436
  76.2 27.5 %collective-permute-start.5 = (bf16[128,1024]{1,0:T(8,128)(2,1)S(1)}, bf16[128,1024]{1,0:T(8,128)(2,1)S(1)}, u32[]{:S(2)}, u32[]{:S(2)}) collective-permute-start(bf16[128,1024]{1,0:T(8,128)(2,1)S(1)} %get-tuple-element.47.u), channel_id=1, source_target_pairs={{8,0},{12,4},{16,8},{20,12},{24,16},{28,20},{32,24},{36,28},{40,32... | collective-permute-start | bytes 786440 | tf_op jit(solution)/shard_map/ppermute | solution.py:25
  77.5 28.7 %collective-permute-start.6 = (bf16[128,1024]{1,0:T(8,128)(2,1)S(1)}, bf16[128,1024]{1,0:T(8,128)(2,1)}, u32[]{:S(2)}, u32[]{:S(2)}) collective-permute-start(bf16[128,1024]{1,0:T(8,128)(2,1)S(1)} %get-tuple-element.47.u), channel_id=1, source_target_pairs={{16,4},{24,12},{32,20},{40,28},{48,36},{56,44},{64,52},{72,60},{80... | collective-permute-start | bytes 786440 | tf_op jit(solution)/shard_map/ppermute | solution.py:25
  87.5 23.6 %all-to-all-start.3 = ((f32[8,8,1024]{2,1,0:T(8,128)}), f32[8,8,1024]{2,1,0:T(8,128)S(1)}, u32[]{:S(2)}, u32[]{:S(2)}) async-start(f32[8,8,1024]{2,1,0:T(8,128)} %bitcast.7), calls=%async_computation.3 | async-start | bytes 524288 | tf_op jit(solution)/shard_map/all_to_all | solution.py:345
  98.6 7.6 %copy-start.5 = (bf16[256,1024]{1,0:T(8,128)(2,1)S(1)}, bf16[256,1024]{1,0:T(8,128)(2,1)}, u32[]{:S(2)}) copy-start(bf16[256,1024]{1,0:T(8,128)(2,1)} %copy-done.4) | copy-start | bytes 1572868
  98.6 7.6 %copy-start.8 = (bf16[128,1024]{1,0:T(8,128)(2,1)S(1)}, bf16[128,1024]{1,0:T(8,128)(2,1)}, u32[]{:S(2)}) copy-start(bf16[128,1024]{1,0:T(8,128)(2,1)} %q.5) | copy-start | bytes 786436
  98.6 7.6 %copy-start.14 = (bf16[128,1024]{1,0:T(8,128)(2,1)S(1)}, bf16[128,1024]{1,0:T(8,128)(2,1)}, u32[]{:S(2)}) copy-start(bf16[128,1024]{1,0:T(8,128)(2,1)} %copy-done.13) | copy-start | bytes 786436
  98.6 7.6 %copy-start.15 = (s32[16384]{0:T(1024)S(1)}, s32[16384]{0:T(1024)}, u32[]{:S(2)}) copy-start(s32[16384]{0:T(1024)} %param.12) | copy-start | bytes 196612
  98.6 7.6 %copy-start.18 = (s32[3]{0:T(128)S(1)}, s32[3]{0:T(128)}, u32[]{:S(2)}) copy-start(s32[3]{0:T(128)} %pad_add_fusion.info) | copy-start | bytes 40
  (2 other events, 1.8 us)

commit v5 on v4

--- a/solution.py
+++ b/solution.py
@@ -39,6 +39,11 @@
 
 def sigmoid(s):
     return 0.5 * jnp.tanh(0.5 * s) + 0.5
+
+
+def position():
+    y, z, x, c = (lax.axis_index(axis) for axis in BLK)
+    return ((y * NZ + z) * NX + x) * NC + c, c
 
 
 class Loader:
@@ -104,19 +109,20 @@
 
 
 def forward_kernel(
-    info, seg, q, kv, k_pair, v_pair, chip, cross, far, gate, perm,
+    seg, q, kv, k_pair, v_pair, chip, cross, far, gate, perm,
     normed_o, rstd_o, hidden_o,
     segs, qb, kb, vb, gb, pb, att, sems,
 ):
     load = Loader(sems)
-    even = info[1] == 0
+    block, core = position()
+    even = core == 0
     first = [load.start(seg, segs), load.start(q, qb)]
     first += load_memory(load, even, kv, k_pair, v_pair, chip, cross, far, kb, vb)
     later = [load.start(gate, gb), load.start(perm, pb)]
     for copy in first:
         copy.wait()
     width = qb.shape[1]
-    allowed = allowed_pairs(segs, info[0], -1)
+    allowed = allowed_pairs(segs, block, -1)
     for at in head_groups(width):
         scores = [dot(qb[:, h], kb[:, h], (1, 1)) * SCALE for h in at]
         weights = [jnp.where(allowed, s * sigmoid(s), 0.0).astype(BF16) for s in scores]
@@ -135,13 +141,13 @@
     hidden_o[...] = dot(hidden, pb[...], (1, 0)).astype(BF16)
 
 
-def columns_kernel(info, cot, w_sub, mine_o, sent_o, wb, sems):
+def columns_kernel(cot, w_sub, mine_o, sent_o, wb, sems):
     load = Loader(sems)
     rows, half = mine_o.shape
     step = half // 4
     chunks = [pl.ds(i * step, step) for i in range(half // step)]
     copies = [load.start(w_sub.at[chunk, :], wb.at[chunk, :]) for chunk in chunks]
-    core = info[1]
+    core = position()[1]
     own = pl.ds(pl.multiple_of(core * rows, rows), rows)
     other = pl.ds(pl.multiple_of((1 - core) * rows, rows), rows)
     for chunk, copy in zip(chunks, copies):
@@ -150,16 +156,17 @@
         sent_o[:, chunk] = dot(cot[other, :], wb[chunk, :], (1, 1))
 
 
-def weight_kernel(info, hidden, cot, out):
+def weight_kernel(hidden, cot, out):
     half = out.shape[0]
-    columns = hidden[:, pl.ds(pl.multiple_of(info[1] * half, half), half)]
+    columns = hidden[:, pl.ds(pl.multiple_of(position()[1] * half, half), half)]
     out[...] = dot(columns, cot[...], (0, 0)).astype(BF16)
 
 
-def upstream_kernel(info, mine, both, normed, rstd, gate, perm, gate_o, upper_o):
+def upstream_kernel(mine, both, normed, rstd, gate, perm, gate_o, upper_o):
     rows = mine.shape[0]
     own = mine[...]
-    even = info[1] == 0
+    block, core = position()
+    even = core == 0
     first = jnp.where(even, own, both[:rows])
     second = jnp.where(even, both[rows:], own)
     placed = jnp.concatenate([first, second], 1)
@@ -178,18 +185,19 @@
 
 
 def query_kernel(
-    info, seg, q, u, kv, k_pair, v_pair, chip, cross, far,
+    seg, q, u, kv, k_pair, v_pair, chip, cross, far,
     query_o,
     segs, qb, ub, kb, vb, sems,
 ):
     load = Loader(sems)
-    even = info[1] == 0
+    block, core = position()
+    even = core == 0
     copies = [load.start(seg, segs), load.start(q, qb), load.start(u, ub)]
     copies += load_memory(load, even, kv, k_pair, v_pair, chip, cross, far, kb, vb)
     for copy in copies:
         copy.wait()
     width = query_o.shape[1]
-    allowed = allowed_pairs(segs, info[0], -1)
+    allowed = allowed_pairs(segs, block, -1)
     for at in head_groups(width):
         scores = [dot(qb[:, h], kb[:, h], (1, 1)) * SCALE for h in at]
         weight_grads = [dot(ub[:, h], vb[:, h], (1, 1)) for h in at]
@@ -203,12 +211,13 @@
 
 
 def memory_kernel(
-    info, seg, kv, q, q_pair, q_chip, q_chips, q_far, u, u_pair, u_chip, u_chips, u_far,
+    seg, kv, q, q_pair, q_chip, q_chips, q_far, u, u_pair, u_chip, u_chips, u_far,
     key_o, value_o,
     segs, kvb, qb, ub, sems,
 ):
     load = Loader(sems)
-    even = info[1] == 0
+    block, core = position()
+    even = core == 0
     rows, width = key_o.shape
     copies = [load.start(seg, segs), load.start(kv, kvb)]
     slot = lambda buffer, o: buffer.at[pl.ds(o * rows, rows), :]
@@ -223,7 +232,7 @@
         copies.append(load.choose(even, chips.at[second, :], far, slot(buffer, 3)))
     for copy in copies:
         copy.wait()
-    allowed = allowed_pairs(segs, info[0], 1)
+    allowed = allowed_pairs(segs, block, 1)
     for at in head_groups(width):
         scores = [dot(kvb[:rows, h], qb[:, h], (1, 1)) * SCALE for h in at]
         weight_grads = [dot(kvb[rows:, h], ub[:, h], (1, 1)) for h in at]
@@ -268,8 +277,6 @@
 
 def body(query_rows, key_rows, value_rows, gate_rows, segment, w_out, cotangent):
     rows, width = query_rows.shape
-    device = lax.axis_index(BLK)
-    info = jnp.stack([device, lax.axis_index("c"), lax.axis_index("x")]).astype(jnp.int32)
     seg = segment.reshape(-1, rows)
     unit = w_out.shape[0]
     span = REACH * rows
@@ -315,28 +322,28 @@
     normed, rstd, hidden = call(
         forward_kernel,
         (like(rows, width, dtype=F32), like(rows, 128, dtype=F32), like(rows, width)),
-        "shhahhhhhhh",
+        "hhahhhhhhh",
         [
             seg_scratch, scratch(rows, width), scratch(span, width), scratch(span, width),
             scratch(rows, width), scratch(width, width), scratch(rows, width, dtype=F32), sems(12),
         ],
         limit=LARGE_LIMIT,
-    )(info, seg, query_rows, *memory, gate_rows, perm)
+    )(seg, query_rows, *memory, gate_rows, perm)
     mine, sent = call(
         columns_kernel,
         (like(rows, CHIPS * unit, dtype=F32),) * 2,
-        "svh",
+        "vh",
         [scratch(CHIPS * unit, width), sems(4)],
-    )(info, cot, w_sub)
-    gate_grad, upper = call(upstream_kernel, (like(rows, width), like(rows, width)), "svvvvvv")(
-        info, mine, pair(sent), normed, rstd, gate_rows, perm
+    )(cot, w_sub)
+    gate_grad, upper = call(upstream_kernel, (like(rows, width), like(rows, width)), "vvvvvv")(
+        mine, pair(sent), normed, rstd, gate_rows, perm
     )
 
     u_chip, u_far = ahead(upper)
     u_pair = pair(upper)
 
     hidden, q_chip, q_far = lax.optimization_barrier((hidden, q_chip, q_far))
-    w_part = call(weight_kernel, like(CHIPS * unit, width), "svv")(info, pair(hidden), cot)
+    w_part = call(weight_kernel, like(CHIPS * unit, width), "vv")(pair(hidden), cot)
     w_parts = lax.all_to_all(w_part.reshape(NY * NX, NZ * unit, width), PLANE, 0, 0, tiled=True)
     q_late, q_chip_late, _ = lax.optimization_barrier((query_rows, q_chip, u_pair))
     q_pair, q_chips = pair(q_late), pair(q_chip_late)
@@ -347,24 +354,24 @@
     query_grad = call(
         query_kernel,
         like(rows, width),
-        "s" + "a" * 9,
+        "a" * 9,
         [
             seg_scratch, scratch(rows, width), scratch(rows, width), scratch(span, width), scratch(span, width),
             sems(11),
         ],
         20_000_000_000,
         LARGE_LIMIT,
-    )(info, seg, query_rows, upper_late, *memory)
+    )(seg, query_rows, upper_late, *memory)
     u_chip, _ = lax.optimization_barrier((u_chip, query_grad))
     u_chips = pair(u_chip)
     key_grad, value_grad = call(
         memory_kernel,
         (like(rows, width), like(rows, width)),
-        "s" + "a" * 12,
+        "a" * 12,
         [seg_scratch, scratch(2 * rows, width), scratch(span, width), scratch(span, width), sems(10)],
         20_000_000_000,
     )(
-        info, seg, kv, query_rows, q_pair, q_chip, q_chips, q_far,
+        seg, kv, query_rows, q_pair, q_chip, q_chips, q_far,
         upper, u_pair, u_chip, u_chips, u_far,
     )
     w_line, _ = lax.optimization_barrier((w_line, key_grad))

time: 113 us -> 110 us (0.973)
  Pallas kernels: 23.5 us -> 19.9 us
  waiting for transfers between devices: 2.26 us -> 4.27 us
    pallas_call x5, Pallas kernels: 15.6 us -> 12.7 us  [the longest x1 4.38 us: body(): call(query_kernel, like(rows, width), 'a' * 9, [seg_scratch, scratch(rows...]
    all_to_all x1, waiting for transfers between devices: 1.02 us -> 2.37 us  [body(): lax.all_to_all(jnp.broadcast_to(w_line[None], (NY * NX,) + w_line.shape),...]
    unnamed x46 -> x42, local copies, waits for them, and re-layouts: 5.98 us -> 5.95 us
  transfers between devices with their start and end apart: 11 -> 11, of which waited for: 2 -> 2; matrix products, arithmetic and copies ran while one was open for 2% -> 1% of each run, Pallas kernels for 20% -> 18%
where the time goes in v5:
time: 110 us; the launch traced here: 109 us
  starting transfers between devices  52 us (47%)
  blocking collectives  23.3 us (21%)
  Pallas kernels  19.9 us (18%)
  local copies, waits for them, and re-layouts  8.54 us (8%)
  waiting for transfers between devices  4.27 us (4%)
    all_gather x9, blocking collectives, pair(): return lax.all_gather(rows_of, 'c', axis=0, tiled=True)  23.3 us
    ppermute x6, starting transfers between devices, shift(): return lax.ppermute(value, BLK, pairs)  14.5 us
    all_to_all x1, starting transfers between devices, body(): lax.all_to_all(jnp.broadcast_to(w_out[None], (NZ,) + w_out.shape), 'z', 0...  13.9 us
    all_to_all x1, starting transfers between devices, body(): w_line = lax.all_to_all(w_sum, 'z', 0, 0, tiled=True)  10.6 us
    all_to_all x1, starting transfers between devices, body(): lax.all_to_all(jnp.broadcast_to(w_line[None], (NY * NX,) + w_line.shape),...  6.76 us
    unnamed x42, local copies, waits for them, and re-layouts  5.95 us
    pallas_call x1, Pallas kernels, body(): call(query_kernel, like(rows, width), 'a' * 9, [seg_scratch, scratch(rows...  4.38 us
    all_to_all x1, starting transfers between devices, body(): lax.all_to_all(w_part.reshape(NY * NX, NZ * unit, width), PLANE, 0, 0, ti...  4.37 us
  transfers between devices with their start and end apart: 11, of which 2 were waited for; matrix products, arithmetic and copies ran while one was open for 1% of the time, Pallas kernels for 18%

profile of v5, /device:TPU:1, one launch (start us, length us, event | category | flops | bytes accessed | tf_op | source)
XLA Modules:
  0.0 108.9 jit_solution(17055624361382206347)
XLA Ops:
  2.6 4.1 %collective-permute-start = (bf16[256,1024]{1,0:T(8,128)(2,1)S(1)}, bf16[256,1024]{1,0:T(8,128)(2,1)S(1)}, u32[]{:S(2)}, u32[]{:S(2)}) collective-permute-start(bf16[256,1024]{1,0:T(8,128)(2,1)S(1)} %shard_map.119.kv), channel_id=1, source_target_pairs={{0,8},{4,12},{8,16},{12,20},{16,24},{20,28},{24,32},{28,36},{32,40... | collective-permute-start | bytes 1572872 | tf_op jit(solution)/shard_map/ppermute | solution.py:25
  6.7 5.2 %collective-permute-start.1 = (bf16[256,1024]{1,0:T(8,128)(2,1)S(1)}, bf16[256,1024]{1,0:T(8,128)(2,1)S(1)}, u32[]{:S(2)}, u32[]{:S(2)}) collective-permute-start(bf16[256,1024]{1,0:T(8,128)(2,1)S(1)} %shard_map.119.kv), channel_id=1, source_target_pairs={{4,16},{12,24},{20,32},{28,40},{36,48},{44,56},{52,64},{60,72},{68... | collective-permute-start | bytes 1572872 | tf_op jit(solution)/shard_map/ppermute | solution.py:25
  11.9 1.3 %collective-permute-start.2 = (bf16[128,1024]{1,0:T(8,128)(2,1)}, bf16[128,1024]{1,0:T(8,128)(2,1)S(1)}, u32[]{:S(2)}, u32[]{:S(2)}) collective-permute-start(bf16[128,1024]{1,0:T(8,128)(2,1)} %q.5), channel_id=1, source_target_pairs={{8,0},{12,4},{16,8},{20,12},{24,16},{28,20},{32,24},{36,28},{40,32... | collective-permute-start | bytes 786440 | tf_op jit(solution)/shard_map/ppermute | solution.py:25
  13.2 1.3 %collective-permute-start.3 = (bf16[128,1024]{1,0:T(8,128)(2,1)}, bf16[128,1024]{1,0:T(8,128)(2,1)S(1)}, u32[]{:S(2)}, u32[]{:S(2)}) collective-permute-start(bf16[128,1024]{1,0:T(8,128)(2,1)} %q.5), channel_id=1, source_target_pairs={{16,4},{24,12},{32,20},{40,28},{48,36},{56,44},{64,52},{72,60},{80... | collective-permute-start | bytes 786440 | tf_op jit(solution)/shard_map/ppermute | solution.py:25
  14.5 1.4 %broadcast_in_dim.4 = bf16[8,8,1024]{2,1,0:T(8,128)(2,1)} broadcast(bf16[8,1024]{1,0:T(8,128)(2,1)} %param.13), dimensions={1,2} | broadcast | bytes 147456 | tf_op jit(solution)/shard_map/broadcast_in_dim | solution.py:307
  15.9 13.9 %all-to-all-start = ((bf16[8,8,1024]{2,1,0:T(8,128)(2,1)}), bf16[8,8,1024]{2,1,0:T(8,128)(2,1)S(1)}, u32[]{:S(2)}, u32[]{:S(2)}) async-start(bf16[8,8,1024]{2,1,0:T(8,128)(2,1)} %broadcast_in_dim.4), calls=%async_computation | async-start | bytes 262144 | tf_op jit(solution)/shard_map/all_to_all | solution.py:306
  29.8 5.2 %all_gather.28.k_pair = bf16[256,1024]{1,0:T(8,128)(2,1)} all-gather(bf16[128,1024]{1,0:T(8,128)(2,1)} %key.1), channel_id=1, replica_groups=mesh['y'=2,'z'=8,'x'=4,'c'=2,'grp'=4] {'c'}, dimensions={0}, use_global_device_ids=true | all-gather | bytes 786432 | tf_op jit(solution)/shard_map/all_gather | solution.py:300
  35.0 2.3 %all_gather.29.v_pair = bf16[256,1024]{1,0:T(8,128)(2,1)} all-gather(bf16[128,1024]{1,0:T(8,128)(2,1)S(1)} %copy-done.11), channel_id=1, replica_groups=mesh['y'=2,'z'=8,'x'=4,'c'=2,'grp'=4] {'c'}, dimensions={0}, use_global_device_ids=true | all-gather | bytes 786432 | tf_op jit(solution)/shard_map/all_gather | solution.py:300
  37.3 2.2 %all_gather.27.cot = bf16[256,1024]{1,0:T(8,128)(2,1)S(1)} all-gather(bf16[128,1024]{1,0:T(8,128)(2,1)S(1)} %copy-done.20), channel_id=1, replica_groups=mesh['y'=2,'z'=8,'x'=4,'c'=2,'grp'=4] {'c'}, dimensions={0}, use_global_device_ids=true | all-gather | bytes 786432 | tf_op jit(solution)/shard_map/all_gather | solution.py:300
  39.5 1.2 %broadcast_in_dim.5 = bf16[8,64,1024]{2,1,0:T(8,128)(2,1)} broadcast(bf16[64,1024]{1,0:T(8,128)(2,1)S(1)} %bitcast.10), dimensions={1,2} | broadcast | bytes 1179648 | tf_op jit(solution)/shard_map/broadcast_in_dim | solution.py:317
  40.8 6.8 %all-to-all-start.1 = ((bf16[8,64,1024]{2,1,0:T(8,128)(2,1)}), bf16[8,64,1024]{2,1,0:T(8,128)(2,1)S(1)}, u32[]{:S(2)}, u32[]{:S(2)}) async-start(bf16[8,64,1024]{2,1,0:T(8,128)(2,1)} %broadcast_in_dim.5), calls=%async_computation.1 | async-start | bytes 2097152 | tf_op jit(solution)/shard_map/all_to_all | solution.py:316
  47.5 1.9 %collective-permute-start.4 = (bf16[256,1024]{1,0:T(8,128)(2,1)S(1)}, bf16[256,1024]{1,0:T(8,128)(2,1)S(1)}, u32[]{:S(2)}, u32[]{:S(2)}) collective-permute-start(bf16[256,1024]{1,0:T(8,128)(2,1)S(1)} %collective-permute-done.chip), channel_id=1, source_target_pairs={{0,4},{4,0},{1,5},{5,1},{2,6},{6,2},{3,7},{7,3},{8,12},{12,8},{9,1... | collective-permute-start | bytes 1572872 | tf_op jit(solution)/shard_map/ppermute | solution.py:29
  49.4 1.9 %collective-permute-done.4.cross = bf16[256,1024]{1,0:T(8,128)(2,1)S(1)} collective-permute-done((bf16[256,1024]{1,0:T(8,128)(2,1)S(1)}, bf16[256,1024]{1,0:T(8,128)(2,1)S(1)}, u32[]{:S(2)}, u32[]{:S(2)}) %collective-permute-start.4) | collective-permute-done | bytes 524320 | tf_op jit(solution)/shard_map/ppermute | solution.py:29
  52.1 4.4 %shard_map.121 = (f32[128,1024]{1,0:T(8,128)}, f32[128,128]{1,0:T(8,128)}, bf16[128,1024]{1,0:T(8,128)(2,1)}) custom-call(s32[128,128]{1,0:T(8,128)} %bitcast.7, bf16[128,1024]{1,0:T(8,128)(2,1)} %q.5, bf16[256,1024]{1,0:T(8,128)(2,1)} %copy-done.4, bf16[256,1024]{1,0:T(8,128)(2,1)} %all_gather.28.k_pair, bf16[256,1024]{1,0:T(8,128)(2,1)} %all_gather.29.v_pair, ...), custom_call_target="tpu_custom_call" | custom-call | flops 1000 | bytes 1000 | tf_op jit(solution)/shard_map/pallas_call | solution.py:322
  56.5 2.4 %all_gather.31.hidden = bf16[256,1024]{1,0:T(8,128)(2,1)S(1)} all-gather(bf16[128,1024]{1,0:T(8,128)(2,1)} %get-tuple-element.45), channel_id=1, replica_groups=mesh['y'=2,'z'=8,'x'=4,'c'=2,'grp'=4] {'c'}, dimensions={0}, use_global_device_ids=true | all-gather | bytes 786432 | tf_op jit(solution)/shard_map/all_gather | solution.py:300
  60.4 2.4 %all-to-all-done.1 = bf16[8,64,1024]{2,1,0:T(8,128)(2,1)S(1)} async-done(((bf16[8,64,1024]{2,1,0:T(8,128)(2,1)}), bf16[8,64,1024]{2,1,0:T(8,128)(2,1)S(1)}, u32[]{:S(2)}, u32[]{:S(2)}) %all-to-all-start.1) | async-done | bytes 1048608 | tf_op jit(solution)/shard_map/all_to_all | solution.py:316
  62.7 1.0 copy-done.2
  63.7 4.4 %all-to-all-start.2 = ((bf16[8,64,1024]{2,1,0:T(8,128)(2,1)}), bf16[8,64,1024]{2,1,0:T(8,128)(2,1)}, u32[]{:S(2)}, u32[]{:S(2)}) async-start(bf16[8,64,1024]{2,1,0:T(8,128)(2,1)} %bitcast.5), calls=%async_computation.2 | async-start | bytes 2097152 | tf_op jit(solution)/shard_map/all_to_all | solution.py:347
  68.1 1.2 %copy-done.3 = bf16[8,64,1024]{2,1,0:T(8,128)(2,1)S(1)} copy-done((bf16[8,64,1024]{2,1,0:T(8,128)(2,1)S(1)}, bf16[8,64,1024]{2,1,0:T(8,128)(2,1)}, u32[]{:S(2)}) %copy-start.3) | copy-done | bytes 1048600
  69.3 1.4 %shard_map.120 = (f32[128,512]{1,0:T(8,128)S(1)}, f32[128,512]{1,0:T(8,128)S(1)}) custom-call(bf16[256,1024]{1,0:T(8,128)(2,1)S(1)} %all_gather.27.cot, bf16[512,1024]{1,0:T(8,128)(2,1)S(1)} %bitcast.6), custom_call_target="tpu_custom_call" | custom-call | flops 1000 | bytes 1000 | tf_op jit(solution)/shard_map/pallas_call | solution.py:332
  70.7 2.2 %all_gather.30.both = f32[256,512]{1,0:T(8,128)S(1)} all-gather(f32[128,512]{1,0:T(8,128)S(1)} %get-tuple-element.34), channel_id=1, replica_groups=mesh['y'=2,'z'=8,'x'=4,'c'=2,'grp'=4] {'c'}, dimensions={0}, use_global_device_ids=true | all-gather | bytes 786432 | tf_op jit(solution)/shard_map/all_gather | solution.py:300
  72.9 2.2 %shard_map.122 = (bf16[128,1024]{1,0:T(8,128)(2,1)}, bf16[128,1024]{1,0:T(8,128)(2,1)S(1)}) custom-call(f32[128,512]{1,0:T(8,128)S(1)} %get-tuple-element.33.mine, f32[256,512]{1,0:T(8,128)S(1)} %all_gather.30.both, f32[128,1024]{1,0:T(8,128)S(1)} %copy-done.12, f32[128,128]{1,0:T(8,128)S(1)} %copy-done.16, bf16[128,1024]{1,0:T(8,128)(2,1)S(1)} %copy-done.6, ...), custom_call_target="tpu_custom_call" | custom-call | flops 1000 | bytes 1000 | tf_op jit(solution)/shard_map/pallas_call | solution.py:338
  75.2 1.3 %collective-permute-start.5 = (bf16[128,1024]{1,0:T(8,128)(2,1)S(1)}, bf16[128,1024]{1,0:T(8,128)(2,1)S(1)}, u32[]{:S(2)}, u32[]{:S(2)}) collective-permute-start(bf16[128,1024]{1,0:T(8,128)(2,1)S(1)} %get-tuple-element.47.u), channel_id=1, source_target_pairs={{8,0},{12,4},{16,8},{20,12},{24,16},{28,20},{32,24},{36,28},{40,32... | collective-permute-start | bytes 786440 | tf_op jit(solution)/shard_map/ppermute | solution.py:25
  76.4 1.3 %collective-permute-start.6 = (bf16[128,1024]{1,0:T(8,128)(2,1)S(1)}, bf16[128,1024]{1,0:T(8,128)(2,1)}, u32[]{:S(2)}, u32[]{:S(2)}) collective-permute-start(bf16[128,1024]{1,0:T(8,128)(2,1)S(1)} %get-tuple-element.47.u), channel_id=1, source_target_pairs={{16,4},{24,12},{32,20},{40,28},{48,36},{56,44},{64,52},{72,60},{80... | collective-permute-start | bytes 786440 | tf_op jit(solution)/shard_map/ppermute | solution.py:25
  77.7 2.2 %all_gather.32.u_pair = bf16[256,1024]{1,0:T(8,128)(2,1)S(1)} all-gather(bf16[128,1024]{1,0:T(8,128)(2,1)S(1)} %get-tuple-element.47.u), channel_id=1, replica_groups=mesh['y'=2,'z'=8,'x'=4,'c'=2,'grp'=4] {'c'}, dimensions={0}, use_global_device_ids=true | all-gather | bytes 786432 | tf_op jit(solution)/shard_map/all_gather | solution.py:300
  80.0 2.2 %all_gather.33.q_pair = bf16[256,1024]{1,0:T(8,128)(2,1)S(1)} all-gather(bf16[128,1024]{1,0:T(8,128)(2,1)S(1)} %copy-done.7), channel_id=1, replica_groups=mesh['y'=2,'z'=8,'x'=4,'c'=2,'grp'=4] {'c'}, dimensions={0}, use_global_device_ids=true | all-gather | bytes 786432 | tf_op jit(solution)/shard_map/all_gather | solution.py:300
  82.2 2.2 %all_gather.34.q_chips = bf16[256,1024]{1,0:T(8,128)(2,1)S(1)} all-gather(bf16[128,1024]{1,0:T(8,128)(2,1)S(1)} %collective-permute-done.2.q_chip), channel_id=1, replica_groups=mesh['y'=2,'z'=8,'x'=4,'c'=2,'grp'=4] {'c'}, dimensions={0}, use_global_device_ids=true | all-gather | bytes 786432 | tf_op jit(solution)/shard_map/all_gather | solution.py:300
  84.3 2.1 %shard_map.124 = f32[64,1024]{1,0:T(8,128)} custom-call(bf16[8,64,1024]{2,1,0:T(8,128)(2,1)} %all-to-all-done.2.parts), custom_call_target="tpu_custom_call" | custom-call | flops 1000 | bytes 1000 | tf_op jit(solution)/shard_map/pallas_call | solution.py:351
  86.4 10.6 %all-to-all-start.3 = ((f32[8,8,1024]{2,1,0:T(8,128)}), f32[8,8,1024]{2,1,0:T(8,128)S(1)}, u32[]{:S(2)}, u32[]{:S(2)}) async-start(f32[8,8,1024]{2,1,0:T(8,128)} %bitcast.4), calls=%async_computation.3 | async-start | bytes 524288 | tf_op jit(solution)/shard_map/all_to_all | solution.py:352
  97.1 4.4 %shard_map.125 = bf16[128,1024]{1,0:T(8,128)(2,1)} custom-call(s32[128,128]{1,0:T(8,128)} %bitcast.8, bf16[128,1024]{1,0:T(8,128)(2,1)} %q.5, bf16[128,1024]{1,0:T(8,128)(2,1)} %copy-done.13, bf16[256,1024]{1,0:T(8,128)(2,1)} %copy-done.4, bf16[256,1024]{1,0:T(8,128)(2,1)} %all_gather.28.k_pair, bf16[256,1024]{1,0:T(8,128)(2,1)} %all_gather.29.v_pair, ...), custom_call_target="tpu_custom_call" | custom-call | flops 20000000000 | bytes 1000 | tf_op jit(solution)/shard_map/pallas_call | solution.py:354
  101.5 2.5 %all_gather.35.u_chips = bf16[256,1024]{1,0:T(8,128)(2,1)S(1)} all-gather(bf16[128,1024]{1,0:T(8,128)(2,1)S(1)} %collective-permute-done.5.u_chip), channel_id=1, replica_groups=mesh['y'=2,'z'=8,'x'=4,'c'=2,'grp'=4] {'c'}, dimensions={0}, use_global_device_ids=true | all-gather | bytes 786432 | tf_op jit(solution)/shard_map/all_gather | solution.py:300
  103.9 4.3 %shard_map.126 = (bf16[128,1024]{1,0:T(8,128)(2,1)}, bf16[128,1024]{1,0:T(8,128)(2,1)}) custom-call(s32[128,128]{1,0:T(8,128)S(1)} %bitcast.9, bf16[256,1024]{1,0:T(8,128)(2,1)S(1)} %copy-done.5, bf16[128,1024]{1,0:T(8,128)(2,1)S(1)} %copy-done.8, bf16[256,1024]{1,0:T(8,128)(2,1)S(1)} %all_gather.33.q_pair, ...), custom_call_target="tpu_custom_call" | custom-call | flops 20000000000 | bytes 1000 | tf_op jit(solution)/shard_map/pallas_call | solution.py:367
  (52 shorter events, 4.9 us)
Async XLA Ops:
  0.6 1.0 copy-start.9
  1.6 0.9 copy-start.10
  2.5 32.5 %copy-start.11 = (bf16[128,1024]{1,0:T(8,128)(2,1)S(1)}, bf16[128,1024]{1,0:T(8,128)(2,1)}, u32[]{:S(2)}) copy-start(bf16[128,1024]{1,0:T(8,128)(2,1)} %value.1) | copy-start | bytes 786436
  2.5 34.8 %copy-start.20 = (bf16[128,1024]{1,0:T(8,128)(2,1)S(1)}, bf16[128,1024]{1,0:T(8,128)(2,1)}, u32[]{:S(2)}) copy-start(bf16[128,1024]{1,0:T(8,128)(2,1)} %param.14) | copy-start | bytes 786436
  2.6 38.2 %copy-start.4 = (bf16[256,1024]{1,0:T(8,128)(2,1)}, bf16[256,1024]{1,0:T(8,128)(2,1)S(1)}, u32[]{:S(2)}) copy-start(bf16[256,1024]{1,0:T(8,128)(2,1)S(1)} %shard_map.119.kv) | copy-start | bytes 1572868
  2.6 36.9 %collective-permute-start = (bf16[256,1024]{1,0:T(8,128)(2,1)S(1)}, bf16[256,1024]{1,0:T(8,128)(2,1)S(1)}, u32[]{:S(2)}, u32[]{:S(2)}) collective-permute-start(bf16[256,1024]{1,0:T(8,128)(2,1)S(1)} %shard_map.119.kv), channel_id=1, source_target_pairs={{0,8},{4,12},{8,16},{12,20},{16,24},{20,28},{24,32},{28,36},{32,40... | collective-permute-start | bytes 1572872 | tf_op jit(solution)/shard_map/ppermute | solution.py:25
  6.7 32.8 %collective-permute-start.1 = (bf16[256,1024]{1,0:T(8,128)(2,1)S(1)}, bf16[256,1024]{1,0:T(8,128)(2,1)S(1)}, u32[]{:S(2)}, u32[]{:S(2)}) collective-permute-start(bf16[256,1024]{1,0:T(8,128)(2,1)S(1)} %shard_map.119.kv), channel_id=1, source_target_pairs={{4,16},{12,24},{20,32},{28,40},{36,48},{44,56},{52,64},{60,72},{68... | collective-permute-start | bytes 1572872 | tf_op jit(solution)/shard_map/ppermute | solution.py:25
  11.9 27.6 %collective-permute-start.2 = (bf16[128,1024]{1,0:T(8,128)(2,1)}, bf16[128,1024]{1,0:T(8,128)(2,1)S(1)}, u32[]{:S(2)}, u32[]{:S(2)}) collective-permute-start(bf16[128,1024]{1,0:T(8,128)(2,1)} %q.5), channel_id=1, source_target_pairs={{8,0},{12,4},{16,8},{20,12},{24,16},{28,20},{32,24},{36,28},{40,32... | collective-permute-start | bytes 786440 | tf_op jit(solution)/shard_map/ppermute | solution.py:25
  13.2 26.3 %collective-permute-start.3 = (bf16[128,1024]{1,0:T(8,128)(2,1)}, bf16[128,1024]{1,0:T(8,128)(2,1)S(1)}, u32[]{:S(2)}, u32[]{:S(2)}) collective-permute-start(bf16[128,1024]{1,0:T(8,128)(2,1)} %q.5), channel_id=1, source_target_pairs={{16,4},{24,12},{32,20},{40,28},{48,36},{56,44},{64,52},{72,60},{80... | collective-permute-start | bytes 786440 | tf_op jit(solution)/shard_map/ppermute | solution.py:25
  15.9 23.6 %all-to-all-start = ((bf16[8,8,1024]{2,1,0:T(8,128)(2,1)}), bf16[8,8,1024]{2,1,0:T(8,128)(2,1)S(1)}, u32[]{:S(2)}, u32[]{:S(2)}) async-start(bf16[8,8,1024]{2,1,0:T(8,128)(2,1)} %broadcast_in_dim.4), calls=%async_computation | async-start | bytes 262144 | tf_op jit(solution)/shard_map/all_to_all | solution.py:306
  39.5 11.8 %copy-start.17 = (bf16[256,1024]{1,0:T(8,128)(2,1)}, bf16[256,1024]{1,0:T(8,128)(2,1)S(1)}, u32[]{:S(2)}) copy-start(bf16[256,1024]{1,0:T(8,128)(2,1)S(1)} %collective-permute-done.chip) | copy-start | bytes 1572868
  39.5 1.2 %copy-start.18 = (bf16[256,1024]{1,0:T(8,128)(2,1)}, bf16[256,1024]{1,0:T(8,128)(2,1)S(1)}, u32[]{:S(2)}) copy-start(bf16[256,1024]{1,0:T(8,128)(2,1)S(1)} %collective-permute-done.1.far) | copy-start | bytes 1572868
  40.8 22.0 %all-to-all-start.1 = ((bf16[8,64,1024]{2,1,0:T(8,128)(2,1)}), bf16[8,64,1024]{2,1,0:T(8,128)(2,1)S(1)}, u32[]{:S(2)}, u32[]{:S(2)}) async-start(bf16[8,64,1024]{2,1,0:T(8,128)(2,1)} %broadcast_in_dim.5), calls=%async_computation.1 | async-start | bytes 2097152 | tf_op jit(solution)/shard_map/all_to_all | solution.py:316
  47.5 3.8 %collective-permute-start.4 = (bf16[256,1024]{1,0:T(8,128)(2,1)S(1)}, bf16[256,1024]{1,0:T(8,128)(2,1)S(1)}, u32[]{:S(2)}, u32[]{:S(2)}) collective-permute-start(bf16[256,1024]{1,0:T(8,128)(2,1)S(1)} %collective-permute-done.chip), channel_id=1, source_target_pairs={{0,4},{4,0},{1,5},{5,1},{2,6},{6,2},{3,7},{7,3},{8,12},{12,8},{9,1... | collective-permute-start | bytes 1572872 | tf_op jit(solution)/shard_map/ppermute | solution.py:29
  51.3 0.8 copy-start.19
  59.4 1.0 copy-start.1
  62.7 1.0 copy-start.2
  63.7 9.2 %copy-start = (bf16[1024,1024]{1,0:T(8,128)(2,1)S(1)}, bf16[1024,1024]{1,0:T(8,128)(2,1)}, u32[]{:S(2)}) copy-start(bf16[1024,1024]{1,0:T(8,128)(2,1)} %constant.2.clone.perm) | copy-start | bytes 6291460
  63.7 20.6 %all-to-all-start.2 = ((bf16[8,64,1024]{2,1,0:T(8,128)(2,1)}), bf16[8,64,1024]{2,1,0:T(8,128)(2,1)}, u32[]{:S(2)}, u32[]{:S(2)}) async-start(bf16[8,64,1024]{2,1,0:T(8,128)(2,1)} %bitcast.5), calls=%async_computation.2 | async-start | bytes 2097152 | tf_op jit(solution)/shard_map/all_to_all | solution.py:347
  68.1 1.2 %copy-start.3 = (bf16[8,64,1024]{2,1,0:T(8,128)(2,1)S(1)}, bf16[8,64,1024]{2,1,0:T(8,128)(2,1)}, u32[]{:S(2)}) copy-start(bf16[8,64,1024]{2,1,0:T(8,128)(2,1)} %copy-done.2) | copy-start | bytes 3145732
  69.3 3.6 %copy-start.6 = (bf16[128,1024]{1,0:T(8,128)(2,1)S(1)}, bf16[128,1024]{1,0:T(8,128)(2,1)}, u32[]{:S(2)}) copy-start(bf16[128,1024]{1,0:T(8,128)(2,1)} %gate.3) | copy-start | bytes 786436
  69.3 3.6 %copy-start.12 = (f32[128,1024]{1,0:T(8,128)S(1)}, f32[128,1024]{1,0:T(8,128)}, u32[]{:S(2)}) copy-start(f32[128,1024]{1,0:T(8,128)} %get-tuple-element.39.normed) | copy-start | bytes 1572868
  69.3 3.6 %copy-start.16 = (f32[128,128]{1,0:T(8,128)S(1)}, f32[128,128]{1,0:T(8,128)}, u32[]{:S(2)}) copy-start(f32[128,128]{1,0:T(8,128)} %get-tuple-element.40.rstd) | copy-start | bytes 196612
  72.9 7.1 %copy-start.7 = (bf16[128,1024]{1,0:T(8,128)(2,1)S(1)}, bf16[128,1024]{1,0:T(8,128)(2,1)}, u32[]{:S(2)}) copy-start(bf16[128,1024]{1,0:T(8,128)(2,1)} %q.5) | copy-start | bytes 786436
  75.2 11.3 %copy-start.13 = (bf16[128,1024]{1,0:T(8,128)(2,1)}, bf16[128,1024]{1,0:T(8,128)(2,1)S(1)}, u32[]{:S(2)}) copy-start(bf16[128,1024]{1,0:T(8,128)(2,1)S(1)} %get-tuple-element.47.u) | copy-start | bytes 786436
  75.2 26.3 %collective-permute-start.5 = (bf16[128,1024]{1,0:T(8,128)(2,1)S(1)}, bf16[128,1024]{1,0:T(8,128)(2,1)S(1)}, u32[]{:S(2)}, u32[]{:S(2)}) collective-permute-start(bf16[128,1024]{1,0:T(8,128)(2,1)S(1)} %get-tuple-element.47.u), channel_id=1, source_target_pairs={{8,0},{12,4},{16,8},{20,12},{24,16},{28,20},{32,24},{36,28},{40,32... | collective-permute-start | bytes 786440 | tf_op jit(solution)/shard_map/ppermute | solution.py:25
  76.4 27.5 %collective-permute-start.6 = (bf16[128,1024]{1,0:T(8,128)(2,1)S(1)}, bf16[128,1024]{1,0:T(8,128)(2,1)}, u32[]{:S(2)}, u32[]{:S(2)}) collective-permute-start(bf16[128,1024]{1,0:T(8,128)(2,1)S(1)} %get-tuple-element.47.u), channel_id=1, source_target_pairs={{16,4},{24,12},{32,20},{40,28},{48,36},{56,44},{64,52},{72,60},{80... | collective-permute-start | bytes 786440 | tf_op jit(solution)/shard_map/ppermute | solution.py:25
  86.4 21.9 %all-to-all-start.3 = ((f32[8,8,1024]{2,1,0:T(8,128)}), f32[8,8,1024]{2,1,0:T(8,128)S(1)}, u32[]{:S(2)}, u32[]{:S(2)}) async-start(f32[8,8,1024]{2,1,0:T(8,128)} %bitcast.4), calls=%async_computation.3 | async-start | bytes 524288 | tf_op jit(solution)/shard_map/all_to_all | solution.py:352
  97.0 6.9 %copy-start.5 = (bf16[256,1024]{1,0:T(8,128)(2,1)S(1)}, bf16[256,1024]{1,0:T(8,128)(2,1)}, u32[]{:S(2)}) copy-start(bf16[256,1024]{1,0:T(8,128)(2,1)} %copy-done.4) | copy-start | bytes 1572868
  97.0 6.9 %copy-start.8 = (bf16[128,1024]{1,0:T(8,128)(2,1)S(1)}, bf16[128,1024]{1,0:T(8,128)(2,1)}, u32[]{:S(2)}) copy-start(bf16[128,1024]{1,0:T(8,128)(2,1)} %q.5) | copy-start | bytes 786436
  97.0 6.9 %copy-start.14 = (bf16[128,1024]{1,0:T(8,128)(2,1)S(1)}, bf16[128,1024]{1,0:T(8,128)(2,1)}, u32[]{:S(2)}) copy-start(bf16[128,1024]{1,0:T(8,128)(2,1)} %copy-done.13) | copy-start | bytes 786436
  97.1 6.9 %copy-start.15 = (s32[16384]{0:T(1024)S(1)}, s32[16384]{0:T(1024)}, u32[]{:S(2)}) copy-start(s32[16384]{0:T(1024)} %param.12) | copy-start | bytes 196612

commit v6 on v5

--- a/solution.py
+++ b/solution.py
@@ -309,7 +309,8 @@
     kv_chip = shift(kv, 2)
     cot, k_pair, v_pair = pair(cotangent), pair(key_rows), pair(value_rows)
     kv_far = shift(kv, 3, range(1, COUNT, 2))
-    q_chip, q_far = ahead(query_rows)
+    q_late, k_pair, v_pair = lax.optimization_barrier((query_rows, k_pair, v_pair))
+    q_chip, q_far = ahead(q_late)
     kv_chip, kv_far, w_line, cot, k_pair, v_pair, q_chip, q_far = lax.optimization_barrier(
         (kv_chip, kv_far, w_line, cot, k_pair, v_pair, q_chip, q_far)
     )

time: 110 us -> 111 us (level)
  waiting for transfers between devices: 4.27 us -> 6.87 us
  blocking collectives: 23.3 us -> 21.8 us
    all_to_all x1, waiting for transfers between devices: 0.01 us -> 4.62 us  [body(): lax.all_to_all(jnp.broadcast_to(w_out[None], (NZ,) + w_out.shape), 'z', 0...]
    ppermute x1, starting transfers between devices: 1.91 us -> 5.63 us  [ring(): lax.ppermute(value, axis, [(s, (s + steps) % size) for s in range(size)])]
    all_to_all x1, starting transfers between devices: 6.76 us -> 4.24 us  [body(): lax.all_to_all(jnp.broadcast_to(w_line[None], (NY * NX,) + w_line.shape),...]
    all_to_all x1, waiting for transfers between devices: 2.37 us -> 0.01 us  [body(): lax.all_to_all(jnp.broadcast_to(w_line[None], (NY * NX,) + w_line.shape),...]
    all_to_all x1, starting transfers between devices: 10.6 us -> 9.01 us  [body(): w_line = lax.all_to_all(w_sum, 'z', 0, 0, tiled=True)]
    all_gather x9, blocking collectives: 23.3 us -> 21.8 us  [pair(): return lax.all_gather(rows_of, 'c', axis=0, tiled=True)]
    all_to_all x1, starting transfers between devices: 4.37 us -> 5.56 us  [body(): lax.all_to_all(w_part.reshape(NY * NX, NZ * unit, width), PLANE, 0, 0, ti...]
    unnamed x42 -> x52, local copies, waits for them, and re-layouts: 5.95 us -> 6.01 us
  transfers between devices with their start and end apart: 11 -> 11, of which waited for: 2 -> 3; matrix products, arithmetic and copies ran while one was open for 1% -> 1% of each run, Pallas kernels for 18% -> 17%
where the time goes in v6:
time: 111 us; the launch traced here: 109 us
  starting transfers between devices  52.8 us (48%)
  blocking collectives  21.8 us (20%)
  Pallas kernels  19 us (17%)
  local copies, waits for them, and re-layouts  7.91 us (7%)
  waiting for transfers between devices  6.87 us (6%)
    all_gather x9, blocking collectives, pair(): return lax.all_gather(rows_of, 'c', axis=0, tiled=True)  21.8 us
    ppermute x6, starting transfers between devices, shift(): return lax.ppermute(value, BLK, pairs)  14.5 us
    all_to_all x1, starting transfers between devices, body(): lax.all_to_all(jnp.broadcast_to(w_out[None], (NZ,) + w_out.shape), 'z', 0...  13.9 us
    all_to_all x1, starting transfers between devices, body(): w_line = lax.all_to_all(w_sum, 'z', 0, 0, tiled=True)  9.01 us
    unnamed x52, local copies, waits for them, and re-layouts  6.01 us
    ppermute x1, starting transfers between devices, ring(): lax.ppermute(value, axis, [(s, (s + steps) % size) for s in range(size)])  5.63 us
    all_to_all x1, starting transfers between devices, body(): lax.all_to_all(w_part.reshape(NY * NX, NZ * unit, width), PLANE, 0, 0, ti...  5.56 us
    all_to_all x1, waiting for transfers between devices, body(): lax.all_to_all(jnp.broadcast_to(w_out[None], (NZ,) + w_out.shape), 'z', 0...  4.62 us
  transfers between devices with their start and end apart: 11, of which 3 were waited for; matrix products, arithmetic and copies ran while one was open for 1% of the time, Pallas kernels for 17%

profile of v6, /device:TPU:1, one launch (start us, length us, event | category | flops | bytes accessed | tf_op | source)
XLA Modules:
  0.0 109.2 jit_solution(1617057409973651159)
XLA Ops:
  0.7 1.0 copy-done.10
  2.7 4.1 %collective-permute-start = (bf16[256,1024]{1,0:T(8,128)(2,1)S(1)}, bf16[256,1024]{1,0:T(8,128)(2,1)S(1)}, u32[]{:S(2)}, u32[]{:S(2)}) collective-permute-start(bf16[256,1024]{1,0:T(8,128)(2,1)S(1)} %shard_map.119.kv), channel_id=1, source_target_pairs={{0,8},{4,12},{8,16},{12,20},{16,24},{20,28},{24,32},{28,36},{32,40... | collective-permute-start | bytes 1572872 | tf_op jit(solution)/shard_map/ppermute | solution.py:25
  6.8 5.2 %collective-permute-start.1 = (bf16[256,1024]{1,0:T(8,128)(2,1)S(1)}, bf16[256,1024]{1,0:T(8,128)(2,1)S(1)}, u32[]{:S(2)}, u32[]{:S(2)}) collective-permute-start(bf16[256,1024]{1,0:T(8,128)(2,1)S(1)} %shard_map.119.kv), channel_id=1, source_target_pairs={{4,16},{12,24},{20,32},{28,40},{36,48},{44,56},{52,64},{60,72},{68... | collective-permute-start | bytes 1572872 | tf_op jit(solution)/shard_map/ppermute | solution.py:25
  12.0 2.3 %all_gather.28.k_pair = bf16[256,1024]{1,0:T(8,128)(2,1)} all-gather(bf16[128,1024]{1,0:T(8,128)(2,1)S(1)} %copy-done.10), channel_id=1, replica_groups=mesh['y'=2,'z'=8,'x'=4,'c'=2,'grp'=4] {'c'}, dimensions={0}, use_global_device_ids=true | all-gather | bytes 786432 | tf_op jit(solution)/shard_map/all_gather | solution.py:300
  14.3 2.3 %all_gather.29.v_pair = bf16[256,1024]{1,0:T(8,128)(2,1)} all-gather(bf16[128,1024]{1,0:T(8,128)(2,1)S(1)} %copy-done.11), channel_id=1, replica_groups=mesh['y'=2,'z'=8,'x'=4,'c'=2,'grp'=4] {'c'}, dimensions={0}, use_global_device_ids=true | all-gather | bytes 786432 | tf_op jit(solution)/shard_map/all_gather | solution.py:300
  16.6 1.3 %collective-permute-start.2 = (bf16[128,1024]{1,0:T(8,128)(2,1)S(1)}, bf16[128,1024]{1,0:T(8,128)(2,1)S(1)}, u32[]{:S(2)}, u32[]{:S(2)}) collective-permute-start(bf16[128,1024]{1,0:T(8,128)(2,1)S(1)} %copy-done.7), channel_id=1, source_target_pairs={{8,0},{12,4},{16,8},{20,12},{24,16},{28,20},{32,24},{36,28},{40,32... | collective-permute-start | bytes 786440 | tf_op jit(solution)/shard_map/ppermute | solution.py:25
  17.9 1.3 %collective-permute-start.3 = (bf16[128,1024]{1,0:T(8,128)(2,1)S(1)}, bf16[128,1024]{1,0:T(8,128)(2,1)S(1)}, u32[]{:S(2)}, u32[]{:S(2)}) collective-permute-start(bf16[128,1024]{1,0:T(8,128)(2,1)S(1)} %copy-done.7), channel_id=1, source_target_pairs={{16,4},{24,12},{32,20},{40,28},{48,36},{56,44},{64,52},{72,60},{80... | collective-permute-start | bytes 786440 | tf_op jit(solution)/shard_map/ppermute | solution.py:25
  19.9 13.9 %all-to-all-start = ((bf16[8,8,1024]{2,1,0:T(8,128)(2,1)}), bf16[8,8,1024]{2,1,0:T(8,128)(2,1)S(1)}, u32[]{:S(2)}, u32[]{:S(2)}) async-start(bf16[8,8,1024]{2,1,0:T(8,128)(2,1)} %broadcast_in_dim.4), calls=%async_computation | async-start | bytes 262144 | tf_op jit(solution)/shard_map/all_to_all | solution.py:306
  33.8 3.3 %all_gather.27.cot = bf16[256,1024]{1,0:T(8,128)(2,1)S(1)} all-gather(bf16[128,1024]{1,0:T(8,128)(2,1)S(1)} %copy-done.24), channel_id=1, replica_groups=mesh['y'=2,'z'=8,'x'=4,'c'=2,'grp'=4] {'c'}, dimensions={0}, use_global_device_ids=true | all-gather | bytes 786432 | tf_op jit(solution)/shard_map/all_gather | solution.py:300
  37.1 4.6 %all-to-all-done = bf16[8,8,1024]{2,1,0:T(8,128)(2,1)S(1)} async-done(((bf16[8,8,1024]{2,1,0:T(8,128)(2,1)}), bf16[8,8,1024]{2,1,0:T(8,128)(2,1)S(1)}, u32[]{:S(2)}, u32[]{:S(2)}) %all-to-all-start) | async-done | bytes 131104 | tf_op jit(solution)/shard_map/all_to_all | solution.py:306
  41.8 1.2 %broadcast_in_dim.5 = bf16[8,64,1024]{2,1,0:T(8,128)(2,1)} broadcast(bf16[64,1024]{1,0:T(8,128)(2,1)S(1)} %bitcast.10), dimensions={1,2} | broadcast | bytes 1179648 | tf_op jit(solution)/shard_map/broadcast_in_dim | solution.py:318
  43.0 4.2 %all-to-all-start.1 = ((bf16[8,64,1024]{2,1,0:T(8,128)(2,1)}), bf16[8,64,1024]{2,1,0:T(8,128)(2,1)S(1)}, u32[]{:S(2)}, u32[]{:S(2)}) async-start(bf16[8,64,1024]{2,1,0:T(8,128)(2,1)} %broadcast_in_dim.5), calls=%async_computation.1 | async-start | bytes 2097152 | tf_op jit(solution)/shard_map/all_to_all | solution.py:317
  47.3 5.6 %collective-permute-start.4 = (bf16[256,1024]{1,0:T(8,128)(2,1)S(1)}, bf16[256,1024]{1,0:T(8,128)(2,1)S(1)}, u32[]{:S(2)}, u32[]{:S(2)}) collective-permute-start(bf16[256,1024]{1,0:T(8,128)(2,1)S(1)} %collective-permute-done.chip), channel_id=1, source_target_pairs={{0,4},{4,0},{1,5},{5,1},{2,6},{6,2},{3,7},{7,3},{8,12},{12,8},{9,1... | collective-permute-start | bytes 1572872 | tf_op jit(solution)/shard_map/ppermute | solution.py:29
  52.9 1.5 %collective-permute-done.4.cross = bf16[256,1024]{1,0:T(8,128)(2,1)S(1)} collective-permute-done((bf16[256,1024]{1,0:T(8,128)(2,1)S(1)}, bf16[256,1024]{1,0:T(8,128)(2,1)S(1)}, u32[]{:S(2)}, u32[]{:S(2)}) %collective-permute-start.4) | collective-permute-done | bytes 524320 | tf_op jit(solution)/shard_map/ppermute | solution.py:29
  55.2 4.4 %shard_map.121 = (f32[128,1024]{1,0:T(8,128)}, f32[128,128]{1,0:T(8,128)}, bf16[128,1024]{1,0:T(8,128)(2,1)}) custom-call(s32[128,128]{1,0:T(8,128)} %bitcast.7, bf16[128,1024]{1,0:T(8,128)(2,1)} %q.5, bf16[256,1024]{1,0:T(8,128)(2,1)} %copy-done.4, bf16[256,1024]{1,0:T(8,128)(2,1)} %all_gather.28.k_pair, bf16[256,1024]{1,0:T(8,128)(2,1)} %all_gather.29.v_pair, ...), custom_call_target="tpu_custom_call" | custom-call | flops 1000 | bytes 1000 | tf_op jit(solution)/shard_map/pallas_call | solution.py:323
  59.6 2.4 %all_gather.31.hidden = bf16[256,1024]{1,0:T(8,128)(2,1)S(1)} all-gather(bf16[128,1024]{1,0:T(8,128)(2,1)} %get-tuple-element.51), channel_id=1, replica_groups=mesh['y'=2,'z'=8,'x'=4,'c'=2,'grp'=4] {'c'}, dimensions={0}, use_global_device_ids=true | all-gather | bytes 786432 | tf_op jit(solution)/shard_map/all_gather | solution.py:300
  63.5 1.0 copy-done.2
  64.5 5.6 %all-to-all-start.2 = ((bf16[8,64,1024]{2,1,0:T(8,128)(2,1)}), bf16[8,64,1024]{2,1,0:T(8,128)(2,1)}, u32[]{:S(2)}, u32[]{:S(2)}) async-start(bf16[8,64,1024]{2,1,0:T(8,128)(2,1)} %bitcast.5), calls=%async_computation.2 | async-start | bytes 2097152 | tf_op jit(solution)/shard_map/all_to_all | solution.py:348
  70.0 1.2 %copy-done.3 = bf16[8,64,1024]{2,1,0:T(8,128)(2,1)S(1)} copy-done((bf16[8,64,1024]{2,1,0:T(8,128)(2,1)S(1)}, bf16[8,64,1024]{2,1,0:T(8,128)(2,1)}, u32[]{:S(2)}) %copy-start.3) | copy-done | bytes 1048600
  71.2 1.4 %shard_map.120 = (f32[128,512]{1,0:T(8,128)S(1)}, f32[128,512]{1,0:T(8,128)S(1)}) custom-call(bf16[256,1024]{1,0:T(8,128)(2,1)S(1)} %all_gather.27.cot, bf16[512,1024]{1,0:T(8,128)(2,1)S(1)} %bitcast.6), custom_call_target="tpu_custom_call" | custom-call | flops 1000 | bytes 1000 | tf_op jit(solution)/shard_map/pallas_call | solution.py:333
  72.6 2.5 %all_gather.30.both = f32[256,512]{1,0:T(8,128)S(1)} all-gather(f32[128,512]{1,0:T(8,128)S(1)} %get-tuple-element.40), channel_id=1, replica_groups=mesh['y'=2,'z'=8,'x'=4,'c'=2,'grp'=4] {'c'}, dimensions={0}, use_global_device_ids=true | all-gather | bytes 786432 | tf_op jit(solution)/shard_map/all_gather | solution.py:300
  75.1 2.2 %shard_map.122 = (bf16[128,1024]{1,0:T(8,128)(2,1)}, bf16[128,1024]{1,0:T(8,128)(2,1)S(1)}) custom-call(f32[128,512]{1,0:T(8,128)S(1)} %get-tuple-element.39.mine, f32[256,512]{1,0:T(8,128)S(1)} %all_gather.30.both, f32[128,1024]{1,0:T(8,128)S(1)} %copy-done.12, f32[128,128]{1,0:T(8,128)S(1)} %copy-done.18, bf16[128,1024]{1,0:T(8,128)(2,1)S(1)} %copy-done.6, ...), custom_call_target="tpu_custom_call" | custom-call | flops 1000 | bytes 1000 | tf_op jit(solution)/shard_map/pallas_call | solution.py:339
  77.3 1.3 %collective-permute-start.5 = (bf16[128,1024]{1,0:T(8,128)(2,1)S(1)}, bf16[128,1024]{1,0:T(8,128)(2,1)S(1)}, u32[]{:S(2)}, u32[]{:S(2)}) collective-permute-start(bf16[128,1024]{1,0:T(8,128)(2,1)S(1)} %get-tuple-element.53.u), channel_id=1, source_target_pairs={{8,0},{12,4},{16,8},{20,12},{24,16},{28,20},{32,24},{36,28},{40,32... | collective-permute-start | bytes 786440 | tf_op jit(solution)/shard_map/ppermute | solution.py:25
  78.6 1.3 %collective-permute-start.6 = (bf16[128,1024]{1,0:T(8,128)(2,1)S(1)}, bf16[128,1024]{1,0:T(8,128)(2,1)S(1)}, u32[]{:S(2)}, u32[]{:S(2)}) collective-permute-start(bf16[128,1024]{1,0:T(8,128)(2,1)S(1)} %get-tuple-element.53.u), channel_id=1, source_target_pairs={{16,4},{24,12},{32,20},{40,28},{48,36},{56,44},{64,52},{72,60},{80... | collective-permute-start | bytes 786440 | tf_op jit(solution)/shard_map/ppermute | solution.py:25
  79.9 2.2 %all_gather.32.u_pair = bf16[256,1024]{1,0:T(8,128)(2,1)S(1)} all-gather(bf16[128,1024]{1,0:T(8,128)(2,1)S(1)} %get-tuple-element.53.u), channel_id=1, replica_groups=mesh['y'=2,'z'=8,'x'=4,'c'=2,'grp'=4] {'c'}, dimensions={0}, use_global_device_ids=true | all-gather | bytes 786432 | tf_op jit(solution)/shard_map/all_gather | solution.py:300
  82.1 2.2 %all_gather.33.q_pair = bf16[256,1024]{1,0:T(8,128)(2,1)S(1)} all-gather(bf16[128,1024]{1,0:T(8,128)(2,1)S(1)} %copy-done.8), channel_id=1, replica_groups=mesh['y'=2,'z'=8,'x'=4,'c'=2,'grp'=4] {'c'}, dimensions={0}, use_global_device_ids=true | all-gather | bytes 786432 | tf_op jit(solution)/shard_map/all_gather | solution.py:300
  84.3 2.2 %all_gather.34.q_chips = bf16[256,1024]{1,0:T(8,128)(2,1)S(1)} all-gather(bf16[128,1024]{1,0:T(8,128)(2,1)S(1)} %copy-done.14), channel_id=1, replica_groups=mesh['y'=2,'z'=8,'x'=4,'c'=2,'grp'=4] {'c'}, dimensions={0}, use_global_device_ids=true | all-gather | bytes 786432 | tf_op jit(solution)/shard_map/all_gather | solution.py:300
  86.4 2.1 %shard_map.124 = f32[64,1024]{1,0:T(8,128)} custom-call(bf16[8,64,1024]{2,1,0:T(8,128)(2,1)} %all-to-all-done.2.parts), custom_call_target="tpu_custom_call" | custom-call | flops 1000 | bytes 1000 | tf_op jit(solution)/shard_map/pallas_call | solution.py:352
  88.5 9.0 %all-to-all-start.3 = ((f32[8,8,1024]{2,1,0:T(8,128)}), f32[8,8,1024]{2,1,0:T(8,128)S(1)}, u32[]{:S(2)}, u32[]{:S(2)}) async-start(f32[8,8,1024]{2,1,0:T(8,128)} %bitcast.4), calls=%async_computation.3 | async-start | bytes 524288 | tf_op jit(solution)/shard_map/all_to_all | solution.py:353
  97.6 4.4 %shard_map.125 = bf16[128,1024]{1,0:T(8,128)(2,1)} custom-call(s32[128,128]{1,0:T(8,128)} %bitcast.8, bf16[128,1024]{1,0:T(8,128)(2,1)} %q.5, bf16[128,1024]{1,0:T(8,128)(2,1)} %copy-done.15, bf16[256,1024]{1,0:T(8,128)(2,1)} %copy-done.4, bf16[256,1024]{1,0:T(8,128)(2,1)} %all_gather.28.k_pair, bf16[256,1024]{1,0:T(8,128)(2,1)} %all_gather.29.v_pair, ...), custom_call_target="tpu_custom_call" | custom-call | flops 20000000000 | bytes 1000 | tf_op jit(solution)/shard_map/pallas_call | solution.py:355
  102.0 2.5 %all_gather.35.u_chips = bf16[256,1024]{1,0:T(8,128)(2,1)S(1)} all-gather(bf16[128,1024]{1,0:T(8,128)(2,1)S(1)} %collective-permute-done.5.u_chip), channel_id=1, replica_groups=mesh['y'=2,'z'=8,'x'=4,'c'=2,'grp'=4] {'c'}, dimensions={0}, use_global_device_ids=true | all-gather | bytes 786432 | tf_op jit(solution)/shard_map/all_gather | solution.py:300
  104.5 3.4 %shard_map.126 = (bf16[128,1024]{1,0:T(8,128)(2,1)}, bf16[128,1024]{1,0:T(8,128)(2,1)}) custom-call(s32[128,128]{1,0:T(8,128)S(1)} %bitcast.9, bf16[256,1024]{1,0:T(8,128)(2,1)S(1)} %copy-done.5, bf16[128,1024]{1,0:T(8,128)(2,1)S(1)} %copy-done.9, bf16[256,1024]{1,0:T(8,128)(2,1)S(1)} %all_gather.33.q_pair, bf16[128,1024]{1,0:T(8,128)(2,1)S(1)} %copy-done.14, ...), custom_call_target="tpu_custom_call" | custom-call | flops 20000000000 | bytes 1000 | tf_op jit(solution)/shard_map/pallas_call | solution.py:368
  (62 shorter events, 5.4 us)
Async XLA Ops:
  0.6 16.0 %copy-start.7 = (bf16[128,1024]{1,0:T(8,128)(2,1)S(1)}, bf16[128,1024]{1,0:T(8,128)(2,1)}, u32[]{:S(2)}) copy-start(bf16[128,1024]{1,0:T(8,128)(2,1)} %q.5) | copy-start | bytes 786436
  2.6 16.6 %copy-start.25 = (bf16[8,1024]{1,0:T(8,128)(2,1)S(1)}, bf16[8,1024]{1,0:T(8,128)(2,1)}, u32[]{:S(2)}) copy-start(bf16[8,1024]{1,0:T(8,128)(2,1)} %param.13) | copy-start | bytes 49156
  2.6 31.2 %copy-start.24 = (bf16[128,1024]{1,0:T(8,128)(2,1)S(1)}, bf16[128,1024]{1,0:T(8,128)(2,1)}, u32[]{:S(2)}) copy-start(bf16[128,1024]{1,0:T(8,128)(2,1)} %param.14) | copy-start | bytes 786436
  2.7 40.4 %copy-start.4 = (bf16[256,1024]{1,0:T(8,128)(2,1)}, bf16[256,1024]{1,0:T(8,128)(2,1)S(1)}, u32[]{:S(2)}) copy-start(bf16[256,1024]{1,0:T(8,128)(2,1)S(1)} %shard_map.119.kv) | copy-start | bytes 1572868
  2.7 39.1 %collective-permute-start = (bf16[256,1024]{1,0:T(8,128)(2,1)S(1)}, bf16[256,1024]{1,0:T(8,128)(2,1)S(1)}, u32[]{:S(2)}, u32[]{:S(2)}) collective-permute-start(bf16[256,1024]{1,0:T(8,128)(2,1)S(1)} %shard_map.119.kv), channel_id=1, source_target_pairs={{0,8},{4,12},{8,16},{12,20},{16,24},{20,28},{24,32},{28,36},{32,40... | collective-permute-start | bytes 1572872 | tf_op jit(solution)/shard_map/ppermute | solution.py:25
  6.8 35.0 %collective-permute-start.1 = (bf16[256,1024]{1,0:T(8,128)(2,1)S(1)}, bf16[256,1024]{1,0:T(8,128)(2,1)S(1)}, u32[]{:S(2)}, u32[]{:S(2)}) collective-permute-start(bf16[256,1024]{1,0:T(8,128)(2,1)S(1)} %shard_map.119.kv), channel_id=1, source_target_pairs={{4,16},{12,24},{20,32},{28,40},{36,48},{44,56},{52,64},{60,72},{68... | collective-permute-start | bytes 1572872 | tf_op jit(solution)/shard_map/ppermute | solution.py:25
  16.6 25.1 %collective-permute-start.2 = (bf16[128,1024]{1,0:T(8,128)(2,1)S(1)}, bf16[128,1024]{1,0:T(8,128)(2,1)S(1)}, u32[]{:S(2)}, u32[]{:S(2)}) collective-permute-start(bf16[128,1024]{1,0:T(8,128)(2,1)S(1)} %copy-done.7), channel_id=1, source_target_pairs={{8,0},{12,4},{16,8},{20,12},{24,16},{28,20},{32,24},{36,28},{40,32... | collective-permute-start | bytes 786440 | tf_op jit(solution)/shard_map/ppermute | solution.py:25
  17.9 23.8 %collective-permute-start.3 = (bf16[128,1024]{1,0:T(8,128)(2,1)S(1)}, bf16[128,1024]{1,0:T(8,128)(2,1)S(1)}, u32[]{:S(2)}, u32[]{:S(2)}) collective-permute-start(bf16[128,1024]{1,0:T(8,128)(2,1)S(1)} %copy-done.7), channel_id=1, source_target_pairs={{16,4},{24,12},{32,20},{40,28},{48,36},{56,44},{64,52},{72,60},{80... | collective-permute-start | bytes 786440 | tf_op jit(solution)/shard_map/ppermute | solution.py:25
  19.9 21.8 %all-to-all-start = ((bf16[8,8,1024]{2,1,0:T(8,128)(2,1)}), bf16[8,8,1024]{2,1,0:T(8,128)(2,1)S(1)}, u32[]{:S(2)}, u32[]{:S(2)}) async-start(bf16[8,8,1024]{2,1,0:T(8,128)(2,1)} %broadcast_in_dim.4), calls=%async_computation | async-start | bytes 262144 | tf_op jit(solution)/shard_map/all_to_all | solution.py:306
  41.7 1.3 %copy-start.13 = (bf16[128,1024]{1,0:T(8,128)(2,1)}, bf16[128,1024]{1,0:T(8,128)(2,1)S(1)}, u32[]{:S(2)}) copy-start(bf16[128,1024]{1,0:T(8,128)(2,1)S(1)} %collective-permute-done.2.q_chip) | copy-start | bytes 786436
  41.7 1.3 %copy-start.19 = (bf16[128,1024]{1,0:T(8,128)(2,1)}, bf16[128,1024]{1,0:T(8,128)(2,1)S(1)}, u32[]{:S(2)}) copy-start(bf16[128,1024]{1,0:T(8,128)(2,1)S(1)} %collective-permute-done.3.q_far) | copy-start | bytes 786436
  41.8 12.7 %copy-start.21 = (bf16[256,1024]{1,0:T(8,128)(2,1)}, bf16[256,1024]{1,0:T(8,128)(2,1)S(1)}, u32[]{:S(2)}) copy-start(bf16[256,1024]{1,0:T(8,128)(2,1)S(1)} %collective-permute-done.chip) | copy-start | bytes 1572868
  41.8 12.7 %copy-start.22 = (bf16[256,1024]{1,0:T(8,128)(2,1)}, bf16[256,1024]{1,0:T(8,128)(2,1)S(1)}, u32[]{:S(2)}) copy-start(bf16[256,1024]{1,0:T(8,128)(2,1)S(1)} %collective-permute-done.1.far) | copy-start | bytes 1572868
  43.0 20.4 %all-to-all-start.1 = ((bf16[8,64,1024]{2,1,0:T(8,128)(2,1)}), bf16[8,64,1024]{2,1,0:T(8,128)(2,1)S(1)}, u32[]{:S(2)}, u32[]{:S(2)}) async-start(bf16[8,64,1024]{2,1,0:T(8,128)(2,1)} %broadcast_in_dim.5), calls=%async_computation.1 | async-start | bytes 2097152 | tf_op jit(solution)/shard_map/all_to_all | solution.py:317
  47.3 7.1 %collective-permute-start.4 = (bf16[256,1024]{1,0:T(8,128)(2,1)S(1)}, bf16[256,1024]{1,0:T(8,128)(2,1)S(1)}, u32[]{:S(2)}, u32[]{:S(2)}) collective-permute-start(bf16[256,1024]{1,0:T(8,128)(2,1)S(1)} %collective-permute-done.chip), channel_id=1, source_target_pairs={{0,4},{4,0},{1,5},{5,1},{2,6},{6,2},{3,7},{7,3},{8,12},{12,8},{9,1... | collective-permute-start | bytes 1572872 | tf_op jit(solution)/shard_map/ppermute | solution.py:29
  64.5 10.6 %copy-start = (bf16[1024,1024]{1,0:T(8,128)(2,1)S(1)}, bf16[1024,1024]{1,0:T(8,128)(2,1)}, u32[]{:S(2)}) copy-start(bf16[1024,1024]{1,0:T(8,128)(2,1)} %constant.2.clone.perm) | copy-start | bytes 6291460
  64.5 22.0 %all-to-all-start.2 = ((bf16[8,64,1024]{2,1,0:T(8,128)(2,1)}), bf16[8,64,1024]{2,1,0:T(8,128)(2,1)}, u32[]{:S(2)}, u32[]{:S(2)}) async-start(bf16[8,64,1024]{2,1,0:T(8,128)(2,1)} %bitcast.5), calls=%async_computation.2 | async-start | bytes 2097152 | tf_op jit(solution)/shard_map/all_to_all | solution.py:348
  70.0 1.2 %copy-start.3 = (bf16[8,64,1024]{2,1,0:T(8,128)(2,1)S(1)}, bf16[8,64,1024]{2,1,0:T(8,128)(2,1)}, u32[]{:S(2)}) copy-start(bf16[8,64,1024]{2,1,0:T(8,128)(2,1)} %copy-done.2) | copy-start | bytes 3145732
  71.2 3.8 %copy-start.6 = (bf16[128,1024]{1,0:T(8,128)(2,1)S(1)}, bf16[128,1024]{1,0:T(8,128)(2,1)}, u32[]{:S(2)}) copy-start(bf16[128,1024]{1,0:T(8,128)(2,1)} %gate.3) | copy-start | bytes 786436
  71.2 3.8 %copy-start.12 = (f32[128,1024]{1,0:T(8,128)S(1)}, f32[128,1024]{1,0:T(8,128)}, u32[]{:S(2)}) copy-start(f32[128,1024]{1,0:T(8,128)} %get-tuple-element.45.normed) | copy-start | bytes 1572868
  71.2 3.8 %copy-start.18 = (f32[128,128]{1,0:T(8,128)S(1)}, f32[128,128]{1,0:T(8,128)}, u32[]{:S(2)}) copy-start(f32[128,128]{1,0:T(8,128)} %get-tuple-element.46.rstd) | copy-start | bytes 196612
  75.1 7.0 %copy-start.8 = (bf16[128,1024]{1,0:T(8,128)(2,1)S(1)}, bf16[128,1024]{1,0:T(8,128)(2,1)}, u32[]{:S(2)}) copy-start(bf16[128,1024]{1,0:T(8,128)(2,1)} %q.5) | copy-start | bytes 786436
  75.1 9.2 %copy-start.14 = (bf16[128,1024]{1,0:T(8,128)(2,1)S(1)}, bf16[128,1024]{1,0:T(8,128)(2,1)}, u32[]{:S(2)}) copy-start(bf16[128,1024]{1,0:T(8,128)(2,1)} %copy-done.13) | copy-start | bytes 786436
  77.3 11.2 %copy-start.15 = (bf16[128,1024]{1,0:T(8,128)(2,1)}, bf16[128,1024]{1,0:T(8,128)(2,1)S(1)}, u32[]{:S(2)}) copy-start(bf16[128,1024]{1,0:T(8,128)(2,1)S(1)} %get-tuple-element.53.u) | copy-start | bytes 786436
  77.3 24.7 %collective-permute-start.5 = (bf16[128,1024]{1,0:T(8,128)(2,1)S(1)}, bf16[128,1024]{1,0:T(8,128)(2,1)S(1)}, u32[]{:S(2)}, u32[]{:S(2)}) collective-permute-start(bf16[128,1024]{1,0:T(8,128)(2,1)S(1)} %get-tuple-element.53.u), channel_id=1, source_target_pairs={{8,0},{12,4},{16,8},{20,12},{24,16},{28,20},{32,24},{36,28},{40,32... | collective-permute-start | bytes 786440 | tf_op jit(solution)/shard_map/ppermute | solution.py:25
  78.6 25.8 %collective-permute-start.6 = (bf16[128,1024]{1,0:T(8,128)(2,1)S(1)}, bf16[128,1024]{1,0:T(8,128)(2,1)S(1)}, u32[]{:S(2)}, u32[]{:S(2)}) collective-permute-start(bf16[128,1024]{1,0:T(8,128)(2,1)S(1)} %get-tuple-element.53.u), channel_id=1, source_target_pairs={{16,4},{24,12},{32,20},{40,28},{48,36},{56,44},{64,52},{72,60},{80... | collective-permute-start | bytes 786440 | tf_op jit(solution)/shard_map/ppermute | solution.py:25
  88.5 20.1 %all-to-all-start.3 = ((f32[8,8,1024]{2,1,0:T(8,128)}), f32[8,8,1024]{2,1,0:T(8,128)S(1)}, u32[]{:S(2)}, u32[]{:S(2)}) async-start(f32[8,8,1024]{2,1,0:T(8,128)} %bitcast.4), calls=%async_computation.3 | async-start | bytes 524288 | tf_op jit(solution)/shard_map/all_to_all | solution.py:353
  97.5 6.9 %copy-start.5 = (bf16[256,1024]{1,0:T(8,128)(2,1)S(1)}, bf16[256,1024]{1,0:T(8,128)(2,1)}, u32[]{:S(2)}) copy-start(bf16[256,1024]{1,0:T(8,128)(2,1)} %copy-done.4) | copy-start | bytes 1572868
  97.5 6.9 %copy-start.9 = (bf16[128,1024]{1,0:T(8,128)(2,1)S(1)}, bf16[128,1024]{1,0:T(8,128)(2,1)}, u32[]{:S(2)}) copy-start(bf16[128,1024]{1,0:T(8,128)(2,1)} %q.5) | copy-start | bytes 786436
  97.5 6.9 %copy-start.16 = (bf16[128,1024]{1,0:T(8,128)(2,1)S(1)}, bf16[128,1024]{1,0:T(8,128)(2,1)}, u32[]{:S(2)}) copy-start(bf16[128,1024]{1,0:T(8,128)(2,1)} %copy-done.15) | copy-start | bytes 786436
  97.6 6.9 %copy-start.17 = (s32[16384]{0:T(1024)S(1)}, s32[16384]{0:T(1024)}, u32[]{:S(2)}) copy-start(s32[16384]{0:T(1024)} %param.12) | copy-start | bytes 196612
  97.6 6.9 %copy-start.20 = (bf16[128,1024]{1,0:T(8,128)(2,1)S(1)}, bf16[128,1024]{1,0:T(8,128)(2,1)}, u32[]{:S(2)}) copy-start(bf16[128,1024]{1,0:T(8,128)(2,1)} %copy-done.19) | copy-start | bytes 786436
  (5 other events, 4.7 us)
